TPU v7x, 768 devices: a whole 4x8x12 slice. The times are simulated.
768 devices in a mesh: fsdp: 16 (over y, core), dp: 48 (over z, x).
Axes of the slice: x: 4, y: 8, z: 12, core: 2. Of those that a mesh axis runs over, the one named last changes fastest.
Arguments:
- gradients: float32 [48, 48, 512, 512], P('dp', None, 'fsdp'), may hold values from -0.625 to 0.625
- owners: int32 [48], replicated, may hold values from 0 to 15
- left_factor: float32 [48, 512, 512], P('dp', 'fsdp'), may hold values from -1 to 9, as said below
- right_factor: float32 [48, 512, 512], P('dp', 'fsdp'), may hold values from -1 to 9, as said below
- left_root: bfloat16 [48, 16, 512, 512], P('dp', 'fsdp'), may hold values from -1 to 3, as said below
- right_root: bfloat16 [48, 16, 512, 512], P('dp', 'fsdp'), may hold values from -1 to 3, as said below
Outputs:
- left_new: float32 [48, 512, 512], P('dp', 'fsdp')
- right_new: float32 [48, 512, 512], P('dp', 'fsdp')
- directions: bfloat16 [48, 512, 512], P('dp', 'fsdp')
Inputs may be any that keep to these rules, and one draw needn't show every extreme that they name: `left_factor`: symmetric in its last two dimensions. `right_factor`: symmetric in its last two dimensions. `left_root`: symmetric in its last two dimensions. `right_root`: symmetric in its last two dimensions.
All inputs are finite; a program needn't handle non-finite values.
Results may differ from a plain program's by a relative error of at most 0.004.
Values may be sent and summed in bfloat16 or wider, within the bound.
No kernel may reach another device: no remote copies, remote signals or barrier semaphores. Data moves between devices by JAX's collectives and lax.ppermute only.
A program may use at most 32 MiB of HBM per device.

v0:
```python
import jax
import jax.numpy as jnp
from jax import lax
from jax.sharding import PartitionSpec as P


def from_root(value, axis, root):
    mine = lax.axis_index(axis) == root
    return lax.psum(jnp.where(mine, value, jnp.zeros_like(value)), axis)


def on_device(gradients, owners, left_factor, right_factor, left_root, right_root):
    reduced = lax.psum_scatter(gradients[0], "dp", scatter_dimension=0, tiled=True)
    my_rows = reduced[0]
    row_count = my_rows.shape[0]
    whole = lax.all_gather(my_rows, "fsdp", axis=0, tiled=True)
    my_index = lax.axis_index("fsdp")
    first_row = my_index * row_count
    holder = owners[lax.axis_index("dp")]
    left_stat = lax.dot_general(
        whole, whole, (((1,), (1,)), ((), ())), precision=lax.Precision.HIGHEST
    )
    right_stat = lax.dot_general(
        whole, whole, (((0,), (0,)), ((), ())), precision=lax.Precision.HIGHEST
    )
    product = jnp.dot(left_root[0, 0].astype(jnp.float32), whole, precision=lax.Precision.HIGHEST)
    product = jnp.dot(
        product, right_root[0, 0].astype(jnp.float32), precision=lax.Precision.HIGHEST
    )
    received = (
        from_root(left_stat.astype(jnp.bfloat16), "fsdp", holder).astype(left_stat.dtype),
        from_root(right_stat.astype(jnp.bfloat16), "fsdp", holder).astype(right_stat.dtype),
        from_root(product.astype(jnp.bfloat16), "fsdp", holder).astype(product.dtype),
    )
    left_rows = lax.dynamic_slice_in_dim(received[0], first_row, row_count, 0)
    right_rows = lax.dynamic_slice_in_dim(received[1], first_row, row_count, 0)
    product_rows = lax.dynamic_slice_in_dim(received[2], first_row, row_count, 0)
    left_new = 0.9 * left_factor + 0.1 * left_rows[None]
    right_new = 0.9 * right_factor + 0.1 * right_rows[None]
    directions = product_rows.astype(jnp.bfloat16)[None]
    return (left_new, right_new, directions)


def solution(mesh):
    placed = (
        P("dp", None, "fsdp", None),
        P(),
        P("dp", "fsdp", None),
        P("dp", "fsdp", None),
        P("dp", "fsdp", None, None),
        P("dp", "fsdp", None, None),
    )
    return jax.shard_map(
        on_device,
        mesh=mesh,
        in_specs=placed,
        out_specs=(P("dp", "fsdp", None), P("dp", "fsdp", None), P("dp", "fsdp", None)),
        check_vma=False,
    )
```

profile of v0, /device:TPU:1, one launch (start us, length us, event | category | flops | bytes accessed | tf_op | source)
XLA Modules:
  0.0 638.3 jit_solution(8805563233243922564)
XLA Ops:
  7.2 0.0 copy-start
  7.2 0.0 copy-start.5
  7.2 0.0 copy-start.2
  7.2 0.0 reduce-scatter.2.cloned.1.call-start
  7.2 0.7 reduce-scatter.2.cloned.1.call-update
  7.9 0.0 all-gather.3.cloned.1.call-start
  8.0 436.6 %reduce-scatter.2.cloned.1.call-done = f32[1,32,512]{2,1,0:T(8,128)} async-done(((f32[48,32,512]{2,1,0:T(8,128)}), f32[1,32,512]{2,1,0:T(8,128)}) %reduce-scatter.2.cloned.1.call-update) | async-done | bytes 65552 | tf_op jit(solution)/shard_map/reduce_scatter | solution.py:13
  444.6 0.0 all-gather.3.cloned.1.call-update
  444.6 0.0 all-reduce.3.cloned.1.call-start
  444.7 0.0 copy-done.5
  444.7 0.6 dynamic_slice.12
  446.0 50.5 %all-gather.3.cloned.1.call-done = f32[1,512,512]{2,1,0:T(8,128)} async-done(((f32[1,32,512]{2,1,0:T(8,128)}), f32[1,512,512]{2,1,0:T(8,128)}) %all-gather.3.cloned.1.call-update) | async-done | bytes 1048592 | tf_op jit(solution)/shard_map/all_gather | solution.py:16
  496.5 0.0 copy-done
  496.5 2.4 fusion.3
  498.9 0.0 copy-done.2
  498.9 0.0 copy-start.3
  498.9 0.0 copy-start.4
  498.9 1.8 fusion
  500.7 2.7 fusion.2
  503.4 2.7 fusion.1
  506.1 0.0 all-reduce.3.cloned.1.call-update
  506.1 122.8 %all-reduce.3.cloned.1.call-done = (bf16[512,512]{1,0:T(8,128)(2,1)}, bf16[512,512]{1,0:T(8,128)(2,1)}, bf16[512,512]{1,0:T(8,128)(2,1)}) async-done(((bf16[512,512]{1,0:T(8,128)(2,1)}, bf16[512,512]{1,0:T(8,128)(2,1)}, bf16[512,512]{1,0:T(8,128)(2,1)}), (bf16[512,512]{1,0:T(8,128)(2,1)}, bf16[512,512]{1,0:T(8,128)(2,1)}, bf16[512,512]{1,0:T(8,128)(2,1)})) %all-reduce.3.cloned.1.call-update) | async-done | bytes 1572880 | tf_op jit(solution)/shard_map/psum | solution.py:9
  628.9 1.4 fusion.9
  630.3 1.4 bitcast_add_fusion
  (4 shorter events, 0.0 us)
Async XLA Ops:
  7.2 489.3 %copy-start = (bf16[1,1,512,512]{3,2,1,0:T(8,128)(2,1)S(1)}, bf16[1,1,512,512]{3,2,1,0:T(8,128)(2,1)}, u32[]{:S(2)}) copy-start(bf16[1,1,512,512]{3,2,1,0:T(8,128)(2,1)} %param.10) | copy-start | bytes 1572868
  7.2 437.5 %copy-start.5 = (s32[48]{0:T(128)S(1)}, s32[48]{0:T(128)}, u32[]{:S(2)}) copy-start(s32[48]{0:T(128)} %param.7) | copy-start | bytes 580
  7.2 491.7 %copy-start.2 = (bf16[1,1,512,512]{3,2,1,0:T(8,128)(2,1)S(1)}, bf16[1,1,512,512]{3,2,1,0:T(8,128)(2,1)}, u32[]{:S(2)}) copy-start(bf16[1,1,512,512]{3,2,1,0:T(8,128)(2,1)} %param.11) | copy-start | bytes 1572868
  7.2 437.4 %reduce-scatter.2.cloned.1.call-start = ((), (), s32[]{:S(2)}) async-start(), calls=%async_computation.1 | async-start | bytes 3211264 | tf_op jit(solution)/shard_map/reduce_scatter | solution.py:13
  7.9 488.5 %all-gather.3.cloned.1.call-start = ((), (), s32[]{:S(2)}) async-start(), calls=%async_computation.2 | async-start | bytes 1114112 | tf_op jit(solution)/shard_map/all_gather | solution.py:16
  444.6 184.3 %all-reduce.3.cloned.1.call-start = ((), (), s32[]{:S(2)}) async-start(), calls=%async_computation.3 | async-start | bytes 3145728 | tf_op jit(solution)/shard_map/psum | solution.py:9
  496.5 4.2 copy-start.1
  498.9 131.4 %copy-start.3 = (f32[1,32,512]{2,1,0:T(8,128)S(1)}, f32[1,32,512]{2,1,0:T(8,128)}, u32[]{:S(2)}) copy-start(f32[1,32,512]{2,1,0:T(8,128)} %param.9) | copy-start | bytes 196612
  498.9 131.4 %copy-start.4 = (f32[1,32,512]{2,1,0:T(8,128)S(1)}, f32[1,32,512]{2,1,0:T(8,128)}, u32[]{:S(2)}) copy-start(f32[1,32,512]{2,1,0:T(8,128)} %param.8) | copy-start | bytes 196612
Sparse Core Ops, SparseCore 0:
  13.1 431.5 reduce-scatter.1
  447.0 49.4 all-gather.2
  506.2 122.6 all-reduce.2
where the time goes:
time: 639 us; the launch traced here: 638 us
  waiting for transfers between devices  611 us (96%)
  between operations  14.5 us (2%)
  matrix products  9.53 us (1%)
    reduce_scatter x1, waiting for transfers between devices, on_device(): lax.psum_scatter(gradients[0], 'dp', scatter_dimension=0, tiled=True)  437 us
    psum x1, waiting for transfers between devices, from_root(): return lax.psum(jnp.where(mine, value, jnp.zeros_like(value)), axis)  123 us
    all_gather x1, waiting for transfers between devices, on_device(): whole = lax.all_gather(my_rows, 'fsdp', axis=0, tiled=True)  50.5 us
  transfers between devices with their start and end apart: 3, of which 3 were waited for; matrix products, arithmetic and copies ran while one was open for 0% of the time, Pallas kernels for 0%

commit v1 on v0

v1 whole, which is shorter than its diff:
```python
import jax
import jax.numpy as jnp
from jax import lax
from jax.sharding import Mesh
from jax.sharding import PartitionSpec as P

Y, C, Z, X = 8, 2, 12, 4
BF, F32 = jnp.bfloat16, jnp.float32
ROWS = ("y", "c")


def to_column(value, step):
    return lax.ppermute(value, "x", [(i, (i + step) % X) for i in range(X)])


def mm(a, b, ca, cb):
    return lax.dot_general(a, b, (((ca,), (cb,)), ((), ())), preferred_element_type=F32)


def on_device(gradients, owners, left_factor, right_factor, left_root, right_root):
    rows, width = gradients.shape[2:]
    mine = gradients.reshape(Z, X, rows, width)
    x, z = lax.axis_index("x"), lax.axis_index("z")
    me = lax.axis_index("y") * C + lax.axis_index("c")

    def column(step):
        return lax.dynamic_index_in_dim(mine, lax.rem(x + step, X), 1, keepdims=False)

    with jax.named_scope("sum_over_x"):
        came = [to_column(column(step).astype(BF), step) for step in (2, 1, 3)]
        partial = column(0) + came[0].astype(F32) + came[1].astype(F32) + came[2].astype(F32)
    with jax.named_scope("sum_over_z"):
        got = lax.all_to_all(partial.astype(BF), "z", 0, 0, tiled=True)
        my_rows = jnp.sum(got.astype(F32), axis=0).astype(BF)
    with jax.named_scope("whole_block"):
        whole = lax.all_gather(my_rows, ROWS, axis=0, tiled=True)
    with jax.named_scope("direction"):
        left = mm(left_root[0, 0], whole, 1, 0)
        high = left.astype(BF)
        low = (left - high.astype(F32)).astype(BF)
        product = (mm(high, right_root[0, 0], 1, 0) + mm(low, right_root[0, 0], 1, 0)).astype(BF)
        every = lax.all_to_all(product.reshape(Y * C, rows, width), ROWS, 0, 0, tiled=True)
        directions = lax.dynamic_index_in_dim(every, owners[z * X + x], 0, keepdims=True)
    with jax.named_scope("statistics"):
        columns = lax.dynamic_slice_in_dim(whole, me * rows, rows, 1)
        left_new = 0.9 * left_factor + 0.1 * mm(my_rows, whole, 1, 1)[None]
        right_new = 0.9 * right_factor + 0.1 * mm(columns, whole, 0, 0)[None]
    return left_new, right_new, directions


def solution(mesh):
    grid = Mesh(mesh.devices.reshape(Y, C, Z, X), ("y", "c", "z", "x"))
    dp = ("z", "x")
    stat = P(dp, ROWS, None)
    return jax.shard_map(
        on_device,
        mesh=grid,
        in_specs=(P(dp, None, ROWS, None), P(), stat, stat, P(dp, ROWS, None, None), P(dp, ROWS, None, None)),
        out_specs=(stat, stat, stat),
        check_vma=False,
    )
```

time: 639 us -> 106 us (0.17)
  waiting for transfers between devices: 611 us -> 25.6 us
  blocking collectives: 0 us -> 53.9 us
  starting transfers between devices: 0.11 us -> 15.2 us
  between operations: 14.5 us -> 2.72 us
    reduce_scatter x1 -> x0, waiting for transfers between devices: 437 us -> none  [on_device(): lax.psum_scatter(gradients[0], 'dp', scatter_dimension=0, tiled=True)]
    psum x1 -> x0, waiting for transfers between devices: 123 us -> none  [from_root(): return lax.psum(jnp.where(mine, value, jnp.zeros_like(value)), axis)]
    all_gather x1 -> x0, waiting for transfers between devices: 50.5 us -> none  [on_device(): whole = lax.all_gather(my_rows, 'fsdp', axis=0, tiled=True)]
    all_to_all x0 -> x1, blocking collectives: none -> 31 us  [on_device(): got = lax.all_to_all(partial.astype(BF), 'z', 0, 0, tiled=True)]
    all_gather x0 -> x1, blocking collectives: none -> 22.9 us  [on_device(): whole = lax.all_gather(my_rows, ROWS, axis=0, tiled=True)]
    all_to_all x0 -> x1, waiting for transfers between devices: none -> 12.9 us  [on_device(): lax.all_to_all(product.reshape(Y * C, rows, width), ROWS, 0, 0, tiled=True)]
    ppermute x0 -> x3, waiting for transfers between devices: none -> 12.6 us  [to_column(): return lax.ppermute(value, 'x', [(i, (i + step) % X) for i in range(X)])]
    ppermute x0 -> x3, starting transfers between devices: none -> 10.8 us  [to_column(): return lax.ppermute(value, 'x', [(i, (i + step) % X) for i in range(X)])]
  transfers between devices with their start and end apart: 3 -> 4, of which waited for: 3 -> 3; matrix products, arithmetic and copies ran while one was open for 0% -> 2% of each run, Pallas kernels for 0% -> 0%
where the time goes in v1:
time: 106 us
  blocking collectives  53.9 us (51%)
  waiting for transfers between devices  25.6 us (24%)
  starting transfers between devices  15.2 us (14%)
  matrix products  4.07 us (4%)
  local copies, waits for them, and re-layouts  3.12 us (3%)
  between operations  2.72 us (3%)
  other arithmetic  1.42 us (1%)
    all_to_all x1, blocking collectives, on_device(): got = lax.all_to_all(partial.astype(BF), 'z', 0, 0, tiled=True)  31 us
    all_gather x1, blocking collectives, on_device(): whole = lax.all_gather(my_rows, ROWS, axis=0, tiled=True)  22.9 us
    all_to_all x1, waiting for transfers between devices, on_device(): lax.all_to_all(product.reshape(Y * C, rows, width), ROWS, 0, 0, tiled=True)  12.9 us
    ppermute x3, waiting for transfers between devices, to_column(): return lax.ppermute(value, 'x', [(i, (i + step) % X) for i in range(X)])  12.6 us
    ppermute x3, starting transfers between devices, to_column(): return lax.ppermute(value, 'x', [(i, (i + step) % X) for i in range(X)])  10.8 us
    all_to_all x1, starting transfers between devices, on_device(): lax.all_to_all(product.reshape(Y * C, rows, width), ROWS, 0, 0, tiled=True)  4.49 us
    dot_general x5, matrix products, mm(): lax.dot_general(a, b, (((ca,), (cb,)), ((), ())), preferred_element_type=...  4.07 us
  transfers between devices with their start and end apart: 4, of which 3 were waited for; matrix products, arithmetic and copies ran while one was open for 2% of the time, Pallas kernels for 0%

profile of v1, /device:TPU:1, one launch (start us, length us, event | category | flops | bytes accessed | tf_op | source)
XLA Modules:
  0.0 106.0 jit_solution(16197196303874315016)
XLA Ops:
  0.6 0.0 copy-start
  0.7 1.9 %fusion.13 = (bf16[12,32,512]{2,1,0:T(8,128)(2,1)S(1)}, bf16[12,32,512]{2,1,0:T(8,128)(2,1)S(1)}, bf16[12,32,512]{2,1,0:T(8,128)(2,1)S(1)}) fusion(f32[12,4,32,512]{3,2,1,0:T(8,128)} %bitcast.47, s32[]{:T(128)S(6)} %select_n.24, s32[]{:T(128)S(6)} %select_n.26, s32[]{:T(128)S(6)} %select_n.25), kind=kLoop, calls=%fused_computation.22 | loop fusion | bytes 2359308 | tf_op jit(solution)/shard_map/sum_over_x/convert_element_type | solution.py:30
  2.6 5.5 %collective-permute-start = (bf16[12,32,512]{2,1,0:T(8,128)(2,1)S(1)}, bf16[12,32,512]{2,1,0:T(8,128)(2,1)S(1)}, u32[]{:S(2)}, u32[]{:S(2)}) collective-permute-start(bf16[12,32,512]{2,1,0:T(8,128)(2,1)S(1)} %get-tuple-element.3), channel_id=1, source_target_pairs={{0,2},{1,3},{2,0},{3,1},{4,6},{5,7},{6,4},{7,5},{8,10},{9,11},{10,... | collective-permute-start | bytes 1179656 | tf_op jit(solution)/shard_map/sum_over_x/ppermute | solution.py:13
  8.1 2.8 %collective-permute-start.2 = (bf16[12,32,512]{2,1,0:T(8,128)(2,1)S(1)}, bf16[12,32,512]{2,1,0:T(8,128)(2,1)S(1)}, u32[]{:S(2)}, u32[]{:S(2)}) collective-permute-start(bf16[12,32,512]{2,1,0:T(8,128)(2,1)S(1)} %get-tuple-element.4), channel_id=1, source_target_pairs={{0,3},{1,0},{2,1},{3,2},{4,7},{5,4},{6,5},{7,6},{8,11},{9,8},{10,9... | collective-permute-start | bytes 1179656 | tf_op jit(solution)/shard_map/sum_over_x/ppermute | solution.py:13
  10.8 2.5 %collective-permute-start.1 = (bf16[12,32,512]{2,1,0:T(8,128)(2,1)S(1)}, bf16[12,32,512]{2,1,0:T(8,128)(2,1)S(1)}, u32[]{:S(2)}, u32[]{:S(2)}) collective-permute-start(bf16[12,32,512]{2,1,0:T(8,128)(2,1)S(1)} %get-tuple-element.5), channel_id=1, source_target_pairs={{0,1},{1,2},{2,3},{3,0},{4,5},{5,6},{6,7},{7,4},{8,9},{9,10},{10,1... | collective-permute-start | bytes 1179656 | tf_op jit(solution)/shard_map/sum_over_x/ppermute | solution.py:13
  13.4 0.0 collective-permute-done
  13.4 11.1 %collective-permute-done.2 = bf16[12,32,512]{2,1,0:T(8,128)(2,1)S(1)} collective-permute-done((bf16[12,32,512]{2,1,0:T(8,128)(2,1)S(1)}, bf16[12,32,512]{2,1,0:T(8,128)(2,1)S(1)}, u32[]{:S(2)}, u32[]{:S(2)}) %collective-permute-start.2) | collective-permute-done | bytes 393248 | tf_op jit(solution)/shard_map/sum_over_x/ppermute | solution.py:13
  24.5 1.6 %collective-permute-done.1 = bf16[12,32,512]{2,1,0:T(8,128)(2,1)S(1)} collective-permute-done((bf16[12,32,512]{2,1,0:T(8,128)(2,1)S(1)}, bf16[12,32,512]{2,1,0:T(8,128)(2,1)S(1)}, u32[]{:S(2)}, u32[]{:S(2)}) %collective-permute-start.1) | collective-permute-done | bytes 393248 | tf_op jit(solution)/shard_map/sum_over_x/ppermute | solution.py:13
  26.0 1.4 %fusion.7 = bf16[12,32,512]{2,1,0:T(8,128)(2,1)S(1)} fusion(bf16[12,32,512]{2,1,0:T(8,128)(2,1)S(1)} %collective-permute-done.2, bf16[12,32,512]{2,1,0:T(8,128)(2,1)S(1)} %collective-permute-done.1, bf16[12,32,512]{2,1,0:T(8,128)(2,1)S(1)} %collective-permute-done, f32[12,4,32,512]{3,2,1,0:T(8,128)} %bitcast.48, s32[]{:T(128)S(6)} %select_n.23), kind=kLoop, calls=%fused_computation.15 | loop fusion | flops 1376256 | bytes 2359300 | tf_op jit(solution)/shard_map/sum_over_z/convert_element_type | solution.py:33
  27.4 31.0 %all_to_all.10 = bf16[12,32,512]{2,1,0:T(8,128)(2,1)S(1)} all-to-all(bf16[12,32,512]{2,1,0:T(8,128)(2,1)S(1)} %fusion.7), channel_id=1, replica_groups=mesh['y'=8,'c'=2,'z'=12,'x'=4] {'z'}, dimensions={0} | all-to-all | bytes 786432 | tf_op jit(solution)/shard_map/sum_over_z/all_to_all | solution.py:33
  58.4 0.1 reduce_sum.12
  58.5 22.9 %all_gather.3 = bf16[512,512]{1,0:T(8,128)(2,1)S(1)} all-gather(bf16[32,512]{1,0:T(8,128)(2,1)S(1)} %reduce_sum.12), channel_id=1, replica_groups=mesh['y'=8,'c'=2,'z'=12,'x'=4] {'y','c'}, dimensions={0}, use_global_device_ids=true | all-gather | bytes 557056 | tf_op jit(solution)/shard_map/whole_block/all_gather | solution.py:36
  81.3 0.5 convolution_bitcast_fusion
  81.8 0.0 copy-start.4
  81.8 0.0 copy-start.2
  81.9 0.0 copy-start.3
  81.9 0.5 fusion.9
  82.3 1.3 %fusion = bf16[512,512]{1,0:T(8,128)(2,1)} fusion(f32[512,512]{1,0:T(8,128)S(1)} %fusion.9, f32[512,512]{0,1:T(8,128)S(1)} %convolution_bitcast_fusion, bf16[1,1,512,512]{3,2,1,0:T(8,128)(2,1)S(1)} %copy-done), kind=kOutput, calls=%fused_computation.2 | convolution fusion | flops 270008320 | bytes 3145728 | tf_op jit(solution)/shard_map/direction/dot_general | solution.py:17
  83.6 4.5 %all-to-all-start.1 = ((bf16[16,32,512]{2,1,0:T(8,128)(2,1)}), bf16[16,32,512]{2,1,0:T(8,128)(2,1)S(1)}, u32[]{:S(2)}, u32[]{:S(2)}) async-start(bf16[16,32,512]{2,1,0:T(8,128)(2,1)} %bitcast.10), calls=%async_computation.1 | async-start | bytes 1048576 | tf_op jit(solution)/shard_map/direction/all_to_all | solution.py:42
  88.1 0.6 dynamic_slice.28
  90.7 0.9 fusion.2
  91.6 0.9 fusion.4
  92.5 12.9 %all-to-all-done.1 = bf16[16,32,512]{2,1,0:T(8,128)(2,1)S(1)} async-done(((bf16[16,32,512]{2,1,0:T(8,128)(2,1)}), bf16[16,32,512]{2,1,0:T(8,128)(2,1)S(1)}, u32[]{:S(2)}, u32[]{:S(2)}) %all-to-all-start.1) | async-done | bytes 524320 | tf_op jit(solution)/shard_map/direction/all_to_all | solution.py:42
  105.4 0.6 constant_dynamic-slice_fusion
  (6 shorter events, 0.0 us)
Async XLA Ops:
  0.6 81.2 %copy-start = (bf16[1,1,512,512]{3,2,1,0:T(8,128)(2,1)S(1)}, bf16[1,1,512,512]{3,2,1,0:T(8,128)(2,1)}, u32[]{:S(2)}) copy-start(bf16[1,1,512,512]{3,2,1,0:T(8,128)(2,1)} %param.11) | copy-start | bytes 1572868
  0.7 80.7 %copy-start.1 = (bf16[1,1,512,512]{3,2,1,0:T(8,128)(2,1)S(1)}, bf16[1,1,512,512]{3,2,1,0:T(8,128)(2,1)}, u32[]{:S(2)}) copy-start(bf16[1,1,512,512]{3,2,1,0:T(8,128)(2,1)} %param.10) | copy-start | bytes 1572868
  2.6 10.8 %collective-permute-start = (bf16[12,32,512]{2,1,0:T(8,128)(2,1)S(1)}, bf16[12,32,512]{2,1,0:T(8,128)(2,1)S(1)}, u32[]{:S(2)}, u32[]{:S(2)}) collective-permute-start(bf16[12,32,512]{2,1,0:T(8,128)(2,1)S(1)} %get-tuple-element.3), channel_id=1, source_target_pairs={{0,2},{1,3},{2,0},{3,1},{4,6},{5,7},{6,4},{7,5},{8,10},{9,11},{10,... | collective-permute-start | bytes 1179656 | tf_op jit(solution)/shard_map/sum_over_x/ppermute | solution.py:13
  8.1 16.4 %collective-permute-start.2 = (bf16[12,32,512]{2,1,0:T(8,128)(2,1)S(1)}, bf16[12,32,512]{2,1,0:T(8,128)(2,1)S(1)}, u32[]{:S(2)}, u32[]{:S(2)}) collective-permute-start(bf16[12,32,512]{2,1,0:T(8,128)(2,1)S(1)} %get-tuple-element.4), channel_id=1, source_target_pairs={{0,3},{1,0},{2,1},{3,2},{4,7},{5,4},{6,5},{7,6},{8,11},{9,8},{10,9... | collective-permute-start | bytes 1179656 | tf_op jit(solution)/shard_map/sum_over_x/ppermute | solution.py:13
  10.8 15.2 %collective-permute-start.1 = (bf16[12,32,512]{2,1,0:T(8,128)(2,1)S(1)}, bf16[12,32,512]{2,1,0:T(8,128)(2,1)S(1)}, u32[]{:S(2)}, u32[]{:S(2)}) collective-permute-start(bf16[12,32,512]{2,1,0:T(8,128)(2,1)S(1)} %get-tuple-element.5), channel_id=1, source_target_pairs={{0,1},{1,2},{2,3},{3,0},{4,5},{5,6},{6,7},{7,4},{8,9},{9,10},{10,1... | collective-permute-start | bytes 1179656 | tf_op jit(solution)/shard_map/sum_over_x/ppermute | solution.py:13
  81.8 6.3 %copy-start.4 = (s32[48]{0:T(128)S(1)}, s32[48]{0:T(128)}, u32[]{:S(2)}) copy-start(s32[48]{0:T(128)} %param.7) | copy-start | bytes 580
  81.8 8.8 %copy-start.2 = (f32[1,32,512]{2,1,0:T(8,128)S(1)}, f32[1,32,512]{2,1,0:T(8,128)}, u32[]{:S(2)}) copy-start(f32[1,32,512]{2,1,0:T(8,128)} %param.9) | copy-start | bytes 196612
  81.9 9.7 %copy-start.3 = (f32[1,32,512]{2,1,0:T(8,128)S(1)}, f32[1,32,512]{2,1,0:T(8,128)}, u32[]{:S(2)}) copy-start(f32[1,32,512]{2,1,0:T(8,128)} %param.8) | copy-start | bytes 196612
  83.6 21.8 %all-to-all-start.1 = ((bf16[16,32,512]{2,1,0:T(8,128)(2,1)}), bf16[16,32,512]{2,1,0:T(8,128)(2,1)S(1)}, u32[]{:S(2)}, u32[]{:S(2)}) async-start(bf16[16,32,512]{2,1,0:T(8,128)(2,1)} %bitcast.10), calls=%async_computation.1 | async-start | bytes 1048576 | tf_op jit(solution)/shard_map/direction/all_to_all | solution.py:42

commit v2 on v1

v2 whole, which is shorter than its diff:
```python
import jax
import jax.numpy as jnp
from jax import lax
from jax.sharding import Mesh
from jax.sharding import PartitionSpec as P

Y, C, Z, X = 8, 2, 12, 4
ZN = 3
ZF = Z // ZN
BF, F32 = jnp.bfloat16, jnp.float32
ROWS = ("y", "c")


def along_x(value, step):
    return lax.ppermute(value, "x", [(i, (i + step) % X) for i in range(X)])


def near_z(value, step):
    return lax.ppermute(value, "z", [(i, i - i % ZN + (i + step) % ZN) for i in range(Z)])


def far_z(value, step):
    return lax.ppermute(value, "z", [(i, (i + step * ZN) % Z) for i in range(Z)])


def mm(a, b, ca, cb):
    return lax.dot_general(a, b, (((ca,), (cb,)), ((), ())), preferred_element_type=F32)


def pick(array, index, axis):
    return lax.dynamic_index_in_dim(array, index, axis, keepdims=False)


def on_device(gradients, owners, left_factor, right_factor, left_root, right_root):
    rows, width = gradients.shape[2:]
    mine = gradients.reshape(Z, X, rows, width)
    x, z = lax.axis_index("x"), lax.axis_index("z")
    near, far = lax.rem(z, ZN), lax.div(z, ZN)
    me = lax.axis_index("y") * C + lax.axis_index("c")

    with jax.named_scope("sum_over_x"):
        to_x = [pick(mine, lax.rem(x + step, X), 1).astype(BF) for step in (2, 1, 3)]
        came = [along_x(v, step).reshape(ZF, ZN, rows, width) for v, step in zip(to_x, (2, 1, 3))]
    with jax.named_scope("owner_roots"):
        owner, core = owners[z * X + x], lax.axis_index("c")
        here = lax.rem(owner, C) == core
        left_root, right_root = left_root[0, 0], right_root[0, 0]
        left_inverse = jnp.where(here, left_root, lax.ppermute(left_root, "c", [(0, 1), (1, 0)]))
        right_inverse = jnp.where(here, right_root, lax.ppermute(right_root, "c", [(0, 1), (1, 0)]))
        left_inverse = pick(left_inverse.reshape(Y, C, rows, width), core, 1).reshape(-1, width)
    with jax.named_scope("sum_over_near_z"):
        kept = pick(mine, x, 1).reshape(ZF, ZN, rows, width)

        def over_x(step):
            at = lax.rem(near + step, ZN)
            return sum((pick(v, at, 1).astype(F32) for v in came), pick(kept, at, 1))

        came_z = [near_z(over_x(step).astype(BF), step) for step in (2, 1)]
        over_near = over_x(0)
    with jax.named_scope("sum_over_far_z"):

        def over_z(step):
            at = lax.rem(far + step, ZF)
            return sum((pick(v, at, 0).astype(F32) for v in came_z), pick(over_near, at, 0))

        came_far = [far_z(over_z(step).astype(BF), step) for step in (2, 1, 3)]
        my_rows = sum((v.astype(F32) for v in came_far), over_z(0)).astype(BF)
    with jax.named_scope("whole_block"):
        whole = lax.all_gather(my_rows, ROWS, axis=0, tiled=True)
    with jax.named_scope("direction"):
        left = mm(left_inverse, whole, 1, 0)
        high = lax.reduce_precision(left, 8, 7)
        low = (left - high).astype(BF)
        product = (mm(high.astype(BF), right_inverse, 1, 0) + mm(low, right_inverse, 1, 0)).astype(BF)
        every = lax.all_to_all(product.reshape(Y, rows, width), "y", 0, 0, tiled=True)
        directions = lax.dynamic_index_in_dim(every, lax.div(owner, C), 0, keepdims=True)
    with jax.named_scope("statistics"):
        columns = lax.dynamic_slice_in_dim(whole, me * rows, rows, 1)
        left_new = 0.9 * left_factor + 0.1 * mm(my_rows, whole, 1, 1)[None]
        right_new = 0.9 * right_factor + 0.1 * mm(columns, whole, 0, 0)[None]
    return left_new, right_new, directions


def solution(mesh):
    grid = Mesh(mesh.devices.reshape(Y, C, Z, X), ("y", "c", "z", "x"))
    dp = ("z", "x")
    stat = P(dp, ROWS, None)
    return jax.shard_map(
        on_device,
        mesh=grid,
        in_specs=(P(dp, None, ROWS, None), P(), stat, stat, P(dp, ROWS, None, None), P(dp, ROWS, None, None)),
        out_specs=(stat, stat, stat),
        check_vma=False,
    )
```

time: 106 us -> 109 us (1.028)
  starting transfers between devices: 15.2 us -> 59.9 us
  blocking collectives: 53.9 us -> 22 us
  waiting for transfers between devices: 25.6 us -> 12.3 us
  local copies, waits for them, and re-layouts: 3.12 us -> 5.11 us
  other arithmetic: 1.42 us -> 2.6 us
    ppermute x3 -> x10, starting transfers between devices: 10.8 us -> 55.9 us  [the longest x3 22.7 us: far_z(): lax.ppermute(value, 'z', [(i, (i + step * ZN) % Z) for i in range(Z)])]
    all_to_all x1 -> x0, blocking collectives: 31 us -> none  [on_device(): got = lax.all_to_all(partial.astype(BF), 'z', 0, 0, tiled=True)]
    ppermute x3 -> x10, waiting for transfers between devices: 12.6 us -> 1.89 us  [the longest x3 1.87 us: far_z(): lax.ppermute(value, 'z', [(i, (i + step * ZN) % Z) for i in range(Z)])]
    all_to_all x1, waiting for transfers between devices: 12.9 us -> 10.4 us  [on_device(): lax.all_to_all(product.reshape(Y, rows, width), 'y', 0, 0, tiled=True)]
    add x0 -> x2, other arithmetic: none -> 2.47 us  [over_x(): return sum((pick(v, at, 1).astype(F32) for v in came), pick(kept, at, 1))]
    convert_element_type x1 -> x2, other arithmetic: 1.36 us -> 0.07 us  [the longest x1 0.04 us: on_device(): came_far = [far_z(over_z(step).astype(BF), step) for step in (2, 1, 3)]]
    dynamic_slice x2 -> x4, local copies, waits for them, and re-layouts: 1.2 us -> 2.45 us  [the longest x2 1.24 us: pick(): return lax.dynamic_index_in_dim(array, index, axis, keepdims=False)]
  transfers between devices with their start and end apart: 4 -> 11, of which waited for: 3 -> 3; matrix products, arithmetic and copies ran while one was open for 2% -> 6% of each run, Pallas kernels for 0% -> 0%
where the time goes in v2:
time: 109 us; the launch traced here: 108 us
  starting transfers between devices  59.9 us (55%)
  blocking collectives  22 us (20%)
  waiting for transfers between devices  12.3 us (11%)
  local copies, waits for them, and re-layouts  5.11 us (5%)
  matrix products  3.43 us (3%)
  between operations  3.01 us (3%)
  other arithmetic  2.6 us (2%)
    ppermute x3, starting transfers between devices, far_z(): lax.ppermute(value, 'z', [(i, (i + step * ZN) % Z) for i in range(Z)])  22.7 us
    all_gather x1, blocking collectives, on_device(): whole = lax.all_gather(my_rows, ROWS, axis=0, tiled=True)  22 us
    ppermute x3, starting transfers between devices, along_x(): return lax.ppermute(value, 'x', [(i, (i + step) % X) for i in range(X)])  12 us
    all_to_all x1, waiting for transfers between devices, on_device(): lax.all_to_all(product.reshape(Y, rows, width), 'y', 0, 0, tiled=True)  10.4 us
    ppermute x1, starting transfers between devices, on_device(): lax.ppermute(left_root, 'c', [(0, 1), (1, 0)])  9.43 us
    ppermute x2, starting transfers between devices, near_z(): lax.ppermute(value, 'z', [(i, i - i % ZN + (i + step) % ZN) for i in rang...  8.99 us
    all_to_all x1, starting transfers between devices, on_device(): lax.all_to_all(product.reshape(Y, rows, width), 'y', 0, 0, tiled=True)  4.04 us
    dot_general x5, matrix products, mm(): lax.dot_general(a, b, (((ca,), (cb,)), ((), ())), preferred_element_type=...  3.43 us
  transfers between devices with their start and end apart: 11, of which 3 were waited for; matrix products, arithmetic and copies ran while one was open for 6% of the time, Pallas kernels for 0%

profile of v2, /device:TPU:1, one launch (start us, length us, event | category | flops | bytes accessed | tf_op | source)
XLA Modules:
  0.0 108.4 jit_solution(14144921867689554298)
XLA Ops:
  0.7 2.6 %fusion.6 = (bf16[12,32,512]{2,1,0:T(8,128)(2,1)}, bf16[12,32,512]{2,1,0:T(8,128)(2,1)S(1)}, bf16[12,32,512]{2,1,0:T(8,128)(2,1)S(1)}) fusion(f32[12,4,32,512]{3,2,1,0:T(8,128)} %bitcast.106, s32[]{:T(128)S(6)} %select_n.83, s32[]{:T(128)S(6)} %select_n.85, s32[]{:T(128)S(6)} %select_n.84), kind=kLoop, calls=%fused_computation.16 | loop fusion | bytes 2359308 | tf_op jit(solution)/shard_map/sum_over_x/convert_element_type | solution.py:42
  3.3 5.5 %collective-permute-start = (bf16[12,32,512]{2,1,0:T(8,128)(2,1)}, bf16[12,32,512]{2,1,0:T(8,128)(2,1)}, u32[]{:S(2)}, u32[]{:S(2)}) collective-permute-start(bf16[12,32,512]{2,1,0:T(8,128)(2,1)} %get-tuple-element.3), channel_id=1, source_target_pairs={{0,2},{1,3},{2,0},{3,1},{4,6},{5,7},{6,4},{7,5},{8,10},{9,11},{10,... | collective-permute-start | bytes 1179656 | tf_op jit(solution)/shard_map/sum_over_x/ppermute | solution.py:15
  8.8 2.2 %collective-permute-start.1 = (bf16[12,32,512]{2,1,0:T(8,128)(2,1)S(1)}, bf16[12,32,512]{2,1,0:T(8,128)(2,1)}, u32[]{:S(2)}, u32[]{:S(2)}) collective-permute-start(bf16[12,32,512]{2,1,0:T(8,128)(2,1)S(1)} %get-tuple-element.5), channel_id=1, source_target_pairs={{0,1},{1,2},{2,3},{3,0},{4,5},{5,6},{6,7},{7,4},{8,9},{9,10},{10,1... | collective-permute-start | bytes 1179656 | tf_op jit(solution)/shard_map/sum_over_x/ppermute | solution.py:15
  11.0 4.3 %collective-permute-start.2 = (bf16[12,32,512]{2,1,0:T(8,128)(2,1)S(1)}, bf16[12,32,512]{2,1,0:T(8,128)(2,1)}, u32[]{:S(2)}, u32[]{:S(2)}) collective-permute-start(bf16[12,32,512]{2,1,0:T(8,128)(2,1)S(1)} %get-tuple-element.4), channel_id=1, source_target_pairs={{0,3},{1,0},{2,1},{3,2},{4,7},{5,4},{6,5},{7,6},{8,11},{9,8},{10,9... | collective-permute-start | bytes 1179656 | tf_op jit(solution)/shard_map/sum_over_x/ppermute | solution.py:15
  15.3 9.4 %collective-permute-start.8 = (bf16[512,512]{1,0:T(8,128)(2,1)}, bf16[512,512]{1,0:T(8,128)(2,1)S(1)}, u32[]{:S(2)}, u32[]{:S(2)}) collective-permute-start(bf16[512,512]{1,0:T(8,128)(2,1)} %bitcast.110), channel_id=1, source_target_pairs={{0,48},{48,0},{1,49},{49,1},{2,50},{50,2},{3,51},{51,3},{4,52},{52... | collective-permute-start | bytes 1572872 | tf_op jit(solution)/shard_map/owner_roots/ppermute | solution.py:48
  24.7 1.2 %constant_dynamic-slice_fusion.2 = f32[12,1,32,512]{3,2,1,0:T(8,128)S(1)} fusion(f32[12,4,32,512]{3,2,1,0:T(8,128)} %bitcast.107, s32[]{:T(128)S(6)} %select_n.81), kind=kLoop, calls=%fused_computation.50 | loop fusion | bytes 1572868 | tf_op jit(solution)/shard_map/sum_over_near_z/jit(dynamic_index_in_dim)/dynamic_slice | solution.py:31
  26.0 1.1 %fusion.15 = bf16[4,32,512]{2,1,0:T(8,128)(2,1)S(1)} fusion(f32[4,3,32,512]{3,2,1,0:T(8,128)S(1)} %bitcast.103, s32[]{:T(128)S(6)} %select_n.87, bf16[4,3,32,512]{3,2,1,0:T(8,128)(2,1)} %bitcast.7, bf16[4,3,32,512]{3,2,1,0:T(8,128)(2,1)} %bitcast.5, bf16[4,3,32,512]{3,2,1,0:T(8,128)(2,1)} %bitcast.3), kind=kLoop, calls=%fused_computation.27 | loop fusion | flops 458752 | bytes 786436 | tf_op jit(solution)/shard_map/sum_over_near_z/add | solution.py:56
  27.2 7.1 %collective-permute-start.3 = (bf16[4,32,512]{2,1,0:T(8,128)(2,1)S(1)}, bf16[4,32,512]{2,1,0:T(8,128)(2,1)S(1)}, u32[]{:S(2)}, u32[]{:S(2)}) collective-permute-start(bf16[4,32,512]{2,1,0:T(8,128)(2,1)S(1)} %fusion.15), channel_id=1, source_target_pairs={{0,8},{4,0},{8,4},{12,20},{16,12},{20,16},{24,32},{28,24},{32,28},... | collective-permute-start | bytes 393224 | tf_op jit(solution)/shard_map/sum_over_near_z/ppermute | solution.py:19
  34.2 1.4 %fusion.14 = (bf16[4,32,512]{2,1,0:T(8,128)(2,1)S(1)}, f32[4,1,32,512]{3,2,1,0:T(8,128)S(1)}) fusion(f32[4,3,32,512]{3,2,1,0:T(8,128)S(1)} %bitcast.104, s32[]{:T(128)S(6)} %select_n.88, bf16[4,3,32,512]{3,2,1,0:T(8,128)(2,1)} %bitcast.7, bf16[4,3,32,512]{3,2,1,0:T(8,128)(2,1)} %bitcast.5, bf16[4,3,32,512]{3,2,1,0:T(8,128)(2,1)} %bitcast.3, s32[]{:T(128)S(6)} %select_n.82), kind=kLoop, calls=%fused_computation.26 | loop fusion | flops 851968 | bytes 1703944 | tf_op jit(solution)/shard_map/sum_over_near_z/add | solution.py:56
  35.6 1.9 %collective-permute-start.4 = (bf16[4,32,512]{2,1,0:T(8,128)(2,1)S(1)}, bf16[4,32,512]{2,1,0:T(8,128)(2,1)S(1)}, u32[]{:S(2)}, u32[]{:S(2)}) collective-permute-start(bf16[4,32,512]{2,1,0:T(8,128)(2,1)S(1)} %get-tuple-element.6), channel_id=1, source_target_pairs={{0,4},{4,8},{8,0},{12,16},{16,20},{20,12},{24,28},{28,32},{32,24},... | collective-permute-start | bytes 393224 | tf_op jit(solution)/shard_map/sum_over_near_z/ppermute | solution.py:19
  37.5 2.8 %collective-permute-start.9 = (bf16[512,512]{1,0:T(8,128)(2,1)S(1)}, bf16[512,512]{1,0:T(8,128)(2,1)S(1)}, u32[]{:S(2)}, u32[]{:S(2)}) collective-permute-start(bf16[512,512]{1,0:T(8,128)(2,1)S(1)} %bitcast.105), channel_id=1, source_target_pairs={{0,48},{48,0},{1,49},{49,1},{2,50},{50,2},{3,51},{51,3},{4,52},{52... | collective-permute-start | bytes 1572872 | tf_op jit(solution)/shard_map/owner_roots/ppermute | solution.py:49
  40.4 0.6 dynamic_slice.144
  43.0 14.4 %collective-permute-start.5 = (bf16[32,512]{1,0:T(8,128)(2,1)S(1)}, bf16[32,512]{1,0:T(8,128)(2,1)S(1)}, u32[]{:S(2)}, u32[]{:S(2)}) collective-permute-start(bf16[32,512]{1,0:T(8,128)(2,1)S(1)} %get-tuple-element.8), channel_id=1, source_target_pairs={{0,24},{4,28},{8,32},{12,36},{16,40},{20,44},{24,0},{28,4},{32,8},... | collective-permute-start | bytes 98312 | tf_op jit(solution)/shard_map/sum_over_far_z/ppermute | solution.py:23
  57.5 3.5 %collective-permute-start.6 = (bf16[32,512]{1,0:T(8,128)(2,1)S(1)}, bf16[32,512]{1,0:T(8,128)(2,1)S(1)}, u32[]{:S(2)}, u32[]{:S(2)}) collective-permute-start(bf16[32,512]{1,0:T(8,128)(2,1)S(1)} %get-tuple-element.10), channel_id=1, source_target_pairs={{0,12},{4,16},{8,20},{12,24},{16,28},{20,32},{24,36},{28,40},{32,4... | collective-permute-start | bytes 98312 | tf_op jit(solution)/shard_map/sum_over_far_z/ppermute | solution.py:23
  61.0 4.7 %collective-permute-start.7 = (bf16[32,512]{1,0:T(8,128)(2,1)S(1)}, bf16[32,512]{1,0:T(8,128)(2,1)S(1)}, u32[]{:S(2)}, u32[]{:S(2)}) collective-permute-start(bf16[32,512]{1,0:T(8,128)(2,1)S(1)} %get-tuple-element.9), channel_id=1, source_target_pairs={{0,36},{4,40},{8,44},{12,0},{16,4},{20,8},{24,12},{28,16},{32,20},... | collective-permute-start | bytes 98312 | tf_op jit(solution)/shard_map/sum_over_far_z/ppermute | solution.py:23
  66.1 1.7 %collective-permute-done.7 = bf16[32,512]{1,0:T(8,128)(2,1)S(1)} collective-permute-done((bf16[32,512]{1,0:T(8,128)(2,1)S(1)}, bf16[32,512]{1,0:T(8,128)(2,1)S(1)}, u32[]{:S(2)}, u32[]{:S(2)}) %collective-permute-start.7) | collective-permute-done | bytes 32800 | tf_op jit(solution)/shard_map/sum_over_far_z/ppermute | solution.py:23
  67.8 22.0 %all_gather.3 = bf16[512,512]{1,0:T(8,128)(2,1)S(1)} all-gather(bf16[32,512]{1,0:T(8,128)(2,1)S(1)} %fusion.25), channel_id=1, replica_groups=mesh['y'=8,'c'=2,'z'=12,'x'=4] {'y','c'}, dimensions={0}, use_global_device_ids=true | all-gather | bytes 557056 | tf_op jit(solution)/shard_map/whole_block/all_gather | solution.py:69
  90.1 0.3 fusion.9
  90.5 1.0 fusion
  91.5 4.0 %all-to-all-start = ((bf16[8,32,512]{2,1,0:T(8,128)(2,1)}), bf16[8,32,512]{2,1,0:T(8,128)(2,1)S(1)}, u32[]{:S(2)}, u32[]{:S(2)}) async-start(bf16[8,32,512]{2,1,0:T(8,128)(2,1)} %bitcast.25), calls=%async_computation | async-start | bytes 524288 | tf_op jit(solution)/shard_map/direction/all_to_all | solution.py:75
  95.5 0.9 fusion.2
  96.4 0.9 fusion.4
  97.3 10.4 %all-to-all-done = bf16[8,32,512]{2,1,0:T(8,128)(2,1)S(1)} async-done(((bf16[8,32,512]{2,1,0:T(8,128)(2,1)}), bf16[8,32,512]{2,1,0:T(8,128)(2,1)S(1)}, u32[]{:S(2)}, u32[]{:S(2)}) %all-to-all-start) | async-done | bytes 262176 | tf_op jit(solution)/shard_map/direction/all_to_all | solution.py:75
  107.8 0.6 constant_dynamic-slice_fusion
  (24 shorter events, 0.7 us)
Async XLA Ops:
  0.7 36.9 %copy-start = (bf16[1,1,512,512]{3,2,1,0:T(8,128)(2,1)S(1)}, bf16[1,1,512,512]{3,2,1,0:T(8,128)(2,1)}, u32[]{:S(2)}) copy-start(bf16[1,1,512,512]{3,2,1,0:T(8,128)(2,1)} %param.11) | copy-start | bytes 1572868
  0.7 39.7 %copy-start.4 = (s32[48]{0:T(128)S(1)}, s32[48]{0:T(128)}, u32[]{:S(2)}) copy-start(s32[48]{0:T(128)} %param.7) | copy-start | bytes 580
  0.7 65.1 %copy-start.1 = (bf16[1,1,512,512]{3,2,1,0:T(8,128)(2,1)S(1)}, bf16[1,1,512,512]{3,2,1,0:T(8,128)(2,1)}, u32[]{:S(2)}) copy-start(bf16[1,1,512,512]{3,2,1,0:T(8,128)(2,1)} %param.10) | copy-start | bytes 1572868
  3.3 22.7 %collective-permute-start = (bf16[12,32,512]{2,1,0:T(8,128)(2,1)}, bf16[12,32,512]{2,1,0:T(8,128)(2,1)}, u32[]{:S(2)}, u32[]{:S(2)}) collective-permute-start(bf16[12,32,512]{2,1,0:T(8,128)(2,1)} %get-tuple-element.3), channel_id=1, source_target_pairs={{0,2},{1,3},{2,0},{3,1},{4,6},{5,7},{6,4},{7,5},{8,10},{9,11},{10,... | collective-permute-start | bytes 1179656 | tf_op jit(solution)/shard_map/sum_over_x/ppermute | solution.py:15
  8.8 17.2 %collective-permute-start.1 = (bf16[12,32,512]{2,1,0:T(8,128)(2,1)S(1)}, bf16[12,32,512]{2,1,0:T(8,128)(2,1)}, u32[]{:S(2)}, u32[]{:S(2)}) collective-permute-start(bf16[12,32,512]{2,1,0:T(8,128)(2,1)S(1)} %get-tuple-element.5), channel_id=1, source_target_pairs={{0,1},{1,2},{2,3},{3,0},{4,5},{5,6},{6,7},{7,4},{8,9},{9,10},{10,1... | collective-permute-start | bytes 1179656 | tf_op jit(solution)/shard_map/sum_over_x/ppermute | solution.py:15
  11.0 15.0 %collective-permute-start.2 = (bf16[12,32,512]{2,1,0:T(8,128)(2,1)S(1)}, bf16[12,32,512]{2,1,0:T(8,128)(2,1)}, u32[]{:S(2)}, u32[]{:S(2)}) collective-permute-start(bf16[12,32,512]{2,1,0:T(8,128)(2,1)S(1)} %get-tuple-element.4), channel_id=1, source_target_pairs={{0,3},{1,0},{2,1},{3,2},{4,7},{5,4},{6,5},{7,6},{8,11},{9,8},{10,9... | collective-permute-start | bytes 1179656 | tf_op jit(solution)/shard_map/sum_over_x/ppermute | solution.py:15
  15.3 50.5 %collective-permute-start.8 = (bf16[512,512]{1,0:T(8,128)(2,1)}, bf16[512,512]{1,0:T(8,128)(2,1)S(1)}, u32[]{:S(2)}, u32[]{:S(2)}) collective-permute-start(bf16[512,512]{1,0:T(8,128)(2,1)} %bitcast.110), channel_id=1, source_target_pairs={{0,48},{48,0},{1,49},{49,1},{2,50},{50,2},{3,51},{51,3},{4,52},{52... | collective-permute-start | bytes 1572872 | tf_op jit(solution)/shard_map/owner_roots/ppermute | solution.py:48
  27.2 15.8 %collective-permute-start.3 = (bf16[4,32,512]{2,1,0:T(8,128)(2,1)S(1)}, bf16[4,32,512]{2,1,0:T(8,128)(2,1)S(1)}, u32[]{:S(2)}, u32[]{:S(2)}) collective-permute-start(bf16[4,32,512]{2,1,0:T(8,128)(2,1)S(1)} %fusion.15), channel_id=1, source_target_pairs={{0,8},{4,0},{8,4},{12,20},{16,12},{20,16},{24,32},{28,24},{32,28},... | collective-permute-start | bytes 393224 | tf_op jit(solution)/shard_map/sum_over_near_z/ppermute | solution.py:19
  35.6 7.4 %collective-permute-start.4 = (bf16[4,32,512]{2,1,0:T(8,128)(2,1)S(1)}, bf16[4,32,512]{2,1,0:T(8,128)(2,1)S(1)}, u32[]{:S(2)}, u32[]{:S(2)}) collective-permute-start(bf16[4,32,512]{2,1,0:T(8,128)(2,1)S(1)} %get-tuple-element.6), channel_id=1, source_target_pairs={{0,4},{4,8},{8,0},{12,16},{16,20},{20,12},{24,28},{28,32},{32,24},... | collective-permute-start | bytes 393224 | tf_op jit(solution)/shard_map/sum_over_near_z/ppermute | solution.py:19
  37.5 52.6 %collective-permute-start.9 = (bf16[512,512]{1,0:T(8,128)(2,1)S(1)}, bf16[512,512]{1,0:T(8,128)(2,1)S(1)}, u32[]{:S(2)}, u32[]{:S(2)}) collective-permute-start(bf16[512,512]{1,0:T(8,128)(2,1)S(1)} %bitcast.105), channel_id=1, source_target_pairs={{0,48},{48,0},{1,49},{49,1},{2,50},{50,2},{3,51},{51,3},{4,52},{52... | collective-permute-start | bytes 1572872 | tf_op jit(solution)/shard_map/owner_roots/ppermute | solution.py:49
  43.0 22.9 %collective-permute-start.5 = (bf16[32,512]{1,0:T(8,128)(2,1)S(1)}, bf16[32,512]{1,0:T(8,128)(2,1)S(1)}, u32[]{:S(2)}, u32[]{:S(2)}) collective-permute-start(bf16[32,512]{1,0:T(8,128)(2,1)S(1)} %get-tuple-element.8), channel_id=1, source_target_pairs={{0,24},{4,28},{8,32},{12,36},{16,40},{20,44},{24,0},{28,4},{32,8},... | collective-permute-start | bytes 98312 | tf_op jit(solution)/shard_map/sum_over_far_z/ppermute | solution.py:23
  57.5 8.6 %collective-permute-start.6 = (bf16[32,512]{1,0:T(8,128)(2,1)S(1)}, bf16[32,512]{1,0:T(8,128)(2,1)S(1)}, u32[]{:S(2)}, u32[]{:S(2)}) collective-permute-start(bf16[32,512]{1,0:T(8,128)(2,1)S(1)} %get-tuple-element.10), channel_id=1, source_target_pairs={{0,12},{4,16},{8,20},{12,24},{16,28},{20,32},{24,36},{28,40},{32,4... | collective-permute-start | bytes 98312 | tf_op jit(solution)/shard_map/sum_over_far_z/ppermute | solution.py:23
  61.0 6.8 %collective-permute-start.7 = (bf16[32,512]{1,0:T(8,128)(2,1)S(1)}, bf16[32,512]{1,0:T(8,128)(2,1)S(1)}, u32[]{:S(2)}, u32[]{:S(2)}) collective-permute-start(bf16[32,512]{1,0:T(8,128)(2,1)S(1)} %get-tuple-element.9), channel_id=1, source_target_pairs={{0,36},{4,40},{8,44},{12,0},{16,4},{20,8},{24,12},{28,16},{32,20},... | collective-permute-start | bytes 98312 | tf_op jit(solution)/shard_map/sum_over_far_z/ppermute | solution.py:23
  89.8 5.7 %copy-start.2 = (f32[1,32,512]{2,1,0:T(8,128)S(1)}, f32[1,32,512]{2,1,0:T(8,128)}, u32[]{:S(2)}) copy-start(f32[1,32,512]{2,1,0:T(8,128)} %param.9) | copy-start | bytes 196612
  90.1 6.3 %copy-start.3 = (f32[1,32,512]{2,1,0:T(8,128)S(1)}, f32[1,32,512]{2,1,0:T(8,128)}, u32[]{:S(2)}) copy-start(f32[1,32,512]{2,1,0:T(8,128)} %param.8) | copy-start | bytes 196612
  91.5 16.3 %all-to-all-start = ((bf16[8,32,512]{2,1,0:T(8,128)(2,1)}), bf16[8,32,512]{2,1,0:T(8,128)(2,1)S(1)}, u32[]{:S(2)}, u32[]{:S(2)}) async-start(bf16[8,32,512]{2,1,0:T(8,128)(2,1)} %bitcast.25), calls=%async_computation | async-start | bytes 524288 | tf_op jit(solution)/shard_map/direction/all_to_all | solution.py:75

commit v3 on v2

v3 whole, which is shorter than its diff:
```python
import jax
import jax.numpy as jnp
from jax import lax
from jax.sharding import Mesh
from jax.sharding import PartitionSpec as P

Y, C, Z, X = 8, 2, 12, 4
BF, F32 = jnp.bfloat16, jnp.float32
ROWS = ("y", "c")


def mm(a, b, ca, cb):
    return lax.dot_general(a, b, (((ca,), (cb,)), ((), ())), preferred_element_type=F32)


def pick(array, index, axis):
    return lax.dynamic_index_in_dim(array, index, axis, keepdims=False)


def added(parts):
    total = parts[0].astype(F32)
    for i in range(1, parts.shape[0]):
        total = total + parts[i].astype(F32)
    return total


def on_device(gradients, owners, left_factor, right_factor, left_root, right_root):
    rows, width = gradients.shape[2:]
    x, z = lax.axis_index("x"), lax.axis_index("z")
    me = lax.axis_index("y") * C + lax.axis_index("c")

    with jax.named_scope("sum_over_x"):
        by_x = gradients.reshape(Z, X, rows, width).astype(BF).transpose(1, 0, 2, 3)
        over_x = added(lax.all_to_all(by_x, "x", 0, 0, tiled=True))
    with jax.named_scope("owner_roots"):
        owner, core = owners[z * X + x], lax.axis_index("c")
        here = lax.rem(owner, C) == core
        left_root, right_root = left_root[0, 0], right_root[0, 0]
        left_inverse = jnp.where(here, left_root, lax.ppermute(left_root, "c", [(0, 1), (1, 0)]))
        right_inverse = jnp.where(here, right_root, lax.ppermute(right_root, "c", [(0, 1), (1, 0)]))
        left_inverse = pick(left_inverse.reshape(Y, C, rows, width), core, 1).reshape(-1, width)
    with jax.named_scope("sum_over_z"):
        my_rows = added(lax.all_to_all(over_x.astype(BF), "z", 0, 0, tiled=True)).astype(BF)
    with jax.named_scope("whole_block"):
        whole = lax.all_gather(my_rows, ROWS, axis=0, tiled=True)
    with jax.named_scope("direction"):
        left = mm(left_inverse, whole, 1, 0)
        high = lax.reduce_precision(left, 8, 7)
        low = (left - high).astype(BF)
        product = (mm(high.astype(BF), right_inverse, 1, 0) + mm(low, right_inverse, 1, 0)).astype(BF)
        every = lax.all_to_all(product.reshape(Y, rows, width), "y", 0, 0, tiled=True)
        directions = lax.dynamic_index_in_dim(every, lax.div(owner, C), 0, keepdims=True)
    with jax.named_scope("statistics"):
        columns = lax.dynamic_slice_in_dim(whole, me * rows, rows, 1)
        left_new = 0.9 * left_factor + 0.1 * mm(my_rows, whole, 1, 1)[None]
        right_new = 0.9 * right_factor + 0.1 * mm(columns, whole, 0, 0)[None]
    return left_new, right_new, directions


def solution(mesh):
    grid = Mesh(mesh.devices.reshape(Y, C, Z, X), ("y", "c", "z", "x"))
    dp = ("z", "x")
    stat = P(dp, ROWS, None)
    return jax.shard_map(
        on_device,
        mesh=grid,
        in_specs=(P(dp, None, ROWS, None), P(), stat, stat, P(dp, ROWS, None, None), P(dp, ROWS, None, None)),
        out_specs=(stat, stat, stat),
        check_vma=False,
    )
```

time: 109 us -> 102 us (0.936)
  starting transfers between devices: 59.9 us -> 32.1 us
  blocking collectives: 22 us -> 40.6 us
  waiting for transfers between devices: 12.3 us -> 18.1 us
  local copies, waits for them, and re-layouts: 5.11 us -> 1.36 us
    ppermute x8 -> x0, starting transfers between devices: 43.7 us -> none  [the longest x3 22.7 us: far_z(): lax.ppermute(value, 'z', [(i, (i + step * ZN) % Z) for i in range(Z)])]
    all_to_all x0 -> x1, starting transfers between devices: none -> 22.1 us  [on_device(): lax.all_to_all(over_x.astype(BF), 'z', 0, 0, tiled=True)]
    all_to_all x0 -> x1, blocking collectives: none -> 17.2 us  [on_device(): over_x = added(lax.all_to_all(by_x, 'x', 0, 0, tiled=True))]
    all_to_all x0 -> x1, waiting for transfers between devices: none -> 7.67 us  [on_device(): lax.all_to_all(over_x.astype(BF), 'z', 0, 0, tiled=True)]
    ppermute x1, starting transfers between devices: 9.43 us -> 4.05 us  [on_device(): lax.ppermute(left_root, 'c', [(0, 1), (1, 0)])]
    convert_element_type x1 -> x0, local copies, waits for them, and re-layouts: 2.64 us -> none  [on_device(): pick(mine, lax.rem(x + step, X), 1).astype(BF)]
    convert_element_type x2, other arithmetic: 0.07 us -> 2.18 us  [the longest x1 2.13 us: on_device(): by_x = gradients.reshape(Z, X, rows, width).astype(BF).transpose(1, 0, 2, 3)]
    ppermute x8 -> x0, waiting for transfers between devices: 1.88 us -> none  [the longest x3 1.87 us: far_z(): lax.ppermute(value, 'z', [(i, (i + step * ZN) % Z) for i in range(Z)])]
  transfers between devices with their start and end apart: 11 -> 4, of which waited for: 3 -> 2; matrix products, arithmetic and copies ran while one was open for 6% -> 3% of each run, Pallas kernels for 0% -> 0%
where the time goes in v3:
time: 102 us
  blocking collectives  40.6 us (40%)
  starting transfers between devices  32.1 us (31%)
  waiting for transfers between devices  18.1 us (18%)
  matrix products  3.45 us (3%)
  other arithmetic  3.22 us (3%)
  between operations  2.75 us (3%)
  local copies, waits for them, and re-layouts  1.36 us (1%)
    all_gather x1, blocking collectives, on_device(): whole = lax.all_gather(my_rows, ROWS, axis=0, tiled=True)  23.4 us
    all_to_all x1, starting transfers between devices, on_device(): lax.all_to_all(over_x.astype(BF), 'z', 0, 0, tiled=True)  22.1 us
    all_to_all x1, blocking collectives, on_device(): over_x = added(lax.all_to_all(by_x, 'x', 0, 0, tiled=True))  17.2 us
    all_to_all x1, waiting for transfers between devices, on_device(): lax.all_to_all(product.reshape(Y, rows, width), 'y', 0, 0, tiled=True)  10.4 us
    all_to_all x1, waiting for transfers between devices, on_device(): lax.all_to_all(over_x.astype(BF), 'z', 0, 0, tiled=True)  7.67 us
    ppermute x1, starting transfers between devices, on_device(): lax.ppermute(left_root, 'c', [(0, 1), (1, 0)])  4.05 us
    all_to_all x1, starting transfers between devices, on_device(): lax.all_to_all(product.reshape(Y, rows, width), 'y', 0, 0, tiled=True)  4.03 us
    dot_general x5, matrix products, mm(): lax.dot_general(a, b, (((ca,), (cb,)), ((), ())), preferred_element_type=...  3.45 us
  transfers between devices with their start and end apart: 4, of which 2 were waited for; matrix products, arithmetic and copies ran while one was open for 3% of the time, Pallas kernels for 0%

profile of v3, /device:TPU:1, one launch (start us, length us, event | category | flops | bytes accessed | tf_op | source)
XLA Modules:
  0.0 101.6 jit_solution(8645989241524701337)
XLA Ops:
  0.6 2.1 %convert_element_type.99 = bf16[1,48,32,512]{3,2,1,0:T(8,128)(2,1)S(1)} convert(f32[1,48,32,512]{3,2,1,0:T(8,128)} %param.6) | non-fusion elementwise | flops 786432 | bytes 4718592 | tf_op jit(solution)/shard_map/sum_over_x/convert_element_type | solution.py:33
  2.8 0.1 copy.9
  2.9 17.2 %all_to_all.15 = bf16[4,12,32,512]{3,2,1,0:T(8,128)(2,1)S(1)} all-to-all(bf16[4,12,32,512]{3,2,1,0:T(8,128)(2,1)S(1)} %copy.9), channel_id=1, replica_groups=mesh['y'=8,'c'=2,'z'=12,'x'=4] {'x'}, dimensions={0} | all-to-all | bytes 3145728 | tf_op jit(solution)/shard_map/sum_over_x/all_to_all | solution.py:34
  20.1 1.0 fusion.6
  21.1 22.1 %all-to-all-start.1 = ((bf16[12,32,512]{2,1,0:T(8,128)(2,1)}), bf16[12,32,512]{2,1,0:T(8,128)(2,1)S(1)}, u32[]{:S(2)}, u32[]{:S(2)}) async-start(bf16[12,32,512]{2,1,0:T(8,128)(2,1)} %fusion.6), calls=%async_computation.1 | async-start | bytes 786432 | tf_op jit(solution)/shard_map/sum_over_z/all_to_all | solution.py:43
  43.2 4.1 %collective-permute-start = (bf16[512,512]{1,0:T(8,128)(2,1)S(1)}, bf16[512,512]{1,0:T(8,128)(2,1)S(1)}, u32[]{:S(2)}, u32[]{:S(2)}) collective-permute-start(bf16[512,512]{1,0:T(8,128)(2,1)S(1)} %bitcast.39), channel_id=1, source_target_pairs={{0,48},{48,0},{1,49},{49,1},{2,50},{50,2},{3,51},{51,3},{4,52},{52... | collective-permute-start | bytes 1572872 | tf_op jit(solution)/shard_map/owner_roots/ppermute | solution.py:39
  47.3 1.9 %collective-permute-start.1 = (bf16[512,512]{1,0:T(8,128)(2,1)S(1)}, bf16[512,512]{1,0:T(8,128)(2,1)S(1)}, u32[]{:S(2)}, u32[]{:S(2)}) collective-permute-start(bf16[512,512]{1,0:T(8,128)(2,1)S(1)} %bitcast.36), channel_id=1, source_target_pairs={{0,48},{48,0},{1,49},{49,1},{2,50},{50,2},{3,51},{51,3},{4,52},{52... | collective-permute-start | bytes 1572872 | tf_op jit(solution)/shard_map/owner_roots/ppermute | solution.py:40
  49.2 0.6 dynamic_slice.15
  51.8 0.0 collective-permute-done
  51.8 0.1 broadcast_select_fusion.1
  51.9 7.7 %all-to-all-done.1 = bf16[12,32,512]{2,1,0:T(8,128)(2,1)S(1)} async-done(((bf16[12,32,512]{2,1,0:T(8,128)(2,1)}), bf16[12,32,512]{2,1,0:T(8,128)(2,1)S(1)}, u32[]{:S(2)}, u32[]{:S(2)}) %all-to-all-start.1) | async-done | bytes 393248 | tf_op jit(solution)/shard_map/sum_over_z/all_to_all | solution.py:43
  59.6 0.1 fusion.10
  59.6 23.4 %all_gather.3 = bf16[512,512]{1,0:T(8,128)(2,1)S(1)} all-gather(bf16[32,512]{1,0:T(8,128)(2,1)S(1)} %fusion.10), channel_id=1, replica_groups=mesh['y'=8,'c'=2,'z'=12,'x'=4] {'y','c'}, dimensions={0}, use_global_device_ids=true | all-gather | bytes 557056 | tf_op jit(solution)/shard_map/whole_block/all_gather | solution.py:45
  83.0 0.3 fusion.14
  83.3 0.0 collective-permute-done.1
  83.3 0.3 fusion.7
  83.6 0.0 copy-start.2
  83.6 0.0 copy-start.3
  83.6 1.0 %fusion = bf16[256,512]{1,0:T(8,128)(2,1)} fusion(f32[256,512]{1,0:T(8,128)S(1)} %fusion.7, f32[256,512]{1,0:T(8,128)S(1)} %fusion.14, bf16[512,512]{1,0:T(8,128)(2,1)S(1)} %collective-permute-done.1, pred[]{:T(512)S(6)} %eq.3, bf16[1,1,512,512]{3,2,1,0:T(8,128)(2,1)S(1)} %copy-done), kind=kOutput, calls=%fused_computation.1 | convolution fusion | flops 135004160 | bytes 2359297 | tf_op jit(solution)/shard_map/direction/dot_general | solution.py:13
  84.7 4.0 %all-to-all-start.2 = ((bf16[8,32,512]{2,1,0:T(8,128)(2,1)}), bf16[8,32,512]{2,1,0:T(8,128)(2,1)S(1)}, u32[]{:S(2)}, u32[]{:S(2)}) async-start(bf16[8,32,512]{2,1,0:T(8,128)(2,1)} %bitcast.11), calls=%async_computation.2 | async-start | bytes 524288 | tf_op jit(solution)/shard_map/direction/all_to_all | solution.py:51
  88.7 0.9 fusion.2
  89.6 0.9 fusion.4
  90.5 10.4 %all-to-all-done.2 = bf16[8,32,512]{2,1,0:T(8,128)(2,1)S(1)} async-done(((bf16[8,32,512]{2,1,0:T(8,128)(2,1)}), bf16[8,32,512]{2,1,0:T(8,128)(2,1)S(1)}, u32[]{:S(2)}, u32[]{:S(2)}) %all-to-all-start.2) | async-done | bytes 262176 | tf_op jit(solution)/shard_map/direction/all_to_all | solution.py:51
  101.0 0.6 constant_dynamic-slice_fusion
  (9 shorter events, 0.0 us)
Async XLA Ops:
  20.1 23.1 %copy-start.1 = (bf16[1,1,512,512]{3,2,1,0:T(8,128)(2,1)S(1)}, bf16[1,1,512,512]{3,2,1,0:T(8,128)(2,1)}, u32[]{:S(2)}) copy-start(bf16[1,1,512,512]{3,2,1,0:T(8,128)(2,1)} %param.10) | copy-start | bytes 1572868
  20.1 27.2 %copy-start = (bf16[1,1,512,512]{3,2,1,0:T(8,128)(2,1)S(1)}, bf16[1,1,512,512]{3,2,1,0:T(8,128)(2,1)}, u32[]{:S(2)}) copy-start(bf16[1,1,512,512]{3,2,1,0:T(8,128)(2,1)} %param.11) | copy-start | bytes 1572868
  20.1 29.1 %copy-start.4 = (s32[48]{0:T(128)S(1)}, s32[48]{0:T(128)}, u32[]{:S(2)}) copy-start(s32[48]{0:T(128)} %param.7) | copy-start | bytes 580
  21.1 38.5 %all-to-all-start.1 = ((bf16[12,32,512]{2,1,0:T(8,128)(2,1)}), bf16[12,32,512]{2,1,0:T(8,128)(2,1)S(1)}, u32[]{:S(2)}, u32[]{:S(2)}) async-start(bf16[12,32,512]{2,1,0:T(8,128)(2,1)} %fusion.6), calls=%async_computation.1 | async-start | bytes 786432 | tf_op jit(solution)/shard_map/sum_over_z/all_to_all | solution.py:43
  43.2 8.6 %collective-permute-start = (bf16[512,512]{1,0:T(8,128)(2,1)S(1)}, bf16[512,512]{1,0:T(8,128)(2,1)S(1)}, u32[]{:S(2)}, u32[]{:S(2)}) collective-permute-start(bf16[512,512]{1,0:T(8,128)(2,1)S(1)} %bitcast.39), channel_id=1, source_target_pairs={{0,48},{48,0},{1,49},{49,1},{2,50},{50,2},{3,51},{51,3},{4,52},{52... | collective-permute-start | bytes 1572872 | tf_op jit(solution)/shard_map/owner_roots/ppermute | solution.py:39
  47.3 36.0 %collective-permute-start.1 = (bf16[512,512]{1,0:T(8,128)(2,1)S(1)}, bf16[512,512]{1,0:T(8,128)(2,1)S(1)}, u32[]{:S(2)}, u32[]{:S(2)}) collective-permute-start(bf16[512,512]{1,0:T(8,128)(2,1)S(1)} %bitcast.36), channel_id=1, source_target_pairs={{0,48},{48,0},{1,49},{49,1},{2,50},{50,2},{3,51},{51,3},{4,52},{52... | collective-permute-start | bytes 1572872 | tf_op jit(solution)/shard_map/owner_roots/ppermute | solution.py:40
  83.6 5.1 %copy-start.2 = (f32[1,32,512]{2,1,0:T(8,128)S(1)}, f32[1,32,512]{2,1,0:T(8,128)}, u32[]{:S(2)}) copy-start(f32[1,32,512]{2,1,0:T(8,128)} %param.9) | copy-start | bytes 196612
  83.6 6.0 %copy-start.3 = (f32[1,32,512]{2,1,0:T(8,128)S(1)}, f32[1,32,512]{2,1,0:T(8,128)}, u32[]{:S(2)}) copy-start(f32[1,32,512]{2,1,0:T(8,128)} %param.8) | copy-start | bytes 196612
  84.7 16.3 %all-to-all-start.2 = ((bf16[8,32,512]{2,1,0:T(8,128)(2,1)}), bf16[8,32,512]{2,1,0:T(8,128)(2,1)S(1)}, u32[]{:S(2)}, u32[]{:S(2)}) async-start(bf16[8,32,512]{2,1,0:T(8,128)(2,1)} %bitcast.11), calls=%async_computation.2 | async-start | bytes 524288 | tf_op jit(solution)/shard_map/direction/all_to_all | solution.py:51

commit v4 on v3

v4 whole, which is shorter than its diff:
```python
import jax
import jax.numpy as jnp
from jax import lax
from jax.sharding import Mesh
from jax.sharding import PartitionSpec as P

Y, C, Z, X = 8, 2, 12, 4
BF, F32 = jnp.bfloat16, jnp.float32
ROWS = ("y", "c")


def along_x(value, step):
    return lax.ppermute(value, "x", [(i, (i + step) % X) for i in range(X)])


def mm(a, b, ca, cb):
    return lax.dot_general(a, b, (((ca,), (cb,)), ((), ())), preferred_element_type=F32)


def pick(array, index, axis):
    return lax.dynamic_index_in_dim(array, index, axis, keepdims=False)


def added(parts):
    total = parts[0].astype(F32)
    for i in range(1, parts.shape[0]):
        total = total + parts[i].astype(F32)
    return total


def on_device(gradients, owners, left_factor, right_factor, left_root, right_root):
    rows, width = gradients.shape[2:]
    x, z = lax.axis_index("x"), lax.axis_index("z")
    me = lax.axis_index("y") * C + lax.axis_index("c")

    mine = gradients.reshape(Z, X, rows, width)

    def column(step):
        return pick(mine, lax.rem(x + step, X), 1)

    with jax.named_scope("sum_over_x"):
        came = [along_x(column(step).astype(BF), step) for step in (2, 1, 3)]
        over_x = sum((v.astype(F32) for v in came), column(0))
    with jax.named_scope("owner_roots"):
        slots = jnp.concatenate(
            [left_root.reshape(Y * C, rows, width), right_root.reshape(Y * C, rows, width)], axis=1
        )
        roots = pick(lax.all_to_all(slots, ROWS, 0, 0, tiled=True), owners[z * X + x], 0)
        over_x, roots = lax.optimization_barrier((over_x.astype(BF), roots))
        right_inverse = lax.all_gather(roots[rows:], ROWS, axis=0, tiled=True)
    with jax.named_scope("sum_over_z"):
        exact = added(lax.all_to_all(over_x, "z", 0, 0, tiled=True))
        my_rows = exact.astype(BF)
    with jax.named_scope("whole_block"):
        my_rows, right_inverse = lax.optimization_barrier((my_rows, right_inverse))
        whole = lax.all_gather(my_rows, ROWS, axis=0, tiled=True)
    with jax.named_scope("direction"):
        rest = (exact - lax.reduce_precision(exact, 8, 7)).astype(BF)
        corner = lax.dynamic_slice_in_dim(roots[:rows], me * rows, rows, 1)
        left = mm(roots[:rows], whole, 1, 0) + mm(corner, rest, 1, 0)
        high = lax.reduce_precision(left, 8, 7)
        low = (left - high).astype(BF)
        product = mm(high.astype(BF), right_inverse, 1, 0) + mm(low, right_inverse, 1, 0)
        directions = product.astype(BF)[None]
    with jax.named_scope("statistics"):
        columns = lax.dynamic_slice_in_dim(whole, me * rows, rows, 1)
        left_new = 0.9 * left_factor + 0.1 * mm(my_rows, whole, 1, 1)[None]
        right_new = 0.9 * right_factor + 0.1 * mm(columns, whole, 0, 0)[None]
    return left_new, right_new, directions


def solution(mesh):
    grid = Mesh(mesh.devices.reshape(Y, C, Z, X), ("y", "c", "z", "x"))
    dp = ("z", "x")
    stat = P(dp, ROWS, None)
    return jax.shard_map(
        on_device,
        mesh=grid,
        in_specs=(P(dp, None, ROWS, None), P(), stat, stat, P(dp, ROWS, None, None), P(dp, ROWS, None, None)),
        out_specs=(stat, stat, stat),
        check_vma=False,
    )
```

time: 102 us -> 96.5 us (0.946)
  blocking collectives: 40.6 us -> 36.2 us
  waiting for transfers between devices: 18.1 us -> 16 us
  other arithmetic: 3.22 us -> 4.76 us
  starting transfers between devices: 32.1 us -> 30.6 us
  local copies, waits for them, and re-layouts: 1.36 us -> 2.54 us
    all_gather x0 -> x1, blocking collectives: none -> 17.7 us  [on_device(): right_inverse = lax.all_gather(roots[rows:], ROWS, axis=0, tiled=True)]
    all_to_all x1 -> x0, blocking collectives: 17.2 us -> none  [on_device(): over_x = added(lax.all_to_all(by_x, 'x', 0, 0, tiled=True))]
    all_to_all x2, waiting for transfers between devices: 18.1 us -> 2.6 us  [the longest x1 1.57 us: on_device(): lax.all_to_all(slots, ROWS, 0, 0, tiled=True)]
    ppermute x2 -> x3, waiting for transfers between devices: 0.01 us -> 13.4 us  [along_x(): return lax.ppermute(value, 'x', [(i, (i + step) % X) for i in range(X)])]
    all_gather x1, blocking collectives: 23.4 us -> 18.5 us  [on_device(): whole = lax.all_gather(my_rows, ROWS, axis=0, tiled=True)]
    all_to_all x2, starting transfers between devices: 26.2 us -> 23.4 us  [the longest x1 14.6 us: on_device(): lax.all_to_all(slots, ROWS, 0, 0, tiled=True)]
    concatenate x0 -> x1, other arithmetic: none -> 2.45 us  [on_device(): jnp.concatenate([left_root.reshape(Y * C, rows, width), right_root.reshap...]
    ppermute x2 -> x3, starting transfers between devices: 5.97 us -> 7.19 us  [along_x(): return lax.ppermute(value, 'x', [(i, (i + step) % X) for i in range(X)])]
  transfers between devices with their start and end apart: 4 -> 5, of which waited for: 2 -> 5; matrix products, arithmetic and copies ran while one was open for 3% -> 4% of each run, Pallas kernels for 0% -> 0%
where the time goes in v4:
time: 96.5 us; the launch traced here: 96 us
  blocking collectives  36.2 us (38%)
  starting transfers between devices  30.6 us (32%)
  waiting for transfers between devices  16 us (17%)
  other arithmetic  4.76 us (5%)
  matrix products  3.24 us (3%)
  between operations  2.69 us (3%)
  local copies, waits for them, and re-layouts  2.54 us (3%)
    all_gather x1, blocking collectives, on_device(): whole = lax.all_gather(my_rows, ROWS, axis=0, tiled=True)  18.5 us
    all_gather x1, blocking collectives, on_device(): right_inverse = lax.all_gather(roots[rows:], ROWS, axis=0, tiled=True)  17.7 us
    all_to_all x1, starting transfers between devices, on_device(): lax.all_to_all(slots, ROWS, 0, 0, tiled=True)  14.6 us
    ppermute x3, waiting for transfers between devices, along_x(): return lax.ppermute(value, 'x', [(i, (i + step) % X) for i in range(X)])  13.4 us
    all_to_all x1, starting transfers between devices, on_device(): exact = added(lax.all_to_all(over_x, 'z', 0, 0, tiled=True))  8.86 us
    ppermute x3, starting transfers between devices, along_x(): return lax.ppermute(value, 'x', [(i, (i + step) % X) for i in range(X)])  7.19 us
    dot_general x6, matrix products, mm(): lax.dot_general(a, b, (((ca,), (cb,)), ((), ())), preferred_element_type=...  3.24 us
    concatenate x1, other arithmetic, on_device(): jnp.concatenate([left_root.reshape(Y * C, rows, width), right_root.reshap...  2.45 us
  transfers between devices with their start and end apart: 5, of which 5 were waited for; matrix products, arithmetic and copies ran while one was open for 4% of the time, Pallas kernels for 0%

profile of v4, /device:TPU:1, one launch (start us, length us, event | category | flops | bytes accessed | tf_op | source)
XLA Modules:
  0.0 96.0 jit_solution(14987362179193697975)
XLA Ops:
  0.7 2.4 %pad_maximum_fusion = bf16[16,64,512]{2,1,0:T(8,128)(2,1)} fusion(bf16[16,32,512]{2,1,0:T(8,128)(2,1)} %bitcast.50, bf16[16,32,512]{2,1,0:T(8,128)(2,1)} %bitcast.51), kind=kLoop, calls=%fused_computation.10 | loop fusion | flops 2097152 | bytes 2097152 | tf_op jit(solution)/shard_map/owner_roots/concatenate | solution.py:45
  3.1 14.6 %all-to-all-start = ((bf16[16,64,512]{2,1,0:T(8,128)(2,1)}), bf16[16,64,512]{2,1,0:T(8,128)(2,1)}, u32[]{:S(2)}, u32[]{:S(2)}) async-start(bf16[16,64,512]{2,1,0:T(8,128)(2,1)} %pad_maximum_fusion), calls=%async_computation | async-start | bytes 2097152 | tf_op jit(solution)/shard_map/owner_roots/all_to_all | solution.py:48
  17.7 1.1 %fusion.10 = (bf16[12,32,512]{2,1,0:T(8,128)(2,1)}, bf16[12,32,512]{2,1,0:T(8,128)(2,1)}, bf16[12,32,512]{2,1,0:T(8,128)(2,1)S(1)}) fusion(f32[12,4,32,512]{3,2,1,0:T(8,128)S(1)} %bitcast.48, s32[]{:T(128)S(6)} %select_n.25, s32[]{:T(128)S(6)} %select_n.27, s32[]{:T(128)S(6)} %select_n.26), kind=kLoop, calls=%fused_computation.19 | loop fusion | bytes 2359308 | tf_op jit(solution)/shard_map/sum_over_x/convert_element_type | solution.py:42
  18.8 1.9 %collective-permute-start = (bf16[12,32,512]{2,1,0:T(8,128)(2,1)}, bf16[12,32,512]{2,1,0:T(8,128)(2,1)}, u32[]{:S(2)}, u32[]{:S(2)}) collective-permute-start(bf16[12,32,512]{2,1,0:T(8,128)(2,1)} %get-tuple-element.13), channel_id=1, source_target_pairs={{0,2},{1,3},{2,0},{3,1},{4,6},{5,7},{6,4},{7,5},{8,10},{9,11},{10,... | collective-permute-start | bytes 1179656 | tf_op jit(solution)/shard_map/sum_over_x/ppermute | solution.py:13
  20.7 1.9 %collective-permute-start.2 = (bf16[12,32,512]{2,1,0:T(8,128)(2,1)}, bf16[12,32,512]{2,1,0:T(8,128)(2,1)}, u32[]{:S(2)}, u32[]{:S(2)}) collective-permute-start(bf16[12,32,512]{2,1,0:T(8,128)(2,1)} %get-tuple-element.14), channel_id=1, source_target_pairs={{0,3},{1,0},{2,1},{3,2},{4,7},{5,4},{6,5},{7,6},{8,11},{9,8},{10,9... | collective-permute-start | bytes 1179656 | tf_op jit(solution)/shard_map/sum_over_x/ppermute | solution.py:13
  22.6 3.4 %collective-permute-start.1 = (bf16[12,32,512]{2,1,0:T(8,128)(2,1)S(1)}, bf16[12,32,512]{2,1,0:T(8,128)(2,1)}, u32[]{:S(2)}, u32[]{:S(2)}) collective-permute-start(bf16[12,32,512]{2,1,0:T(8,128)(2,1)S(1)} %get-tuple-element.15), channel_id=1, source_target_pairs={{0,1},{1,2},{2,3},{3,0},{4,5},{5,6},{6,7},{7,4},{8,9},{9,10},{10,1... | collective-permute-start | bytes 1179656 | tf_op jit(solution)/shard_map/sum_over_x/ppermute | solution.py:13
  26.0 0.6 dynamic_slice.30
  28.6 4.4 %collective-permute-done = bf16[12,32,512]{2,1,0:T(8,128)(2,1)} collective-permute-done((bf16[12,32,512]{2,1,0:T(8,128)(2,1)}, bf16[12,32,512]{2,1,0:T(8,128)(2,1)}, u32[]{:S(2)}, u32[]{:S(2)}) %collective-permute-start) | collective-permute-done | bytes 393248 | tf_op jit(solution)/shard_map/sum_over_x/ppermute | solution.py:13
  32.9 2.7 %collective-permute-done.2 = bf16[12,32,512]{2,1,0:T(8,128)(2,1)} collective-permute-done((bf16[12,32,512]{2,1,0:T(8,128)(2,1)}, bf16[12,32,512]{2,1,0:T(8,128)(2,1)}, u32[]{:S(2)}, u32[]{:S(2)}) %collective-permute-start.2) | collective-permute-done | bytes 393248 | tf_op jit(solution)/shard_map/sum_over_x/ppermute | solution.py:13
  35.6 6.3 %collective-permute-done.1 = bf16[12,32,512]{2,1,0:T(8,128)(2,1)} collective-permute-done((bf16[12,32,512]{2,1,0:T(8,128)(2,1)S(1)}, bf16[12,32,512]{2,1,0:T(8,128)(2,1)}, u32[]{:S(2)}, u32[]{:S(2)}) %collective-permute-start.1) | collective-permute-done | bytes 393248 | tf_op jit(solution)/shard_map/sum_over_x/ppermute | solution.py:13
  41.9 2.2 %fusion.8 = bf16[12,32,512]{2,1,0:T(8,128)(2,1)} fusion(bf16[12,32,512]{2,1,0:T(8,128)(2,1)} %collective-permute-done.2, bf16[12,32,512]{2,1,0:T(8,128)(2,1)} %collective-permute-done.1, bf16[12,32,512]{2,1,0:T(8,128)(2,1)} %collective-permute-done, f32[12,4,32,512]{3,2,1,0:T(8,128)S(1)} %bitcast.49, s32[]{:T(128)S(6)} %select_n.24), kind=kLoop, calls=%fused_computation.16 | loop fusion | flops 1376256 | bytes 2359300 | tf_op jit(solution)/shard_map/owner_roots/convert_element_type | solution.py:49
  44.2 1.6 %all-to-all-done = bf16[16,64,512]{2,1,0:T(8,128)(2,1)} async-done(((bf16[16,64,512]{2,1,0:T(8,128)(2,1)}), bf16[16,64,512]{2,1,0:T(8,128)(2,1)}, u32[]{:S(2)}, u32[]{:S(2)}) %all-to-all-start) | async-done | bytes 1048608 | tf_op jit(solution)/shard_map/owner_roots/all_to_all | solution.py:48
  45.8 0.8 dynamic-slice_bitcast_fusion
  46.6 8.9 %all-to-all-start.1 = ((bf16[12,32,512]{2,1,0:T(8,128)(2,1)}), bf16[12,32,512]{2,1,0:T(8,128)(2,1)S(1)}, u32[]{:S(2)}, u32[]{:S(2)}) async-start(bf16[12,32,512]{2,1,0:T(8,128)(2,1)} %fusion.8), calls=%async_computation.1 | async-start | bytes 786432 | tf_op jit(solution)/shard_map/sum_over_z/all_to_all | solution.py:52
  55.5 17.7 %all_gather.6 = bf16[512,512]{1,0:T(8,128)(2,1)S(1)} all-gather(bf16[32,512]{1,0:T(8,128)(2,1)S(1)} %get-tuple-element.17), channel_id=1, replica_groups=mesh['y'=8,'c'=2,'z'=12,'x'=4] {'y','c'}, dimensions={0}, use_global_device_ids=true | all-gather | bytes 557056 | tf_op jit(solution)/shard_map/owner_roots/all_gather | solution.py:50
  73.2 1.0 %all-to-all-done.1 = bf16[12,32,512]{2,1,0:T(8,128)(2,1)S(1)} async-done(((bf16[12,32,512]{2,1,0:T(8,128)(2,1)}), bf16[12,32,512]{2,1,0:T(8,128)(2,1)S(1)}, u32[]{:S(2)}, u32[]{:S(2)}) %all-to-all-start.1) | async-done | bytes 393248 | tf_op jit(solution)/shard_map/sum_over_z/all_to_all | solution.py:52
  74.2 0.1 bitcast_convert_fusion.2
  74.3 18.5 %all_gather.7 = bf16[512,512]{1,0:T(8,128)(2,1)S(1)} all-gather(bf16[32,512]{1,0:T(8,128)(2,1)S(1)} %get-tuple-element.9), channel_id=1, replica_groups=mesh['y'=8,'c'=2,'z'=12,'x'=4] {'y','c'}, dimensions={0}, use_global_device_ids=true | all-gather | bytes 557056 | tf_op jit(solution)/shard_map/whole_block/all_gather | solution.py:56
  92.8 0.2 fusion.21
  93.0 0.9 fusion.3
  93.9 0.9 fusion.1
  94.8 0.2 convolution_add_fusion
  95.0 0.2 fusion.17
  95.2 0.8 fusion.5
  (9 shorter events, 0.0 us)
Async XLA Ops:
  0.6 17.1 %copy-start = (f32[1,48,32,512]{3,2,1,0:T(8,128)S(1)}, f32[1,48,32,512]{3,2,1,0:T(8,128)}, u32[]{:S(2)}) copy-start(f32[1,48,32,512]{3,2,1,0:T(8,128)} %param.6) | copy-start | bytes 9437188
  0.6 25.4 %copy-start.3 = (s32[48]{0:T(128)S(1)}, s32[48]{0:T(128)}, u32[]{:S(2)}) copy-start(s32[48]{0:T(128)} %param.7) | copy-start | bytes 580
  3.1 42.7 %all-to-all-start = ((bf16[16,64,512]{2,1,0:T(8,128)(2,1)}), bf16[16,64,512]{2,1,0:T(8,128)(2,1)}, u32[]{:S(2)}, u32[]{:S(2)}) async-start(bf16[16,64,512]{2,1,0:T(8,128)(2,1)} %pad_maximum_fusion), calls=%async_computation | async-start | bytes 2097152 | tf_op jit(solution)/shard_map/owner_roots/all_to_all | solution.py:48
  18.8 14.1 %collective-permute-start = (bf16[12,32,512]{2,1,0:T(8,128)(2,1)}, bf16[12,32,512]{2,1,0:T(8,128)(2,1)}, u32[]{:S(2)}, u32[]{:S(2)}) collective-permute-start(bf16[12,32,512]{2,1,0:T(8,128)(2,1)} %get-tuple-element.13), channel_id=1, source_target_pairs={{0,2},{1,3},{2,0},{3,1},{4,6},{5,7},{6,4},{7,5},{8,10},{9,11},{10,... | collective-permute-start | bytes 1179656 | tf_op jit(solution)/shard_map/sum_over_x/ppermute | solution.py:13
  20.7 14.9 %collective-permute-start.2 = (bf16[12,32,512]{2,1,0:T(8,128)(2,1)}, bf16[12,32,512]{2,1,0:T(8,128)(2,1)}, u32[]{:S(2)}, u32[]{:S(2)}) collective-permute-start(bf16[12,32,512]{2,1,0:T(8,128)(2,1)} %get-tuple-element.14), channel_id=1, source_target_pairs={{0,3},{1,0},{2,1},{3,2},{4,7},{5,4},{6,5},{7,6},{8,11},{9,8},{10,9... | collective-permute-start | bytes 1179656 | tf_op jit(solution)/shard_map/sum_over_x/ppermute | solution.py:13
  22.6 19.3 %collective-permute-start.1 = (bf16[12,32,512]{2,1,0:T(8,128)(2,1)S(1)}, bf16[12,32,512]{2,1,0:T(8,128)(2,1)}, u32[]{:S(2)}, u32[]{:S(2)}) collective-permute-start(bf16[12,32,512]{2,1,0:T(8,128)(2,1)S(1)} %get-tuple-element.15), channel_id=1, source_target_pairs={{0,1},{1,2},{2,3},{3,0},{4,5},{5,6},{6,7},{7,4},{8,9},{9,10},{10,1... | collective-permute-start | bytes 1179656 | tf_op jit(solution)/shard_map/sum_over_x/ppermute | solution.py:13
  41.9 51.0 %copy-start.2 = (f32[1,32,512]{2,1,0:T(8,128)S(1)}, f32[1,32,512]{2,1,0:T(8,128)}, u32[]{:S(2)}) copy-start(f32[1,32,512]{2,1,0:T(8,128)} %param.8) | copy-start | bytes 196612
  41.9 51.9 %copy-start.1 = (f32[1,32,512]{2,1,0:T(8,128)S(1)}, f32[1,32,512]{2,1,0:T(8,128)}, u32[]{:S(2)}) copy-start(f32[1,32,512]{2,1,0:T(8,128)} %param.9) | copy-start | bytes 196612
  46.6 27.6 %all-to-all-start.1 = ((bf16[12,32,512]{2,1,0:T(8,128)(2,1)}), bf16[12,32,512]{2,1,0:T(8,128)(2,1)S(1)}, u32[]{:S(2)}, u32[]{:S(2)}) async-start(bf16[12,32,512]{2,1,0:T(8,128)(2,1)} %fusion.8), calls=%async_computation.1 | async-start | bytes 786432 | tf_op jit(solution)/shard_map/sum_over_z/all_to_all | solution.py:52

commit v5 on v4

v5 whole, which is shorter than its diff:
```python
import jax
import jax.numpy as jnp
from jax import lax
from jax.experimental import pallas as pl
from jax.experimental.pallas import tpu as pltpu
from jax.sharding import Mesh
from jax.sharding import PartitionSpec as P

Y, C, Z, X = 8, 2, 12, 4
BF, F32 = jnp.bfloat16, jnp.float32
ROWS = ("y", "c")


def along_x(value, step):
    return lax.ppermute(value, "x", [(i, (i + step) % X) for i in range(X)])


def mm(a, b, ca, cb):
    return lax.dot_general(a, b, (((ca,), (cb,)), ((), ())), preferred_element_type=F32)


def pick(array, index, axis):
    return lax.dynamic_index_in_dim(array, index, axis, keepdims=False)


def added(parts):
    total = parts[0].astype(F32)
    for i in range(1, parts.shape[0]):
        total = total + parts[i].astype(F32)
    return total


def stacked(left, right):
    count, rows, width = left.shape
    half = count // 2

    def kernel(left_ref, right_ref, out_ref, sems):
        copies = []
        for i in range(2):
            part = pl.ds(i * half, half)
            for j, ref in enumerate((left_ref, right_ref)):
                to = out_ref.at[part, pl.ds(j * rows, rows)]
                copies.append(pltpu.make_async_copy(ref.at[part], to, sems.at[2 * i + j]))
        for copy in copies:
            copy.start()
        for copy in copies:
            copy.wait()

    return pl.pallas_call(
        kernel,
        out_shape=jax.ShapeDtypeStruct((count, 2 * rows, width), left.dtype),
        in_specs=[pl.BlockSpec(memory_space=pl.ANY)] * 2,
        out_specs=pl.BlockSpec(memory_space=pl.ANY),
        scratch_shapes=[pltpu.SemaphoreType.DMA((4,))],
        cost_estimate=pl.CostEstimate(flops=0, bytes_accessed=4 * left.size * 2, transcendentals=0),
    )(left, right)


def after_gather(me, whole, right_inverse, left_rows, exact, left_factor, right_factor):
    rows, width = exact.shape
    slab = 128 // rows

    def kernel(me_ref, whole_ref, right_ref, lrows_ref, exact_ref, lf_ref, rf_ref, ln_ref, rn_ref, d_ref, rest, stat):
        me = me_ref[0]
        first = pl.multiple_of((me // slab) * 128, 128)
        mine = pl.multiple_of((me % slab) * rows, rows)
        block = whole_ref[...]
        exact = exact_ref[...]
        my_rows = exact.astype(BF)
        rest[...] = jnp.zeros_like(rest)
        rest[pl.ds(mine, rows), :] = (exact - my_rows.astype(F32)).astype(BF)
        left = mm(lrows_ref[...], block, 1, 0) + mm(lrows_ref[:, pl.ds(first, 128)], rest[...], 1, 0)
        high = left.astype(BF)
        low = (left - high.astype(F32)).astype(BF)
        right = right_ref[...]
        d_ref[0] = (mm(high, right, 1, 0) + mm(low, right, 1, 0)).astype(BF)
        ln_ref[...] = 0.9 * lf_ref[...] + 0.1 * mm(my_rows, block, 1, 1)[None]
        stat[...] = mm(whole_ref[:, pl.ds(first, 128)], block, 0, 0)
        rn_ref[...] = 0.9 * rf_ref[...] + 0.1 * stat[pl.ds(mine, rows), :][None]

    vmem = pl.BlockSpec(memory_space=pltpu.VMEM)
    stat_shape = jax.ShapeDtypeStruct((1, rows, width), F32)
    return pl.pallas_call(
        kernel,
        out_shape=(stat_shape, stat_shape, jax.ShapeDtypeStruct((1, rows, width), BF)),
        in_specs=[pl.BlockSpec(memory_space=pltpu.SMEM)] + [vmem] * 6,
        out_specs=(vmem, vmem, vmem),
        scratch_shapes=[pltpu.VMEM((128, width), BF), pltpu.VMEM((128, width), F32)],
        cost_estimate=pl.CostEstimate(flops=10**8, bytes_accessed=2 << 20, transcendentals=0),
    )(me, whole, right_inverse, left_rows, exact, left_factor, right_factor)


def x_sum(x, gradients, came):
    parts, _, rows, width = gradients.shape
    step = 4

    def kernel(x_ref, own_ref, a_ref, b_ref, c_ref, out_ref):
        total = own_ref[:, 0] + a_ref[...].astype(F32) + b_ref[...].astype(F32) + c_ref[...].astype(F32)
        out_ref[...] = total.astype(BF)

    part = pl.BlockSpec((step, rows, width), lambda i, x_ref: (i, 0, 0))
    own = pl.BlockSpec((step, 1, rows, width), lambda i, x_ref: (i, x_ref[0], 0, 0))
    return pl.pallas_call(
        kernel,
        out_shape=jax.ShapeDtypeStruct((parts, rows, width), BF),
        grid_spec=pltpu.PrefetchScalarGridSpec(
            num_scalar_prefetch=1, grid=(parts // step,), in_specs=[own, part, part, part], out_specs=part
        ),
        cost_estimate=pl.CostEstimate(flops=10**6, bytes_accessed=3 << 20, transcendentals=0),
    )(x, gradients, *came)


def on_device(gradients, owners, left_factor, right_factor, left_root, right_root):
    rows, width = gradients.shape[2:]
    x, z = lax.axis_index("x"), lax.axis_index("z")
    me = lax.axis_index("y") * C + lax.axis_index("c")
    mine = gradients.reshape(Z, X, rows, width)

    def column(step):
        return pick(mine, lax.rem(x + step, X), 1)

    with jax.named_scope("sum_over_x"):
        came = [along_x(column(step).astype(BF), step) for step in (2, 1, 3)]
        over_x = x_sum(x[None], mine, came)
    with jax.named_scope("owner_roots"):
        slots = stacked(left_root.reshape(Y * C, rows, width), right_root.reshape(Y * C, rows, width))
        roots = pick(lax.all_to_all(slots, ROWS, 0, 0, tiled=True), owners[z * X + x], 0)
        over_x, roots = lax.optimization_barrier((over_x, roots))
        right_inverse = lax.all_gather(roots[rows:], ROWS, axis=0, tiled=True)
    with jax.named_scope("sum_over_z"):
        exact = added(lax.all_to_all(over_x, "z", 0, 0, tiled=True))
        my_rows = exact.astype(BF)
    with jax.named_scope("whole_block"):
        my_rows, right_inverse = lax.optimization_barrier((my_rows, right_inverse))
        whole = lax.all_gather(my_rows, ROWS, axis=0, tiled=True)
    with jax.named_scope("direction_and_statistics"):
        return after_gather(me[None], whole, right_inverse, roots[:rows], exact, left_factor, right_factor)


def solution(mesh):
    grid = Mesh(mesh.devices.reshape(Y, C, Z, X), ("y", "c", "z", "x"))
    dp = ("z", "x")
    stat = P(dp, ROWS, None)
    return jax.shard_map(
        on_device,
        mesh=grid,
        in_specs=(P(dp, None, ROWS, None), P(), stat, stat, P(dp, ROWS, None, None), P(dp, ROWS, None, None)),
        out_specs=(stat, stat, stat),
        check_vma=False,
    )
```

time: 96.5 us -> 133 us (1.38)
  Pallas kernels: 0 us -> 38.6 us
  blocking collectives: 36.2 us -> 40.3 us
  other arithmetic: 4.76 us -> 0.69 us
  matrix products: 3.24 us -> 0 us
  waiting for transfers between devices: 16 us -> 14.1 us
  local copies, waits for them, and re-layouts: 2.54 us -> 3.88 us
    pallas_call x0 -> x3, Pallas kernels: none -> 38.6 us  [the longest x1 32.9 us: stacked(): pl.pallas_call(kernel, out_shape=jax.ShapeDtypeStruct((count, 2 * rows, w...]
    all_gather x1, blocking collectives: 17.7 us -> 22.2 us  [on_device(): right_inverse = lax.all_gather(roots[rows:], ROWS, axis=0, tiled=True)]
    dot_general x6 -> x0, matrix products: 3.24 us -> none  [mm(): lax.dot_general(a, b, (((ca,), (cb,)), ((), ())), preferred_element_type=...]
    concatenate x1 -> x0, other arithmetic: 2.45 us -> none  [on_device(): jnp.concatenate([left_root.reshape(Y * C, rows, width), right_root.reshap...]
    convert_element_type x1 -> x0, other arithmetic: 2.25 us -> none  [on_device(): over_x, roots = lax.optimization_barrier((over_x.astype(BF), roots))]
    all_to_all x1, starting transfers between devices: 8.86 us -> 10.8 us  [on_device(): exact = added(lax.all_to_all(over_x, 'z', 0, 0, tiled=True))]
    all_to_all x1, waiting for transfers between devices: 1.57 us -> 0.01 us  [on_device(): lax.all_to_all(slots, ROWS, 0, 0, tiled=True)]
  transfers between devices with their start and end apart: 5 -> 5, of which waited for: 5 -> 2; matrix products, arithmetic and copies ran while one was open for 4% -> 2% of each run, Pallas kernels for 0% -> 2%
where the time goes in v5:
time: 133 us; the launch traced here: 132 us
  blocking collectives  40.3 us (30%)
  Pallas kernels  38.6 us (29%)
  starting transfers between devices  31.9 us (24%)
  waiting for transfers between devices  14.1 us (11%)
  local copies, waits for them, and re-layouts  3.88 us (3%)
  between operations  2.68 us (2%)
    pallas_call x1, Pallas kernels, stacked(): pl.pallas_call(kernel, out_shape=jax.ShapeDtypeStruct((count, 2 * rows, w...  32.9 us
    all_gather x1, blocking collectives, on_device(): right_inverse = lax.all_gather(roots[rows:], ROWS, axis=0, tiled=True)  22.2 us
    all_gather x1, blocking collectives, on_device(): whole = lax.all_gather(my_rows, ROWS, axis=0, tiled=True)  18.1 us
    ppermute x3, waiting for transfers between devices, along_x(): return lax.ppermute(value, 'x', [(i, (i + step) % X) for i in range(X)])  14.1 us
    all_to_all x1, starting transfers between devices, on_device(): lax.all_to_all(slots, ROWS, 0, 0, tiled=True)  14 us
    all_to_all x1, starting transfers between devices, on_device(): exact = added(lax.all_to_all(over_x, 'z', 0, 0, tiled=True))  10.8 us
    ppermute x3, starting transfers between devices, along_x(): return lax.ppermute(value, 'x', [(i, (i + step) % X) for i in range(X)])  7.2 us
    pallas_call x1, Pallas kernels, x_sum(): pl.pallas_call(kernel, out_shape=jax.ShapeDtypeStruct((parts, rows, width...  3.07 us
  transfers between devices with their start and end apart: 5, of which 2 were waited for; matrix products, arithmetic and copies ran while one was open for 2% of the time, Pallas kernels for 2%

profile of v5, /device:TPU:1, one launch (start us, length us, event | category | flops | bytes accessed | tf_op | source)
XLA Modules:
  0.0 132.3 jit_solution(801742272312830870)
XLA Ops:
  0.6 0.0 copy-start.3
  0.6 32.9 %owner_roots.1 = bf16[16,64,512]{2,1,0:T(8,128)(2,1)} custom-call(bf16[16,32,512]{2,1,0:T(8,128)(2,1)} %bitcast.31, bf16[16,32,512]{2,1,0:T(8,128)(2,1)} %bitcast.32), custom_call_target="tpu_custom_call" | custom-call | bytes 2097152 | tf_op jit(solution)/shard_map/owner_roots/pallas_call | solution.py:49
  33.6 14.0 %all-to-all-start = ((bf16[16,64,512]{2,1,0:T(8,128)(2,1)}), bf16[16,64,512]{2,1,0:T(8,128)(2,1)S(1)}, u32[]{:S(2)}, u32[]{:S(2)}) async-start(bf16[16,64,512]{2,1,0:T(8,128)(2,1)} %owner_roots.1), calls=%async_computation | async-start | bytes 2097152 | tf_op jit(solution)/shard_map/owner_roots/all_to_all | solution.py:127
  47.5 1.8 %fusion.2 = (bf16[12,32,512]{2,1,0:T(8,128)(2,1)S(1)}, bf16[12,32,512]{2,1,0:T(8,128)(2,1)S(1)}, bf16[12,32,512]{2,1,0:T(8,128)(2,1)S(1)}) fusion(f32[12,4,32,512]{3,2,1,0:T(8,128)} %bitcast.29, s32[]{:T(128)S(6)} %select_n.19, s32[]{:T(128)S(6)} %select_n.18, s32[]{:T(128)S(6)} %select_n.17), kind=kLoop, calls=%fused_computation.5 | loop fusion | bytes 2359308 | tf_op jit(solution)/shard_map/sum_over_x/convert_element_type | solution.py:123
  49.3 1.9 %collective-permute-start.2 = (bf16[12,32,512]{2,1,0:T(8,128)(2,1)S(1)}, bf16[12,32,512]{2,1,0:T(8,128)(2,1)S(1)}, u32[]{:S(2)}, u32[]{:S(2)}) collective-permute-start(bf16[12,32,512]{2,1,0:T(8,128)(2,1)S(1)} %get-tuple-element.13), channel_id=1, source_target_pairs={{0,3},{1,0},{2,1},{3,2},{4,7},{5,4},{6,5},{7,6},{8,11},{9,8},{10,9... | collective-permute-start | bytes 1179656 | tf_op jit(solution)/shard_map/sum_over_x/ppermute | solution.py:15
  51.3 3.4 %collective-permute-start.1 = (bf16[12,32,512]{2,1,0:T(8,128)(2,1)S(1)}, bf16[12,32,512]{2,1,0:T(8,128)(2,1)S(1)}, u32[]{:S(2)}, u32[]{:S(2)}) collective-permute-start(bf16[12,32,512]{2,1,0:T(8,128)(2,1)S(1)} %get-tuple-element.14), channel_id=1, source_target_pairs={{0,1},{1,2},{2,3},{3,0},{4,5},{5,6},{6,7},{7,4},{8,9},{9,10},{10,1... | collective-permute-start | bytes 1179656 | tf_op jit(solution)/shard_map/sum_over_x/ppermute | solution.py:15
  54.6 1.9 %collective-permute-start = (bf16[12,32,512]{2,1,0:T(8,128)(2,1)S(1)}, bf16[12,32,512]{2,1,0:T(8,128)(2,1)S(1)}, u32[]{:S(2)}, u32[]{:S(2)}) collective-permute-start(bf16[12,32,512]{2,1,0:T(8,128)(2,1)S(1)} %get-tuple-element.15), channel_id=1, source_target_pairs={{0,2},{1,3},{2,0},{3,1},{4,6},{5,7},{6,4},{7,5},{8,10},{9,11},{10,... | collective-permute-start | bytes 1179656 | tf_op jit(solution)/shard_map/sum_over_x/ppermute | solution.py:15
  56.6 0.0 copy-done.3
  56.6 0.6 dynamic_slice.20
  59.1 2.6 %collective-permute-done.2.c_ref = bf16[12,32,512]{2,1,0:T(8,128)(2,1)S(1)} collective-permute-done((bf16[12,32,512]{2,1,0:T(8,128)(2,1)S(1)}, bf16[12,32,512]{2,1,0:T(8,128)(2,1)S(1)}, u32[]{:S(2)}, u32[]{:S(2)}) %collective-permute-start.2) | collective-permute-done | bytes 393248 | tf_op jit(solution)/shard_map/sum_over_x/ppermute | solution.py:15
  61.7 11.6 %collective-permute-done.1.b_ref = bf16[12,32,512]{2,1,0:T(8,128)(2,1)S(1)} collective-permute-done((bf16[12,32,512]{2,1,0:T(8,128)(2,1)S(1)}, bf16[12,32,512]{2,1,0:T(8,128)(2,1)S(1)}, u32[]{:S(2)}, u32[]{:S(2)}) %collective-permute-start.1) | collective-permute-done | bytes 393248 | tf_op jit(solution)/shard_map/sum_over_x/ppermute | solution.py:15
  73.3 0.0 collective-permute-done.a_ref
  73.3 0.0 copy-done
  73.3 0.8 copy-done.1
  74.0 0.1 copy-done.2
  74.1 3.1 %sum_over_x.1 = bf16[12,32,512]{2,1,0:T(8,128)(2,1)} custom-call(s32[1]{0:T(128)} %bitcast.1.x_ref, f32[12,4,32,512]{3,2,1,0:T(8,128)} %bitcast.30, bf16[12,32,512]{2,1,0:T(8,128)(2,1)} %copy-done.2, bf16[12,32,512]{2,1,0:T(8,128)(2,1)} %copy-done.1, bf16[12,32,512]{2,1,0:T(8,128)(2,1)} %copy-done), custom_call_target="tpu_custom_call" | custom-call | flops 1000000 | bytes 3145728 | tf_op jit(solution)/shard_map/sum_over_x/pallas_call | solution.py:103
  77.2 0.0 all-to-all-done
  77.2 10.8 %all-to-all-start.1 = ((bf16[12,32,512]{2,1,0:T(8,128)(2,1)}), bf16[12,32,512]{2,1,0:T(8,128)(2,1)S(1)}, u32[]{:S(2)}, u32[]{:S(2)}) async-start(bf16[12,32,512]{2,1,0:T(8,128)(2,1)} %sum_over_x.1), calls=%async_computation.1 | async-start | bytes 786432 | tf_op jit(solution)/shard_map/sum_over_z/all_to_all | solution.py:131
  88.0 0.6 fusion.4
  88.6 22.2 %all_gather.6.right_ref = bf16[512,512]{1,0:T(8,128)(2,1)} all-gather(bf16[32,512]{1,0:T(8,128)(2,1)S(1)} %get-tuple-element.17), channel_id=1, replica_groups=mesh['y'=8,'c'=2,'z'=12,'x'=4] {'y','c'}, dimensions={0}, use_global_device_ids=true | all-gather | bytes 557056 | tf_op jit(solution)/shard_map/owner_roots/all_gather | solution.py:129
  110.9 0.0 all-to-all-done.1
  110.9 0.7 fusion.3
  111.5 18.1 %all_gather.7.whole_ref = bf16[512,512]{1,0:T(8,128)(2,1)} all-gather(bf16[32,512]{1,0:T(8,128)(2,1)S(1)} %get-tuple-element.9), channel_id=1, replica_groups=mesh['y'=8,'c'=2,'z'=12,'x'=4] {'y','c'}, dimensions={0}, use_global_device_ids=true | all-gather | bytes 557056 | tf_op jit(solution)/shard_map/whole_block/all_gather | solution.py:135
  129.6 2.7 %direction_and_statistics.1 = (f32[1,32,512]{2,1,0:T(8,128)}, f32[1,32,512]{2,1,0:T(8,128)}, bf16[1,32,512]{2,1,0:T(8,128)(2,1)}) custom-call(s32[1]{0:T(128)} %bitcast.me_ref, bf16[512,512]{1,0:T(8,128)(2,1)} %all_gather.7.whole_ref, bf16[512,512]{1,0:T(8,128)(2,1)} %all_gather.6.right_ref, bf16[32,512]{1,0:T(8,128)(2,1)} %get-tuple-element.16.lrows_ref, ...), custom_call_target="tpu_custom_call" | custom-call | flops 100000000 | bytes 2097152 | tf_op jit(solution)/shard_map/direction_and_statistics/pallas_call | solution.py:83
  (4 shorter events, 0.0 us)
Async XLA Ops:
  0.6 55.9 %copy-start.3 = (s32[48]{0:T(128)S(1)}, s32[48]{0:T(128)}, u32[]{:S(2)}) copy-start(s32[48]{0:T(128)} %param.7) | copy-start | bytes 580
  33.6 43.7 %all-to-all-start = ((bf16[16,64,512]{2,1,0:T(8,128)(2,1)}), bf16[16,64,512]{2,1,0:T(8,128)(2,1)S(1)}, u32[]{:S(2)}, u32[]{:S(2)}) async-start(bf16[16,64,512]{2,1,0:T(8,128)(2,1)} %owner_roots.1), calls=%async_computation | async-start | bytes 2097152 | tf_op jit(solution)/shard_map/owner_roots/all_to_all | solution.py:127
  49.3 12.4 %collective-permute-start.2 = (bf16[12,32,512]{2,1,0:T(8,128)(2,1)S(1)}, bf16[12,32,512]{2,1,0:T(8,128)(2,1)S(1)}, u32[]{:S(2)}, u32[]{:S(2)}) collective-permute-start(bf16[12,32,512]{2,1,0:T(8,128)(2,1)S(1)} %get-tuple-element.13), channel_id=1, source_target_pairs={{0,3},{1,0},{2,1},{3,2},{4,7},{5,4},{6,5},{7,6},{8,11},{9,8},{10,9... | collective-permute-start | bytes 1179656 | tf_op jit(solution)/shard_map/sum_over_x/ppermute | solution.py:15
  51.3 22.0 %collective-permute-start.1 = (bf16[12,32,512]{2,1,0:T(8,128)(2,1)S(1)}, bf16[12,32,512]{2,1,0:T(8,128)(2,1)S(1)}, u32[]{:S(2)}, u32[]{:S(2)}) collective-permute-start(bf16[12,32,512]{2,1,0:T(8,128)(2,1)S(1)} %get-tuple-element.14), channel_id=1, source_target_pairs={{0,1},{1,2},{2,3},{3,0},{4,5},{5,6},{6,7},{7,4},{8,9},{9,10},{10,1... | collective-permute-start | bytes 1179656 | tf_op jit(solution)/shard_map/sum_over_x/ppermute | solution.py:15
  54.6 18.6 %collective-permute-start = (bf16[12,32,512]{2,1,0:T(8,128)(2,1)S(1)}, bf16[12,32,512]{2,1,0:T(8,128)(2,1)S(1)}, u32[]{:S(2)}, u32[]{:S(2)}) collective-permute-start(bf16[12,32,512]{2,1,0:T(8,128)(2,1)S(1)} %get-tuple-element.15), channel_id=1, source_target_pairs={{0,2},{1,3},{2,0},{3,1},{4,6},{5,7},{6,4},{7,5},{8,10},{9,11},{10,... | collective-permute-start | bytes 1179656 | tf_op jit(solution)/shard_map/sum_over_x/ppermute | solution.py:15
  61.7 11.6 %copy-start = (bf16[12,32,512]{2,1,0:T(8,128)(2,1)}, bf16[12,32,512]{2,1,0:T(8,128)(2,1)S(1)}, u32[]{:S(2)}) copy-start(bf16[12,32,512]{2,1,0:T(8,128)(2,1)S(1)} %collective-permute-done.2.c_ref) | copy-start | bytes 1179652
  73.2 0.8 copy-start.1
  73.3 0.9 copy-start.2
  77.2 33.6 %all-to-all-start.1 = ((bf16[12,32,512]{2,1,0:T(8,128)(2,1)}), bf16[12,32,512]{2,1,0:T(8,128)(2,1)S(1)}, u32[]{:S(2)}, u32[]{:S(2)}) async-start(bf16[12,32,512]{2,1,0:T(8,128)(2,1)} %sum_over_x.1), calls=%async_computation.1 | async-start | bytes 786432 | tf_op jit(solution)/shard_map/sum_over_z/all_to_all | solution.py:131

commit v6 on v5

v6 whole, which is shorter than its diff:
```python
import jax
import jax.numpy as jnp
from jax import lax
from jax.experimental import pallas as pl
from jax.experimental.pallas import tpu as pltpu
from jax.sharding import Mesh
from jax.sharding import PartitionSpec as P

Y, C, Z, X = 8, 2, 12, 4
BF, F32 = jnp.bfloat16, jnp.float32
ROWS = ("y", "c")


def along_x(value, step):
    return lax.ppermute(value, "x", [(i, (i + step) % X) for i in range(X)])


def mm(a, b, ca, cb):
    return lax.dot_general(a, b, (((ca,), (cb,)), ((), ())), preferred_element_type=F32)


def pick(array, index, axis):
    return lax.dynamic_index_in_dim(array, index, axis, keepdims=False)


def added(parts):
    total = parts[0].astype(F32)
    for i in range(1, parts.shape[0]):
        total = total + parts[i].astype(F32)
    return total


def in_vmem(value):
    return pltpu.with_memory_space_constraint(value, pltpu.VMEM)


SMEM, VMEM = pl.BlockSpec(memory_space=pltpu.SMEM), pl.BlockSpec(memory_space=pltpu.VMEM)


def cost(flops, size):
    return pl.CostEstimate(flops=flops, bytes_accessed=size, transcendentals=0)


def rows_to_send(where, left, right, other_left, other_right):
    _, _, rows, width = left.shape

    def kernel(where_ref, left_ref, right_ref, other_left_ref, other_right_ref, out_ref):
        core = where_ref[1]

        @pl.when(where_ref[0] == 1)
        def _():
            out_ref[:, :rows] = left_ref[:, core]
            out_ref[:, rows:] = right_ref[:, core]

        @pl.when(where_ref[0] == 0)
        def _():
            out_ref[:, :rows] = other_left_ref[:, core]
            out_ref[:, rows:] = other_right_ref[:, core]

    return pl.pallas_call(
        kernel,
        out_shape=pltpu.VMEM((Y, 2 * rows, width), BF),
        in_specs=[SMEM] + [VMEM] * 4,
        out_specs=VMEM,
        cost_estimate=cost(10**6, 1 << 20),
    )(where, *(in_vmem(v) for v in (left, right, other_left, other_right)))


def x_sum(own, came):
    def kernel(own_ref, a_ref, b_ref, c_ref, out_ref):
        for i in range(own_ref.shape[0]):
            total = own_ref[i] + a_ref[i].astype(F32) + b_ref[i].astype(F32) + c_ref[i].astype(F32)
            out_ref[i] = total.astype(BF)

    return pl.pallas_call(
        kernel,
        out_shape=pltpu.VMEM(own.shape, BF),
        in_specs=[VMEM] * 4,
        out_specs=VMEM,
        cost_estimate=cost(5 * 10**10, 2 << 20),
    )(*(in_vmem(v) for v in (own, *came)))


def after_gather(me, whole, right_inverse, left_rows, exact, left_factor, right_factor):
    rows, width = exact.shape
    slab = 128 // rows

    def kernel(me_ref, whole_ref, right_ref, lrows_ref, exact_ref, lf_ref, rf_ref, ln_ref, rn_ref, d_ref, rest, stat):
        me = me_ref[0]
        first = pl.multiple_of((me // slab) * 128, 128)
        mine = pl.multiple_of((me % slab) * rows, rows)
        block = whole_ref[...]
        exact = exact_ref[...]
        my_rows = exact.astype(BF)
        rest[...] = jnp.zeros_like(rest)
        rest[pl.ds(mine, rows), :] = (exact - my_rows.astype(F32)).astype(BF)
        left = mm(lrows_ref[...], block, 1, 0) + mm(lrows_ref[:, pl.ds(first, 128)], rest[...], 1, 0)
        high = left.astype(BF)
        low = (left - high.astype(F32)).astype(BF)
        right = right_ref[...]
        d_ref[0] = (mm(high, right, 1, 0) + mm(low, right, 1, 0)).astype(BF)
        ln_ref[...] = 0.9 * lf_ref[...] + 0.1 * mm(my_rows, block, 1, 1)[None]
        stat[...] = mm(whole_ref[:, pl.ds(first, 128)], block, 0, 0)
        rn_ref[...] = 0.9 * rf_ref[...] + 0.1 * stat[pl.ds(mine, rows), :][None]

    stat_shape = jax.ShapeDtypeStruct((1, rows, width), F32)
    return pl.pallas_call(
        kernel,
        out_shape=(stat_shape, stat_shape, jax.ShapeDtypeStruct((1, rows, width), BF)),
        in_specs=[SMEM] + [VMEM] * 6,
        out_specs=(VMEM, VMEM, VMEM),
        scratch_shapes=[pltpu.VMEM((128, width), BF), pltpu.VMEM((128, width), F32)],
        cost_estimate=cost(10**8, 2 << 20),
    )(me, *(in_vmem(v) for v in (whole, right_inverse, left_rows, exact, left_factor, right_factor)))


def on_device(gradients, owners, left_factor, right_factor, left_root, right_root):
    rows, width = gradients.shape[2:]
    x, z, core = lax.axis_index("x"), lax.axis_index("z"), lax.axis_index("c")
    me = lax.axis_index("y") * C + core
    mine = gradients.reshape(Z, X, rows, width)
    owner = owners[z * X + x]

    def column(step):
        return pick(mine, lax.rem(x + step, X), 1)

    with jax.named_scope("sum_over_x"):
        to_x = [column(step).astype(BF) for step in (2, 1, 3)]
        came = [along_x(v, step) for v, step in zip(to_x, (2, 1, 3))]
        over_x = x_sum(column(0), came)
    with jax.named_scope("owner_roots"):
        pair = [root.reshape(Y, C, rows, width) for root in (left_root, right_root)]
        others = [lax.ppermute(root.reshape(-1, width), "c", [(0, 1), (1, 0)]) for root in pair]
        where = jnp.stack([(lax.rem(owner, C) == core).astype(jnp.int32), core])
        slots = rows_to_send(where, *pair, *(v.reshape(pair[0].shape) for v in others))
        roots = pick(lax.all_to_all(slots, "y", 0, 0, tiled=True), lax.div(owner, C), 0)
        over_x, roots = lax.optimization_barrier((over_x, roots))
        right_inverse = lax.all_gather(roots[rows:], ROWS, axis=0, tiled=True)
    with jax.named_scope("sum_over_z"):
        exact = added(lax.all_to_all(over_x, "z", 0, 0, tiled=True))
        my_rows = exact.astype(BF)
    with jax.named_scope("whole_block"):
        my_rows, right_inverse = lax.optimization_barrier((my_rows, right_inverse))
        whole = lax.all_gather(my_rows, ROWS, axis=0, tiled=True)
    with jax.named_scope("direction_and_statistics"):
        return after_gather(me[None], whole, right_inverse, roots[:rows], exact, left_factor, right_factor)


def solution(mesh):
    grid = Mesh(mesh.devices.reshape(Y, C, Z, X), ("y", "c", "z", "x"))
    dp = ("z", "x")
    stat = P(dp, ROWS, None)
    return jax.shard_map(
        on_device,
        mesh=grid,
        in_specs=(P(dp, None, ROWS, None), P(), stat, stat, P(dp, ROWS, None, None), P(dp, ROWS, None, None)),
        out_specs=(stat, stat, stat),
        check_vma=False,
    )
```

time: 133 us -> 103 us (0.77)
  Pallas kernels: 38.6 us -> 5.1 us
  starting transfers between devices: 31.9 us -> 36.5 us
  blocking collectives: 40.3 us -> 36.2 us
  waiting for transfers between devices: 14.1 us -> 15.7 us
    pallas_call x2, Pallas kernels: 36 us -> 3.68 us  [the longest x1 2.17 us: x_sum(): pl.pallas_call(kernel, out_shape=pltpu.VMEM(own.shape, BF), in_specs=[VME...]
    ppermute x0 -> x2, starting transfers between devices: none -> 14.5 us  [on_device(): lax.ppermute(root.reshape(-1, width), 'c', [(0, 1), (1, 0)])]
    all_to_all x1, waiting for transfers between devices: 0.01 us -> 11 us  [on_device(): lax.all_to_all(slots, 'y', 0, 0, tiled=True)]
    all_to_all x1, starting transfers between devices: 14 us -> 3.49 us  [on_device(): lax.all_to_all(slots, 'y', 0, 0, tiled=True)]
    ppermute x3, waiting for transfers between devices: 14.1 us -> 4.64 us  [along_x(): return lax.ppermute(value, 'x', [(i, (i + step) % X) for i in range(X)])]
    all_gather x1, blocking collectives: 22.2 us -> 18.7 us  [on_device(): right_inverse = lax.all_gather(roots[rows:], ROWS, axis=0, tiled=True)]
  transfers between devices with their start and end apart: 5 -> 7, of which waited for: 2 -> 2; matrix products, arithmetic and copies ran while one was open for 2% -> 6% of each run, Pallas kernels for 2% -> 4%
where the time goes in v6:
time: 103 us; the launch traced here: 102 us
  starting transfers between devices  36.5 us (35%)
  blocking collectives  36.2 us (35%)
  waiting for transfers between devices  15.7 us (15%)
  local copies, waits for them, and re-layouts  5.2 us (5%)
  Pallas kernels  5.1 us (5%)
  between operations  2.8 us (3%)
    all_gather x1, blocking collectives, on_device(): right_inverse = lax.all_gather(roots[rows:], ROWS, axis=0, tiled=True)  18.7 us
    all_gather x1, blocking collectives, on_device(): whole = lax.all_gather(my_rows, ROWS, axis=0, tiled=True)  17.5 us
    ppermute x2, starting transfers between devices, on_device(): lax.ppermute(root.reshape(-1, width), 'c', [(0, 1), (1, 0)])  14.5 us
    all_to_all x1, waiting for transfers between devices, on_device(): lax.all_to_all(slots, 'y', 0, 0, tiled=True)  11 us
    all_to_all x1, starting transfers between devices, on_device(): exact = added(lax.all_to_all(over_x, 'z', 0, 0, tiled=True))  10.1 us
    ppermute x3, starting transfers between devices, along_x(): return lax.ppermute(value, 'x', [(i, (i + step) % X) for i in range(X)])  8.4 us
    ppermute x3, waiting for transfers between devices, along_x(): return lax.ppermute(value, 'x', [(i, (i + step) % X) for i in range(X)])  4.64 us
    all_to_all x1, starting transfers between devices, on_device(): lax.all_to_all(slots, 'y', 0, 0, tiled=True)  3.49 us
  transfers between devices with their start and end apart: 7, of which 2 were waited for; matrix products, arithmetic and copies ran while one was open for 6% of the time, Pallas kernels for 4%

profile of v6, /device:TPU:1, one launch (start us, length us, event | category | flops | bytes accessed | tf_op | source)
XLA Modules:
  0.0 102.1 jit_solution(216725135609388313)
XLA Ops:
  0.7 12.6 %collective-permute-start.3 = (bf16[512,512]{1,0:T(8,128)(2,1)}, bf16[512,512]{1,0:T(8,128)(2,1)S(1)}, u32[]{:S(2)}, u32[]{:S(2)}) collective-permute-start(bf16[512,512]{1,0:T(8,128)(2,1)} %bitcast.36), channel_id=1, source_target_pairs={{0,48},{48,0},{1,49},{49,1},{2,50},{50,2},{3,51},{51,3},{4,52},{52... | collective-permute-start | bytes 1572872 | tf_op jit(solution)/shard_map/owner_roots/ppermute | solution.py:133
  13.2 1.9 %collective-permute-start.4 = (bf16[512,512]{1,0:T(8,128)(2,1)}, bf16[512,512]{1,0:T(8,128)(2,1)S(1)}, u32[]{:S(2)}, u32[]{:S(2)}) collective-permute-start(bf16[512,512]{1,0:T(8,128)(2,1)} %bitcast.38), channel_id=1, source_target_pairs={{0,48},{48,0},{1,49},{49,1},{2,50},{50,2},{3,51},{51,3},{4,52},{52... | collective-permute-start | bytes 1572872 | tf_op jit(solution)/shard_map/owner_roots/ppermute | solution.py:133
  15.2 2.7 %fusion.2 = (bf16[12,32,512]{2,1,0:T(8,128)(2,1)}, bf16[12,32,512]{2,1,0:T(8,128)(2,1)}, bf16[12,32,512]{2,1,0:T(8,128)(2,1)}) fusion(f32[12,4,32,512]{3,2,1,0:T(8,128)} %bitcast.42, s32[]{:T(128)S(6)} %select_n.23, s32[]{:T(128)S(6)} %select_n.22, s32[]{:T(128)S(6)} %select_n.21), kind=kLoop, calls=%fused_computation.6 | loop fusion | bytes 2359308 | tf_op jit(solution)/shard_map/sum_over_x/convert_element_type | solution.py:128
  17.9 1.9 %collective-permute-start = (bf16[12,32,512]{2,1,0:T(8,128)(2,1)}, bf16[12,32,512]{2,1,0:T(8,128)(2,1)}, u32[]{:S(2)}, u32[]{:S(2)}) collective-permute-start(bf16[12,32,512]{2,1,0:T(8,128)(2,1)} %get-tuple-element.15), channel_id=1, source_target_pairs={{0,2},{1,3},{2,0},{3,1},{4,6},{5,7},{6,4},{7,5},{8,10},{9,11},{10,... | collective-permute-start | bytes 1179656 | tf_op jit(solution)/shard_map/sum_over_x/ppermute | solution.py:15
  19.8 1.9 %collective-permute-start.1 = (bf16[12,32,512]{2,1,0:T(8,128)(2,1)}, bf16[12,32,512]{2,1,0:T(8,128)(2,1)}, u32[]{:S(2)}, u32[]{:S(2)}) collective-permute-start(bf16[12,32,512]{2,1,0:T(8,128)(2,1)} %get-tuple-element.14), channel_id=1, source_target_pairs={{0,1},{1,2},{2,3},{3,0},{4,5},{5,6},{6,7},{7,4},{8,9},{9,10},{10,1... | collective-permute-start | bytes 1179656 | tf_op jit(solution)/shard_map/sum_over_x/ppermute | solution.py:15
  21.7 4.6 %collective-permute-start.2 = (bf16[12,32,512]{2,1,0:T(8,128)(2,1)}, bf16[12,32,512]{2,1,0:T(8,128)(2,1)}, u32[]{:S(2)}, u32[]{:S(2)}) collective-permute-start(bf16[12,32,512]{2,1,0:T(8,128)(2,1)} %get-tuple-element.13), channel_id=1, source_target_pairs={{0,3},{1,0},{2,1},{3,2},{4,7},{5,4},{6,5},{7,6},{8,11},{9,8},{10,9... | collective-permute-start | bytes 1179656 | tf_op jit(solution)/shard_map/sum_over_x/ppermute | solution.py:15
  26.3 1.2 %dynamic_slice.24 = s32[1]{0:T(128)} dynamic-slice(s32[48]{0:T(128)} %param.7, s32[]{:T(128)S(6)} %select_n.24), dynamic_slice_sizes={1} | dynamic-slice | bytes 12 | tf_op jit(solution)/shard_map/dynamic_slice | solution.py:122
  29.5 0.6 pad_add_fusion.where_ref
  30.1 1.2 %dynamic-slice_bitcast_fusion.own_ref = f32[12,32,512]{2,1,0:T(8,128)S(1)} fusion(f32[12,4,32,512]{3,2,1,0:T(8,128)} %bitcast.43, s32[]{:T(128)S(6)} %select_n.20), kind=kLoop, calls=%fused_computation.3 | loop fusion | bytes 1572868 | tf_op jit(solution)/shard_map/sum_over_x/jit(dynamic_index_in_dim)/squeeze | solution.py:23
  31.3 0.0 collective-permute-done.3
  31.4 1.5 %owner_roots.1 = bf16[8,64,512]{2,1,0:T(8,128)(2,1)} custom-call(s32[2]{0:T(128)} %pad_add_fusion.where_ref, bf16[8,2,32,512]{3,2,1,0:T(8,128)(2,1)S(1)} %bitcast.37, bf16[8,2,32,512]{3,2,1,0:T(8,128)(2,1)S(1)} %bitcast.39, bf16[8,2,32,512]{3,2,1,0:T(8,128)(2,1)S(1)} %bitcast.40, bf16[8,2,32,512]{3,2,1,0:T(8,128)(2,1)S(1)} %bitcast.41), custom_call_target="tpu_custom_call" | custom-call | flops 1000000 | bytes 1048576 | tf_op jit(solution)/shard_map/owner_roots/pallas_call | solution.py:60
  32.9 3.5 %all-to-all-start = ((bf16[8,64,512]{2,1,0:T(8,128)(2,1)}), bf16[8,64,512]{2,1,0:T(8,128)(2,1)S(1)}, u32[]{:S(2)}, u32[]{:S(2)}) async-start(bf16[8,64,512]{2,1,0:T(8,128)(2,1)} %owner_roots.1), calls=%async_computation | async-start | bytes 1048576 | tf_op jit(solution)/shard_map/owner_roots/all_to_all | solution.py:136
  36.4 0.0 copy-start.2
  36.4 0.0 copy-start.3
  36.4 0.0 collective-permute-done.a_ref
  36.4 4.6 %collective-permute-done.1.b_ref = bf16[12,32,512]{2,1,0:T(8,128)(2,1)} collective-permute-done((bf16[12,32,512]{2,1,0:T(8,128)(2,1)}, bf16[12,32,512]{2,1,0:T(8,128)(2,1)}, u32[]{:S(2)}, u32[]{:S(2)}) %collective-permute-start.1) | collective-permute-done | bytes 393248 | tf_op jit(solution)/shard_map/sum_over_x/ppermute | solution.py:15
  41.1 0.0 collective-permute-done.2.c_ref
  41.1 2.2 %sum_over_x.1 = bf16[12,32,512]{2,1,0:T(8,128)(2,1)} custom-call(f32[12,32,512]{2,1,0:T(8,128)S(1)} %dynamic-slice_bitcast_fusion.own_ref, bf16[12,32,512]{2,1,0:T(8,128)(2,1)} %collective-permute-done.a_ref, bf16[12,32,512]{2,1,0:T(8,128)(2,1)} %collective-permute-done.1.b_ref, bf16[12,32,512]{2,1,0:T(8,128)(2,1)} %collective-permute-done.2.c_ref), custom_call_target="tpu_custom_call" | custom-call | flops 49999998976 | bytes 2097152 | tf_op jit(solution)/shard_map/sum_over_x/pallas_call | solution.py:75
  43.2 11.0 %all-to-all-done = bf16[8,64,512]{2,1,0:T(8,128)(2,1)S(1)} async-done(((bf16[8,64,512]{2,1,0:T(8,128)(2,1)}), bf16[8,64,512]{2,1,0:T(8,128)(2,1)S(1)}, u32[]{:S(2)}, u32[]{:S(2)}) %all-to-all-start) | async-done | bytes 524320 | tf_op jit(solution)/shard_map/owner_roots/all_to_all | solution.py:136
  54.3 10.1 %all-to-all-start.1 = ((bf16[12,32,512]{2,1,0:T(8,128)(2,1)}), bf16[12,32,512]{2,1,0:T(8,128)(2,1)S(1)}, u32[]{:S(2)}, u32[]{:S(2)}) async-start(bf16[12,32,512]{2,1,0:T(8,128)(2,1)} %sum_over_x.1), calls=%async_computation.1 | async-start | bytes 786432 | tf_op jit(solution)/shard_map/sum_over_z/all_to_all | solution.py:140
  64.4 18.7 %all_gather.6.right_ref = bf16[512,512]{1,0:T(8,128)(2,1)S(1)} all-gather(bf16[32,512]{1,0:T(8,128)(2,1)S(1)} %get-tuple-element.17), channel_id=1, replica_groups=mesh['y'=8,'c'=2,'z'=12,'x'=4] {'y','c'}, dimensions={0}, use_global_device_ids=true | all-gather | bytes 557056 | tf_op jit(solution)/shard_map/owner_roots/all_gather | solution.py:138
  83.0 0.1 fusion.3
  83.1 17.5 %all_gather.7.whole_ref = bf16[512,512]{1,0:T(8,128)(2,1)S(1)} all-gather(bf16[32,512]{1,0:T(8,128)(2,1)S(1)} %get-tuple-element.9), channel_id=1, replica_groups=mesh['y'=8,'c'=2,'z'=12,'x'=4] {'y','c'}, dimensions={0}, use_global_device_ids=true | all-gather | bytes 557056 | tf_op jit(solution)/shard_map/whole_block/all_gather | solution.py:144
  100.6 1.4 %direction_and_statistics.1 = (f32[1,32,512]{2,1,0:T(8,128)}, f32[1,32,512]{2,1,0:T(8,128)}, bf16[1,32,512]{2,1,0:T(8,128)(2,1)}) custom-call(s32[1]{0:T(128)} %bitcast.me_ref, bf16[512,512]{1,0:T(8,128)(2,1)S(1)} %all_gather.7.whole_ref, bf16[512,512]{1,0:T(8,128)(2,1)S(1)} %all_gather.6.right_ref, bf16[32,512]{1,0:T(8,128)(2,1)S(1)} %get-tuple-element.16.lrows_ref, ...), custom_call_target="tpu_custom_call" | custom-call | flops 100000000 | bytes 2097152 | tf_op jit(solution)/shard_map/direction_and_statistics/pallas_call | solution.py:107
  (10 shorter events, 0.0 us)
Async XLA Ops:
  0.6 30.7 %copy-start = (bf16[1,1,512,512]{3,2,1,0:T(8,128)(2,1)S(1)}, bf16[1,1,512,512]{3,2,1,0:T(8,128)(2,1)}, u32[]{:S(2)}) copy-start(bf16[1,1,512,512]{3,2,1,0:T(8,128)(2,1)} %param.10) | copy-start | bytes 1572868
  0.6 30.7 %copy-start.1 = (bf16[1,1,512,512]{3,2,1,0:T(8,128)(2,1)S(1)}, bf16[1,1,512,512]{3,2,1,0:T(8,128)(2,1)}, u32[]{:S(2)}) copy-start(bf16[1,1,512,512]{3,2,1,0:T(8,128)(2,1)} %param.11) | copy-start | bytes 1572868
  0.7 30.7 %collective-permute-start.3 = (bf16[512,512]{1,0:T(8,128)(2,1)}, bf16[512,512]{1,0:T(8,128)(2,1)S(1)}, u32[]{:S(2)}, u32[]{:S(2)}) collective-permute-start(bf16[512,512]{1,0:T(8,128)(2,1)} %bitcast.36), channel_id=1, source_target_pairs={{0,48},{48,0},{1,49},{49,1},{2,50},{50,2},{3,51},{51,3},{4,52},{52... | collective-permute-start | bytes 1572872 | tf_op jit(solution)/shard_map/owner_roots/ppermute | solution.py:133
  13.2 18.1 %collective-permute-start.4 = (bf16[512,512]{1,0:T(8,128)(2,1)}, bf16[512,512]{1,0:T(8,128)(2,1)S(1)}, u32[]{:S(2)}, u32[]{:S(2)}) collective-permute-start(bf16[512,512]{1,0:T(8,128)(2,1)} %bitcast.38), channel_id=1, source_target_pairs={{0,48},{48,0},{1,49},{49,1},{2,50},{50,2},{3,51},{51,3},{4,52},{52... | collective-permute-start | bytes 1572872 | tf_op jit(solution)/shard_map/owner_roots/ppermute | solution.py:133
  17.9 18.5 %collective-permute-start = (bf16[12,32,512]{2,1,0:T(8,128)(2,1)}, bf16[12,32,512]{2,1,0:T(8,128)(2,1)}, u32[]{:S(2)}, u32[]{:S(2)}) collective-permute-start(bf16[12,32,512]{2,1,0:T(8,128)(2,1)} %get-tuple-element.15), channel_id=1, source_target_pairs={{0,2},{1,3},{2,0},{3,1},{4,6},{5,7},{6,4},{7,5},{8,10},{9,11},{10,... | collective-permute-start | bytes 1179656 | tf_op jit(solution)/shard_map/sum_over_x/ppermute | solution.py:15
  19.8 21.3 %collective-permute-start.1 = (bf16[12,32,512]{2,1,0:T(8,128)(2,1)}, bf16[12,32,512]{2,1,0:T(8,128)(2,1)}, u32[]{:S(2)}, u32[]{:S(2)}) collective-permute-start(bf16[12,32,512]{2,1,0:T(8,128)(2,1)} %get-tuple-element.14), channel_id=1, source_target_pairs={{0,1},{1,2},{2,3},{3,0},{4,5},{5,6},{6,7},{7,4},{8,9},{9,10},{10,1... | collective-permute-start | bytes 1179656 | tf_op jit(solution)/shard_map/sum_over_x/ppermute | solution.py:15
  21.7 19.3 %collective-permute-start.2 = (bf16[12,32,512]{2,1,0:T(8,128)(2,1)}, bf16[12,32,512]{2,1,0:T(8,128)(2,1)}, u32[]{:S(2)}, u32[]{:S(2)}) collective-permute-start(bf16[12,32,512]{2,1,0:T(8,128)(2,1)} %get-tuple-element.13), channel_id=1, source_target_pairs={{0,3},{1,0},{2,1},{3,2},{4,7},{5,4},{6,5},{7,6},{8,11},{9,8},{10,9... | collective-permute-start | bytes 1179656 | tf_op jit(solution)/shard_map/sum_over_x/ppermute | solution.py:15
  32.9 21.4 %all-to-all-start = ((bf16[8,64,512]{2,1,0:T(8,128)(2,1)}), bf16[8,64,512]{2,1,0:T(8,128)(2,1)S(1)}, u32[]{:S(2)}, u32[]{:S(2)}) async-start(bf16[8,64,512]{2,1,0:T(8,128)(2,1)} %owner_roots.1), calls=%async_computation | async-start | bytes 1048576 | tf_op jit(solution)/shard_map/owner_roots/all_to_all | solution.py:136
  36.4 64.2 %copy-start.2 = (f32[1,32,512]{2,1,0:T(8,128)S(1)}, f32[1,32,512]{2,1,0:T(8,128)}, u32[]{:S(2)}) copy-start(f32[1,32,512]{2,1,0:T(8,128)} %lf_ref.1) | copy-start | bytes 196612
  36.4 64.2 %copy-start.3 = (f32[1,32,512]{2,1,0:T(8,128)S(1)}, f32[1,32,512]{2,1,0:T(8,128)}, u32[]{:S(2)}) copy-start(f32[1,32,512]{2,1,0:T(8,128)} %rf_ref.1) | copy-start | bytes 196612
  54.3 28.8 %all-to-all-start.1 = ((bf16[12,32,512]{2,1,0:T(8,128)(2,1)}), bf16[12,32,512]{2,1,0:T(8,128)(2,1)S(1)}, u32[]{:S(2)}, u32[]{:S(2)}) async-start(bf16[12,32,512]{2,1,0:T(8,128)(2,1)} %sum_over_x.1), calls=%async_computation.1 | async-start | bytes 786432 | tf_op jit(solution)/shard_map/sum_over_z/all_to_all | solution.py:140

commit v7 on v6

--- a/solution.py
+++ b/solution.py
@@ -41,44 +41,20 @@
     return pl.CostEstimate(flops=flops, bytes_accessed=size, transcendentals=0)
 
 
-def rows_to_send(where, left, right, other_left, other_right):
-    _, _, rows, width = left.shape
+def stacked(left, right):
+    count, rows, width = left.shape
 
-    def kernel(where_ref, left_ref, right_ref, other_left_ref, other_right_ref, out_ref):
-        core = where_ref[1]
-
-        @pl.when(where_ref[0] == 1)
-        def _():
-            out_ref[:, :rows] = left_ref[:, core]
-            out_ref[:, rows:] = right_ref[:, core]
-
-        @pl.when(where_ref[0] == 0)
-        def _():
-            out_ref[:, :rows] = other_left_ref[:, core]
-            out_ref[:, rows:] = other_right_ref[:, core]
+    def kernel(left_ref, right_ref, out_ref):
+        out_ref[:, :rows] = left_ref[...]
+        out_ref[:, rows:] = right_ref[...]
 
     return pl.pallas_call(
         kernel,
-        out_shape=pltpu.VMEM((Y, 2 * rows, width), BF),
-        in_specs=[SMEM] + [VMEM] * 4,
+        out_shape=jax.ShapeDtypeStruct((count, 2 * rows, width), BF),
+        in_specs=[VMEM] * 2,
         out_specs=VMEM,
         cost_estimate=cost(10**6, 1 << 20),
-    )(where, *(in_vmem(v) for v in (left, right, other_left, other_right)))
-
-
-def x_sum(own, came):
-    def kernel(own_ref, a_ref, b_ref, c_ref, out_ref):
-        for i in range(own_ref.shape[0]):
-            total = own_ref[i] + a_ref[i].astype(F32) + b_ref[i].astype(F32) + c_ref[i].astype(F32)
-            out_ref[i] = total.astype(BF)
-
-    return pl.pallas_call(
-        kernel,
-        out_shape=pltpu.VMEM(own.shape, BF),
-        in_specs=[VMEM] * 4,
-        out_specs=VMEM,
-        cost_estimate=cost(5 * 10**10, 2 << 20),
-    )(*(in_vmem(v) for v in (own, *came)))
+    )(in_vmem(left), in_vmem(right))
 
 
 def after_gather(me, whole, right_inverse, left_rows, exact, left_factor, right_factor):
@@ -116,25 +92,21 @@
 
 def on_device(gradients, owners, left_factor, right_factor, left_root, right_root):
     rows, width = gradients.shape[2:]
-    x, z, core = lax.axis_index("x"), lax.axis_index("z"), lax.axis_index("c")
-    me = lax.axis_index("y") * C + core
+    x, z = lax.axis_index("x"), lax.axis_index("z")
+    me = lax.axis_index("y") * C + lax.axis_index("c")
+
     mine = gradients.reshape(Z, X, rows, width)
-    owner = owners[z * X + x]
 
     def column(step):
         return pick(mine, lax.rem(x + step, X), 1)
 
     with jax.named_scope("sum_over_x"):
-        to_x = [column(step).astype(BF) for step in (2, 1, 3)]
-        came = [along_x(v, step) for v, step in zip(to_x, (2, 1, 3))]
-        over_x = x_sum(column(0), came)
+        came = [along_x(column(step).astype(BF), step) for step in (2, 1, 3)]
+        over_x = sum((v.astype(F32) for v in came), column(0))
     with jax.named_scope("owner_roots"):
-        pair = [root.reshape(Y, C, rows, width) for root in (left_root, right_root)]
-        others = [lax.ppermute(root.reshape(-1, width), "c", [(0, 1), (1, 0)]) for root in pair]
-        where = jnp.stack([(lax.rem(owner, C) == core).astype(jnp.int32), core])
-        slots = rows_to_send(where, *pair, *(v.reshape(pair[0].shape) for v in others))
-        roots = pick(lax.all_to_all(slots, "y", 0, 0, tiled=True), lax.div(owner, C), 0)
-        over_x, roots = lax.optimization_barrier((over_x, roots))
+        slots = stacked(left_root.reshape(Y * C, rows, width), right_root.reshape(Y * C, rows, width))
+        roots = pick(lax.all_to_all(slots, ROWS, 0, 0, tiled=True), owners[z * X + x], 0)
+        over_x, roots = lax.optimization_barrier((over_x.astype(BF), roots))
         right_inverse = lax.all_gather(roots[rows:], ROWS, axis=0, tiled=True)
     with jax.named_scope("sum_over_z"):
         exact = added(lax.all_to_all(over_x, "z", 0, 0, tiled=True))

time: 103 us -> 95.2 us (0.924)
  starting transfers between devices: 36.5 us -> 31.9 us
  Pallas kernels: 5.1 us -> 2.48 us
  waiting for transfers between devices: 15.7 us -> 13.7 us
  other arithmetic: 0.64 us -> 2.18 us
    ppermute x2 -> x0, starting transfers between devices: 14.5 us -> none  [on_device(): lax.ppermute(root.reshape(-1, width), 'c', [(0, 1), (1, 0)])]
    all_to_all x1, starting transfers between devices: 3.49 us -> 14 us  [on_device(): lax.all_to_all(slots, ROWS, 0, 0, tiled=True)]
    all_to_all x1, waiting for transfers between devices: 11 us -> 1.09 us  [on_device(): lax.all_to_all(slots, ROWS, 0, 0, tiled=True)]
    ppermute x3, waiting for transfers between devices: 4.64 us -> 11.9 us  [along_x(): return lax.ppermute(value, 'x', [(i, (i + step) % X) for i in range(X)])]
    pallas_call x2 -> x1, Pallas kernels: 3.68 us -> 1.05 us  [stacked(): pl.pallas_call(kernel, out_shape=jax.ShapeDtypeStruct((count, 2 * rows, w...]
    convert_element_type x0 -> x1, other arithmetic: none -> 2.12 us  [on_device(): over_x, roots = lax.optimization_barrier((over_x.astype(BF), roots))]
    unnamed x8 -> x10, local copies, waits for them, and re-layouts: 0.02 us -> 2.09 us
    all_gather x1, blocking collectives: 17.5 us -> 19.1 us  [on_device(): whole = lax.all_gather(my_rows, ROWS, axis=0, tiled=True)]
  transfers between devices with their start and end apart: 7 -> 5, of which waited for: 2 -> 4; matrix products, arithmetic and copies ran while one was open for 6% -> 5% of each run, Pallas kernels for 4% -> 0%
where the time goes in v7:
time: 95.2 us; the launch traced here: 94.6 us
  blocking collectives  37.2 us (39%)
  starting transfers between devices  31.9 us (34%)
  waiting for transfers between devices  13.7 us (14%)
  local copies, waits for them, and re-layouts  4.53 us (5%)
  between operations  2.7 us (3%)
  Pallas kernels  2.48 us (3%)
  other arithmetic  2.18 us (2%)
    all_gather x1, blocking collectives, on_device(): whole = lax.all_gather(my_rows, ROWS, axis=0, tiled=True)  19.1 us
    all_gather x1, blocking collectives, on_device(): right_inverse = lax.all_gather(roots[rows:], ROWS, axis=0, tiled=True)  18.1 us
    all_to_all x1, starting transfers between devices, on_device(): lax.all_to_all(slots, ROWS, 0, 0, tiled=True)  14 us
    ppermute x3, waiting for transfers between devices, along_x(): return lax.ppermute(value, 'x', [(i, (i + step) % X) for i in range(X)])  11.9 us
    all_to_all x1, starting transfers between devices, on_device(): exact = added(lax.all_to_all(over_x, 'z', 0, 0, tiled=True))  9.49 us
    ppermute x3, starting transfers between devices, along_x(): return lax.ppermute(value, 'x', [(i, (i + step) % X) for i in range(X)])  8.41 us
    convert_element_type x1, other arithmetic, on_device(): over_x, roots = lax.optimization_barrier((over_x.astype(BF), roots))  2.12 us
    unnamed x10, local copies, waits for them, and re-layouts  2.09 us
  transfers between devices with their start and end apart: 5, of which 4 were waited for; matrix products, arithmetic and copies ran while one was open for 5% of the time, Pallas kernels for 0%

profile of v7, /device:TPU:1, one launch (start us, length us, event | category | flops | bytes accessed | tf_op | source)
XLA Modules:
  0.0 94.6 jit_solution(5136487783484507054)
XLA Ops:
  0.6 0.0 copy-start
  0.6 1.0 %copy-done = bf16[1,1,512,512]{3,2,1,0:T(8,128)(2,1)S(1)} copy-done((bf16[1,1,512,512]{3,2,1,0:T(8,128)(2,1)S(1)}, bf16[1,1,512,512]{3,2,1,0:T(8,128)(2,1)}, u32[]{:S(2)}) %copy-start) | copy-done | bytes 524312
  1.7 1.0 %copy-done.1 = bf16[1,1,512,512]{3,2,1,0:T(8,128)(2,1)S(1)} copy-done((bf16[1,1,512,512]{3,2,1,0:T(8,128)(2,1)S(1)}, bf16[1,1,512,512]{3,2,1,0:T(8,128)(2,1)}, u32[]{:S(2)}) %copy-start.1) | copy-done | bytes 524312
  2.7 1.1 %owner_roots.1 = bf16[16,64,512]{2,1,0:T(8,128)(2,1)} custom-call(bf16[16,32,512]{2,1,0:T(8,128)(2,1)S(1)} %bitcast.36, bf16[16,32,512]{2,1,0:T(8,128)(2,1)S(1)} %bitcast.37), custom_call_target="tpu_custom_call" | custom-call | flops 1000000 | bytes 1048576 | tf_op jit(solution)/shard_map/owner_roots/pallas_call | solution.py:51
  3.8 14.0 %all-to-all-start = ((bf16[16,64,512]{2,1,0:T(8,128)(2,1)}), bf16[16,64,512]{2,1,0:T(8,128)(2,1)S(1)}, u32[]{:S(2)}, u32[]{:S(2)}) async-start(bf16[16,64,512]{2,1,0:T(8,128)(2,1)} %owner_roots.1), calls=%async_computation | async-start | bytes 2097152 | tf_op jit(solution)/shard_map/owner_roots/all_to_all | solution.py:108
  17.7 0.0 copy-start.3
  17.7 1.8 %fusion.3 = (bf16[12,32,512]{2,1,0:T(8,128)(2,1)S(1)}, bf16[12,32,512]{2,1,0:T(8,128)(2,1)S(1)}, bf16[12,32,512]{2,1,0:T(8,128)(2,1)S(1)}) fusion(f32[12,4,32,512]{3,2,1,0:T(8,128)} %bitcast.38, s32[]{:T(128)S(6)} %select_n.21, s32[]{:T(128)S(6)} %select_n.22, s32[]{:T(128)S(6)} %select_n.23), kind=kLoop, calls=%fused_computation.7 | loop fusion | bytes 2359308 | tf_op jit(solution)/shard_map/sum_over_x/convert_element_type | solution.py:104
  19.6 1.9 %collective-permute-start = (bf16[12,32,512]{2,1,0:T(8,128)(2,1)S(1)}, bf16[12,32,512]{2,1,0:T(8,128)(2,1)S(1)}, u32[]{:S(2)}, u32[]{:S(2)}) collective-permute-start(bf16[12,32,512]{2,1,0:T(8,128)(2,1)S(1)} %get-tuple-element.13), channel_id=1, source_target_pairs={{0,2},{1,3},{2,0},{3,1},{4,6},{5,7},{6,4},{7,5},{8,10},{9,11},{10,... | collective-permute-start | bytes 1179656 | tf_op jit(solution)/shard_map/sum_over_x/ppermute | solution.py:15
  21.5 1.9 %collective-permute-start.1 = (bf16[12,32,512]{2,1,0:T(8,128)(2,1)S(1)}, bf16[12,32,512]{2,1,0:T(8,128)(2,1)S(1)}, u32[]{:S(2)}, u32[]{:S(2)}) collective-permute-start(bf16[12,32,512]{2,1,0:T(8,128)(2,1)S(1)} %get-tuple-element.14), channel_id=1, source_target_pairs={{0,1},{1,2},{2,3},{3,0},{4,5},{5,6},{6,7},{7,4},{8,9},{9,10},{10,1... | collective-permute-start | bytes 1179656 | tf_op jit(solution)/shard_map/sum_over_x/ppermute | solution.py:15
  23.4 4.6 %collective-permute-start.2 = (bf16[12,32,512]{2,1,0:T(8,128)(2,1)S(1)}, bf16[12,32,512]{2,1,0:T(8,128)(2,1)S(1)}, u32[]{:S(2)}, u32[]{:S(2)}) collective-permute-start(bf16[12,32,512]{2,1,0:T(8,128)(2,1)S(1)} %get-tuple-element.15), channel_id=1, source_target_pairs={{0,3},{1,0},{2,1},{3,2},{4,7},{5,4},{6,5},{7,6},{8,11},{9,8},{10,9... | collective-permute-start | bytes 1179656 | tf_op jit(solution)/shard_map/sum_over_x/ppermute | solution.py:15
  28.0 0.0 copy-done.4
  28.1 0.6 dynamic_slice.24
  30.6 2.9 %collective-permute-done = bf16[12,32,512]{2,1,0:T(8,128)(2,1)S(1)} collective-permute-done((bf16[12,32,512]{2,1,0:T(8,128)(2,1)S(1)}, bf16[12,32,512]{2,1,0:T(8,128)(2,1)S(1)}, u32[]{:S(2)}, u32[]{:S(2)}) %collective-permute-start) | collective-permute-done | bytes 393248 | tf_op jit(solution)/shard_map/sum_over_x/ppermute | solution.py:15
  33.5 9.0 %collective-permute-done.1 = bf16[12,32,512]{2,1,0:T(8,128)(2,1)S(1)} collective-permute-done((bf16[12,32,512]{2,1,0:T(8,128)(2,1)S(1)}, bf16[12,32,512]{2,1,0:T(8,128)(2,1)S(1)}, u32[]{:S(2)}, u32[]{:S(2)}) %collective-permute-start.1) | collective-permute-done | bytes 393248 | tf_op jit(solution)/shard_map/sum_over_x/ppermute | solution.py:15
  42.5 0.0 collective-permute-done.2
  42.5 2.1 %fusion.2 = bf16[12,32,512]{2,1,0:T(8,128)(2,1)} fusion(bf16[12,32,512]{2,1,0:T(8,128)(2,1)S(1)} %collective-permute-done.2, bf16[12,32,512]{2,1,0:T(8,128)(2,1)S(1)} %collective-permute-done.1, bf16[12,32,512]{2,1,0:T(8,128)(2,1)S(1)} %collective-permute-done, f32[12,4,32,512]{3,2,1,0:T(8,128)} %bitcast.39, s32[]{:T(128)S(6)} %select_n.20), kind=kLoop, calls=%fused_computation.6 | loop fusion | flops 1376256 | bytes 2359300 | tf_op jit(solution)/shard_map/owner_roots/convert_element_type | solution.py:109
  44.6 1.1 %all-to-all-done = bf16[16,64,512]{2,1,0:T(8,128)(2,1)S(1)} async-done(((bf16[16,64,512]{2,1,0:T(8,128)(2,1)}), bf16[16,64,512]{2,1,0:T(8,128)(2,1)S(1)}, u32[]{:S(2)}, u32[]{:S(2)}) %all-to-all-start) | async-done | bytes 1048608 | tf_op jit(solution)/shard_map/owner_roots/all_to_all | solution.py:108
  45.7 9.5 %all-to-all-start.1 = ((bf16[12,32,512]{2,1,0:T(8,128)(2,1)}), bf16[12,32,512]{2,1,0:T(8,128)(2,1)S(1)}, u32[]{:S(2)}, u32[]{:S(2)}) async-start(bf16[12,32,512]{2,1,0:T(8,128)(2,1)} %fusion.2), calls=%async_computation.1 | async-start | bytes 786432 | tf_op jit(solution)/shard_map/sum_over_z/all_to_all | solution.py:112
  55.2 18.1 %all_gather.6.right_ref = bf16[512,512]{1,0:T(8,128)(2,1)S(1)} all-gather(bf16[32,512]{1,0:T(8,128)(2,1)S(1)} %get-tuple-element.17), channel_id=1, replica_groups=mesh['y'=8,'c'=2,'z'=12,'x'=4] {'y','c'}, dimensions={0}, use_global_device_ids=true | all-gather | bytes 557056 | tf_op jit(solution)/shard_map/owner_roots/all_gather | solution.py:110
  73.3 0.8 all-to-all-done.1
  74.1 0.1 fusion.6
  74.1 19.1 %all_gather.7.whole_ref = bf16[512,512]{1,0:T(8,128)(2,1)S(1)} all-gather(bf16[32,512]{1,0:T(8,128)(2,1)S(1)} %get-tuple-element.9), channel_id=1, replica_groups=mesh['y'=8,'c'=2,'z'=12,'x'=4] {'y','c'}, dimensions={0}, use_global_device_ids=true | all-gather | bytes 557056 | tf_op jit(solution)/shard_map/whole_block/all_gather | solution.py:116
  93.2 0.0 copy-done.2
  93.2 1.4 %direction_and_statistics.1 = (f32[1,32,512]{2,1,0:T(8,128)}, f32[1,32,512]{2,1,0:T(8,128)}, bf16[1,32,512]{2,1,0:T(8,128)(2,1)}) custom-call(s32[1]{0:T(128)} %bitcast.me_ref, bf16[512,512]{1,0:T(8,128)(2,1)S(1)} %all_gather.7.whole_ref, bf16[512,512]{1,0:T(8,128)(2,1)S(1)} %all_gather.6.right_ref, bf16[32,512]{1,0:T(8,128)(2,1)S(1)} %get-tuple-element.16.lrows_ref, ...), custom_call_target="tpu_custom_call" | custom-call | flops 100000000 | bytes 2097152 | tf_op jit(solution)/shard_map/direction_and_statistics/pallas_call | solution.py:83
  (6 shorter events, 0.0 us)
Async XLA Ops:
  0.6 1.0 %copy-start = (bf16[1,1,512,512]{3,2,1,0:T(8,128)(2,1)S(1)}, bf16[1,1,512,512]{3,2,1,0:T(8,128)(2,1)}, u32[]{:S(2)}) copy-start(bf16[1,1,512,512]{3,2,1,0:T(8,128)(2,1)} %param.10) | copy-start | bytes 1572868
  1.7 1.0 %copy-start.1 = (bf16[1,1,512,512]{3,2,1,0:T(8,128)(2,1)S(1)}, bf16[1,1,512,512]{3,2,1,0:T(8,128)(2,1)}, u32[]{:S(2)}) copy-start(bf16[1,1,512,512]{3,2,1,0:T(8,128)(2,1)} %param.11) | copy-start | bytes 1572868
  2.7 25.3 %copy-start.4 = (s32[48]{0:T(128)S(1)}, s32[48]{0:T(128)}, u32[]{:S(2)}) copy-start(s32[48]{0:T(128)} %param.7) | copy-start | bytes 580
  3.8 41.9 %all-to-all-start = ((bf16[16,64,512]{2,1,0:T(8,128)(2,1)}), bf16[16,64,512]{2,1,0:T(8,128)(2,1)S(1)}, u32[]{:S(2)}, u32[]{:S(2)}) async-start(bf16[16,64,512]{2,1,0:T(8,128)(2,1)} %owner_roots.1), calls=%async_computation | async-start | bytes 2097152 | tf_op jit(solution)/shard_map/owner_roots/all_to_all | solution.py:108
  17.7 75.5 %copy-start.2 = (f32[1,32,512]{2,1,0:T(8,128)S(1)}, f32[1,32,512]{2,1,0:T(8,128)}, u32[]{:S(2)}) copy-start(f32[1,32,512]{2,1,0:T(8,128)} %lf_ref.1) | copy-start | bytes 196612
  17.7 75.5 %copy-start.3 = (f32[1,32,512]{2,1,0:T(8,128)S(1)}, f32[1,32,512]{2,1,0:T(8,128)}, u32[]{:S(2)}) copy-start(f32[1,32,512]{2,1,0:T(8,128)} %rf_ref.1) | copy-start | bytes 196612
  19.6 13.9 %collective-permute-start = (bf16[12,32,512]{2,1,0:T(8,128)(2,1)S(1)}, bf16[12,32,512]{2,1,0:T(8,128)(2,1)S(1)}, u32[]{:S(2)}, u32[]{:S(2)}) collective-permute-start(bf16[12,32,512]{2,1,0:T(8,128)(2,1)S(1)} %get-tuple-element.13), channel_id=1, source_target_pairs={{0,2},{1,3},{2,0},{3,1},{4,6},{5,7},{6,4},{7,5},{8,10},{9,11},{10,... | collective-permute-start | bytes 1179656 | tf_op jit(solution)/shard_map/sum_over_x/ppermute | solution.py:15
  21.5 21.0 %collective-permute-start.1 = (bf16[12,32,512]{2,1,0:T(8,128)(2,1)S(1)}, bf16[12,32,512]{2,1,0:T(8,128)(2,1)S(1)}, u32[]{:S(2)}, u32[]{:S(2)}) collective-permute-start(bf16[12,32,512]{2,1,0:T(8,128)(2,1)S(1)} %get-tuple-element.14), channel_id=1, source_target_pairs={{0,1},{1,2},{2,3},{3,0},{4,5},{5,6},{6,7},{7,4},{8,9},{9,10},{10,1... | collective-permute-start | bytes 1179656 | tf_op jit(solution)/shard_map/sum_over_x/ppermute | solution.py:15
  23.4 19.0 %collective-permute-start.2 = (bf16[12,32,512]{2,1,0:T(8,128)(2,1)S(1)}, bf16[12,32,512]{2,1,0:T(8,128)(2,1)S(1)}, u32[]{:S(2)}, u32[]{:S(2)}) collective-permute-start(bf16[12,32,512]{2,1,0:T(8,128)(2,1)S(1)} %get-tuple-element.15), channel_id=1, source_target_pairs={{0,3},{1,0},{2,1},{3,2},{4,7},{5,4},{6,5},{7,6},{8,11},{9,8},{10,9... | collective-permute-start | bytes 1179656 | tf_op jit(solution)/shard_map/sum_over_x/ppermute | solution.py:15
  45.7 28.3 %all-to-all-start.1 = ((bf16[12,32,512]{2,1,0:T(8,128)(2,1)}), bf16[12,32,512]{2,1,0:T(8,128)(2,1)S(1)}, u32[]{:S(2)}, u32[]{:S(2)}) async-start(bf16[12,32,512]{2,1,0:T(8,128)(2,1)} %fusion.2), calls=%async_computation.1 | async-start | bytes 786432 | tf_op jit(solution)/shard_map/sum_over_z/all_to_all | solution.py:112

commit v8 on v7

--- a/solution.py
+++ b/solution.py
@@ -43,18 +43,35 @@
 
 def stacked(left, right):
     count, rows, width = left.shape
+    shape = (count, 2 * rows, width)
+    parts = 2
 
-    def kernel(left_ref, right_ref, out_ref):
-        out_ref[:, :rows] = left_ref[...]
-        out_ref[:, rows:] = right_ref[...]
+    def kernel(left_ref, right_ref, out_ref, held, arrived, sent):
+        coming, going = [], []
+        for i in range(parts):
+            part = pl.ds(i * (count // parts), count // parts)
+            for j, ref in enumerate((left_ref, right_ref)):
+                to = held.at[part, pl.ds(j * rows, rows)]
+                coming.append(pltpu.make_async_copy(ref.at[part], to, arrived.at[2 * i + j]))
+            going.append(pltpu.make_async_copy(held.at[part], out_ref.at[part], sent.at[i]))
+        for copy in coming:
+            copy.start()
+        for i in range(parts):
+            coming[2 * i].wait()
+            coming[2 * i + 1].wait()
+            going[i].start()
+        for copy in going:
+            copy.wait()
 
+    hbm = pl.BlockSpec(memory_space=pltpu.HBM)
     return pl.pallas_call(
         kernel,
-        out_shape=jax.ShapeDtypeStruct((count, 2 * rows, width), BF),
-        in_specs=[VMEM] * 2,
-        out_specs=VMEM,
+        out_shape=jax.ShapeDtypeStruct(shape, BF),
+        in_specs=[hbm] * 2,
+        out_specs=hbm,
+        scratch_shapes=[pltpu.VMEM(shape, BF), pltpu.SemaphoreType.DMA((2 * parts,)), pltpu.SemaphoreType.DMA((parts,))],
         cost_estimate=cost(10**6, 1 << 20),
-    )(in_vmem(left), in_vmem(right))
+    )(left, right)
 
 
 def after_gather(me, whole, right_inverse, left_rows, exact, left_factor, right_factor):
@@ -102,7 +119,7 @@
 
     with jax.named_scope("sum_over_x"):
         came = [along_x(column(step).astype(BF), step) for step in (2, 1, 3)]
-        over_x = sum((v.astype(F32) for v in came), column(0))
+        over_x = sum((v.astype(F32) for v in came), lax.optimization_barrier(column(0)))
     with jax.named_scope("owner_roots"):
         slots = stacked(left_root.reshape(Y * C, rows, width), right_root.reshape(Y * C, rows, width))
         roots = pick(lax.all_to_all(slots, ROWS, 0, 0, tiled=True), owners[z * X + x], 0)

time: 95.2 us -> 94.9 us (level)
  waiting for transfers between devices: 13.7 us -> 11.2 us
  blocking collectives: 37.2 us -> 38.7 us
  Pallas kernels: 2.48 us -> 3.48 us
    unnamed x10 -> x6, local copies, waits for them, and re-layouts: 2.09 us -> 0.02 us
    squeeze x1 -> x2, local copies, waits for them, and re-layouts: 0.01 us -> 1.25 us  [pick(): return lax.dynamic_index_in_dim(array, index, axis, keepdims=False)]
    ppermute x3, waiting for transfers between devices: 11.9 us -> 10.8 us  [along_x(): return lax.ppermute(value, 'x', [(i, (i + step) % X) for i in range(X)])]
    pallas_call x1, Pallas kernels: 1.05 us -> 2.05 us  [stacked(): pl.pallas_call(kernel, out_shape=jax.ShapeDtypeStruct(shape, BF), in_spec...]
  transfers between devices with their start and end apart: 5 -> 5, of which waited for: 4 -> 3; matrix products, arithmetic and copies ran while one was open for 5% -> 7% of each run, Pallas kernels for 0% -> 0%
where the time goes in v8:
time: 94.9 us; the launch traced here: 94.3 us
  blocking collectives  38.7 us (41%)
  starting transfers between devices  31.9 us (34%)
  waiting for transfers between devices  11.2 us (12%)
  local copies, waits for them, and re-layouts  4.43 us (5%)
  Pallas kernels  3.48 us (4%)
  between operations  2.71 us (3%)
  other arithmetic  2.04 us (2%)
    all_gather x1, blocking collectives, on_device(): whole = lax.all_gather(my_rows, ROWS, axis=0, tiled=True)  19.7 us
    all_gather x1, blocking collectives, on_device(): right_inverse = lax.all_gather(roots[rows:], ROWS, axis=0, tiled=True)  18.9 us
    all_to_all x1, starting transfers between devices, on_device(): lax.all_to_all(slots, ROWS, 0, 0, tiled=True)  14 us
    ppermute x3, waiting for transfers between devices, along_x(): return lax.ppermute(value, 'x', [(i, (i + step) % X) for i in range(X)])  10.8 us
    all_to_all x1, starting transfers between devices, on_device(): exact = added(lax.all_to_all(over_x, 'z', 0, 0, tiled=True))  9.49 us
    ppermute x3, starting transfers between devices, along_x(): return lax.ppermute(value, 'x', [(i, (i + step) % X) for i in range(X)])  8.4 us
    convert_element_type x1, local copies, waits for them, and re-layouts, on_device(): came = [along_x(column(step).astype(BF), step) for step in (2, 1, 3)]  2.56 us
    pallas_call x1, Pallas kernels, stacked(): pl.pallas_call(kernel, out_shape=jax.ShapeDtypeStruct(shape, BF), in_spec...  2.05 us
  transfers between devices with their start and end apart: 5, of which 3 were waited for; matrix products, arithmetic and copies ran while one was open for 7% of the time, Pallas kernels for 0%

profile of v8, /device:TPU:1, one launch (start us, length us, event | category | flops | bytes accessed | tf_op | source)
XLA Modules:
  0.0 94.3 jit_solution(17867950511797737765)
XLA Ops:
  0.6 2.1 %owner_roots.1 = bf16[16,64,512]{2,1,0:T(8,128)(2,1)} custom-call(bf16[16,32,512]{2,1,0:T(8,128)(2,1)} %bitcast.32, bf16[16,32,512]{2,1,0:T(8,128)(2,1)} %bitcast.33), custom_call_target="tpu_custom_call" | custom-call | flops 1000000 | bytes 1048576 | tf_op jit(solution)/shard_map/owner_roots/pallas_call | solution.py:67
  2.7 0.0 copy-start.2
  2.7 14.0 %all-to-all-start = ((bf16[16,64,512]{2,1,0:T(8,128)(2,1)}), bf16[16,64,512]{2,1,0:T(8,128)(2,1)S(1)}, u32[]{:S(2)}, u32[]{:S(2)}) async-start(bf16[16,64,512]{2,1,0:T(8,128)(2,1)} %owner_roots.1), calls=%async_computation | async-start | bytes 2097152 | tf_op jit(solution)/shard_map/owner_roots/all_to_all | solution.py:125
  16.7 2.6 %fusion = (bf16[12,32,512]{2,1,0:T(8,128)(2,1)}, bf16[12,32,512]{2,1,0:T(8,128)(2,1)S(1)}, bf16[12,32,512]{2,1,0:T(8,128)(2,1)S(1)}) fusion(f32[12,4,32,512]{3,2,1,0:T(8,128)} %bitcast.30, s32[]{:T(128)S(6)} %select_n.21, s32[]{:T(128)S(6)} %select_n.22, s32[]{:T(128)S(6)} %select_n.23), kind=kLoop, calls=%fused_computation.5 | loop fusion | bytes 2359308 | tf_op jit(solution)/shard_map/sum_over_x/convert_element_type | solution.py:121
  19.2 1.9 %collective-permute-start = (bf16[12,32,512]{2,1,0:T(8,128)(2,1)}, bf16[12,32,512]{2,1,0:T(8,128)(2,1)S(1)}, u32[]{:S(2)}, u32[]{:S(2)}) collective-permute-start(bf16[12,32,512]{2,1,0:T(8,128)(2,1)} %get-tuple-element.13), channel_id=1, source_target_pairs={{0,2},{1,3},{2,0},{3,1},{4,6},{5,7},{6,4},{7,5},{8,10},{9,11},{10,... | collective-permute-start | bytes 1179656 | tf_op jit(solution)/shard_map/sum_over_x/ppermute | solution.py:15
  21.2 1.9 %collective-permute-start.1 = (bf16[12,32,512]{2,1,0:T(8,128)(2,1)S(1)}, bf16[12,32,512]{2,1,0:T(8,128)(2,1)S(1)}, u32[]{:S(2)}, u32[]{:S(2)}) collective-permute-start(bf16[12,32,512]{2,1,0:T(8,128)(2,1)S(1)} %get-tuple-element.14), channel_id=1, source_target_pairs={{0,1},{1,2},{2,3},{3,0},{4,5},{5,6},{6,7},{7,4},{8,9},{9,10},{10,1... | collective-permute-start | bytes 1179656 | tf_op jit(solution)/shard_map/sum_over_x/ppermute | solution.py:15
  23.1 4.6 %collective-permute-start.2 = (bf16[12,32,512]{2,1,0:T(8,128)(2,1)S(1)}, bf16[12,32,512]{2,1,0:T(8,128)(2,1)}, u32[]{:S(2)}, u32[]{:S(2)}) collective-permute-start(bf16[12,32,512]{2,1,0:T(8,128)(2,1)S(1)} %get-tuple-element.15), channel_id=1, source_target_pairs={{0,3},{1,0},{2,1},{3,2},{4,7},{5,4},{6,5},{7,6},{8,11},{9,8},{10,9... | collective-permute-start | bytes 1179656 | tf_op jit(solution)/shard_map/sum_over_x/ppermute | solution.py:15
  27.7 0.0 copy-start
  27.7 0.0 copy-start.1
  27.7 1.2 %dynamic-slice_bitcast_fusion = f32[12,32,512]{2,1,0:T(8,128)S(1)} fusion(f32[12,4,32,512]{3,2,1,0:T(8,128)} %bitcast.31, s32[]{:T(128)S(6)} %select_n.20), kind=kLoop, calls=%fused_computation.4 | loop fusion | bytes 1572868 | tf_op jit(solution)/shard_map/sum_over_x/jit(dynamic_index_in_dim)/squeeze | solution.py:23
  29.0 0.0 copy-done.2
  29.0 0.6 dynamic_slice.24
  31.5 1.8 %collective-permute-done = bf16[12,32,512]{2,1,0:T(8,128)(2,1)S(1)} collective-permute-done((bf16[12,32,512]{2,1,0:T(8,128)(2,1)}, bf16[12,32,512]{2,1,0:T(8,128)(2,1)S(1)}, u32[]{:S(2)}, u32[]{:S(2)}) %collective-permute-start) | collective-permute-done | bytes 393248 | tf_op jit(solution)/shard_map/sum_over_x/ppermute | solution.py:15
  33.3 9.0 %collective-permute-done.1 = bf16[12,32,512]{2,1,0:T(8,128)(2,1)S(1)} collective-permute-done((bf16[12,32,512]{2,1,0:T(8,128)(2,1)S(1)}, bf16[12,32,512]{2,1,0:T(8,128)(2,1)S(1)}, u32[]{:S(2)}, u32[]{:S(2)}) %collective-permute-start.1) | collective-permute-done | bytes 393248 | tf_op jit(solution)/shard_map/sum_over_x/ppermute | solution.py:15
  42.3 0.0 collective-permute-done.2
  42.3 2.0 %add_convert_fusion = bf16[12,32,512]{2,1,0:T(8,128)(2,1)} fusion(bf16[12,32,512]{2,1,0:T(8,128)(2,1)} %collective-permute-done.2, bf16[12,32,512]{2,1,0:T(8,128)(2,1)S(1)} %collective-permute-done.1, f32[12,32,512]{2,1,0:T(8,128)S(1)} %dynamic-slice_bitcast_fusion, bf16[12,32,512]{2,1,0:T(8,128)(2,1)S(1)} %collective-permute-done), kind=kLoop, calls=%fused_computation.3 | loop fusion | flops 1376256 | bytes 2359296 | tf_op jit(solution)/shard_map/owner_roots/convert_element_type | solution.py:126
  44.3 0.3 all-to-all-done
  44.7 9.5 %all-to-all-start.1 = ((bf16[12,32,512]{2,1,0:T(8,128)(2,1)}), bf16[12,32,512]{2,1,0:T(8,128)(2,1)S(1)}, u32[]{:S(2)}, u32[]{:S(2)}) async-start(bf16[12,32,512]{2,1,0:T(8,128)(2,1)} %add_convert_fusion), calls=%async_computation.1 | async-start | bytes 786432 | tf_op jit(solution)/shard_map/sum_over_z/all_to_all | solution.py:129
  54.2 18.9 %all_gather.6.right_ref = bf16[512,512]{1,0:T(8,128)(2,1)S(1)} all-gather(bf16[32,512]{1,0:T(8,128)(2,1)S(1)} %get-tuple-element.17), channel_id=1, replica_groups=mesh['y'=8,'c'=2,'z'=12,'x'=4] {'y','c'}, dimensions={0}, use_global_device_ids=true | all-gather | bytes 557056 | tf_op jit(solution)/shard_map/owner_roots/all_gather | solution.py:127
  73.1 0.0 all-to-all-done.1
  73.1 0.1 fusion.3
  73.2 19.7 %all_gather.7.whole_ref = bf16[512,512]{1,0:T(8,128)(2,1)S(1)} all-gather(bf16[32,512]{1,0:T(8,128)(2,1)S(1)} %get-tuple-element.9), channel_id=1, replica_groups=mesh['y'=8,'c'=2,'z'=12,'x'=4] {'y','c'}, dimensions={0}, use_global_device_ids=true | all-gather | bytes 557056 | tf_op jit(solution)/shard_map/whole_block/all_gather | solution.py:133
  92.9 0.0 copy-done
  92.9 1.4 %direction_and_statistics.1 = (f32[1,32,512]{2,1,0:T(8,128)}, f32[1,32,512]{2,1,0:T(8,128)}, bf16[1,32,512]{2,1,0:T(8,128)(2,1)}) custom-call(s32[1]{0:T(128)} %bitcast.me_ref, bf16[512,512]{1,0:T(8,128)(2,1)S(1)} %all_gather.7.whole_ref, bf16[512,512]{1,0:T(8,128)(2,1)S(1)} %all_gather.6.right_ref, bf16[32,512]{1,0:T(8,128)(2,1)S(1)} %get-tuple-element.16.lrows_ref, ...), custom_call_target="tpu_custom_call" | custom-call | flops 100000000 | bytes 2097152 | tf_op jit(solution)/shard_map/direction_and_statistics/pallas_call | solution.py:100
  (3 shorter events, 0.0 us)
Async XLA Ops:
  2.7 26.3 %copy-start.2 = (s32[48]{0:T(128)S(1)}, s32[48]{0:T(128)}, u32[]{:S(2)}) copy-start(s32[48]{0:T(128)} %param.7) | copy-start | bytes 580
  2.7 41.9 %all-to-all-start = ((bf16[16,64,512]{2,1,0:T(8,128)(2,1)}), bf16[16,64,512]{2,1,0:T(8,128)(2,1)S(1)}, u32[]{:S(2)}, u32[]{:S(2)}) async-start(bf16[16,64,512]{2,1,0:T(8,128)(2,1)} %owner_roots.1), calls=%async_computation | async-start | bytes 2097152 | tf_op jit(solution)/shard_map/owner_roots/all_to_all | solution.py:125
  19.2 14.1 %collective-permute-start = (bf16[12,32,512]{2,1,0:T(8,128)(2,1)}, bf16[12,32,512]{2,1,0:T(8,128)(2,1)S(1)}, u32[]{:S(2)}, u32[]{:S(2)}) collective-permute-start(bf16[12,32,512]{2,1,0:T(8,128)(2,1)} %get-tuple-element.13), channel_id=1, source_target_pairs={{0,2},{1,3},{2,0},{3,1},{4,6},{5,7},{6,4},{7,5},{8,10},{9,11},{10,... | collective-permute-start | bytes 1179656 | tf_op jit(solution)/shard_map/sum_over_x/ppermute | solution.py:15
  21.2 21.2 %collective-permute-start.1 = (bf16[12,32,512]{2,1,0:T(8,128)(2,1)S(1)}, bf16[12,32,512]{2,1,0:T(8,128)(2,1)S(1)}, u32[]{:S(2)}, u32[]{:S(2)}) collective-permute-start(bf16[12,32,512]{2,1,0:T(8,128)(2,1)S(1)} %get-tuple-element.14), channel_id=1, source_target_pairs={{0,1},{1,2},{2,3},{3,0},{4,5},{5,6},{6,7},{7,4},{8,9},{9,10},{10,1... | collective-permute-start | bytes 1179656 | tf_op jit(solution)/shard_map/sum_over_x/ppermute | solution.py:15
  23.1 19.3 %collective-permute-start.2 = (bf16[12,32,512]{2,1,0:T(8,128)(2,1)S(1)}, bf16[12,32,512]{2,1,0:T(8,128)(2,1)}, u32[]{:S(2)}, u32[]{:S(2)}) collective-permute-start(bf16[12,32,512]{2,1,0:T(8,128)(2,1)S(1)} %get-tuple-element.15), channel_id=1, source_target_pairs={{0,3},{1,0},{2,1},{3,2},{4,7},{5,4},{6,5},{7,6},{8,11},{9,8},{10,9... | collective-permute-start | bytes 1179656 | tf_op jit(solution)/shard_map/sum_over_x/ppermute | solution.py:15
  27.7 65.2 %copy-start = (f32[1,32,512]{2,1,0:T(8,128)S(1)}, f32[1,32,512]{2,1,0:T(8,128)}, u32[]{:S(2)}) copy-start(f32[1,32,512]{2,1,0:T(8,128)} %lf_ref.1) | copy-start | bytes 196612
  27.7 65.2 %copy-start.1 = (f32[1,32,512]{2,1,0:T(8,128)S(1)}, f32[1,32,512]{2,1,0:T(8,128)}, u32[]{:S(2)}) copy-start(f32[1,32,512]{2,1,0:T(8,128)} %rf_ref.1) | copy-start | bytes 196612
  44.7 28.5 %all-to-all-start.1 = ((bf16[12,32,512]{2,1,0:T(8,128)(2,1)}), bf16[12,32,512]{2,1,0:T(8,128)(2,1)S(1)}, u32[]{:S(2)}, u32[]{:S(2)}) async-start(bf16[12,32,512]{2,1,0:T(8,128)(2,1)} %add_convert_fusion), calls=%async_computation.1 | async-start | bytes 786432 | tf_op jit(solution)/shard_map/sum_over_z/all_to_all | solution.py:129

commit v9 on v8

--- a/solution.py
+++ b/solution.py
@@ -41,22 +41,21 @@
     return pl.CostEstimate(flops=flops, bytes_accessed=size, transcendentals=0)
 
 
-def stacked(left, right):
-    count, rows, width = left.shape
-    shape = (count, 2 * rows, width)
-    parts = 2
+def rows_by_core(core, left, right):
+    chips, _, rows, width = left.shape
+    shape = (chips, 2 * rows, width)
 
-    def kernel(left_ref, right_ref, out_ref, held, arrived, sent):
+    def kernel(core_ref, left_ref, right_ref, mine_ref, other_ref, held, arrived, sent):
+        core = core_ref[0]
         coming, going = [], []
-        for i in range(parts):
-            part = pl.ds(i * (count // parts), count // parts)
+        for i, (which, out) in enumerate(((1 - core, other_ref), (core, mine_ref))):
             for j, ref in enumerate((left_ref, right_ref)):
-                to = held.at[part, pl.ds(j * rows, rows)]
-                coming.append(pltpu.make_async_copy(ref.at[part], to, arrived.at[2 * i + j]))
-            going.append(pltpu.make_async_copy(held.at[part], out_ref.at[part], sent.at[i]))
+                to = held.at[i, :, pl.ds(j * rows, rows)]
+                coming.append(pltpu.make_async_copy(ref.at[:, which], to, arrived.at[2 * i + j]))
+            going.append(pltpu.make_async_copy(held.at[i], out, sent.at[i]))
         for copy in coming:
             copy.start()
-        for i in range(parts):
+        for i in range(2):
             coming[2 * i].wait()
             coming[2 * i + 1].wait()
             going[i].start()
@@ -66,12 +65,47 @@
     hbm = pl.BlockSpec(memory_space=pltpu.HBM)
     return pl.pallas_call(
         kernel,
-        out_shape=jax.ShapeDtypeStruct(shape, BF),
-        in_specs=[hbm] * 2,
-        out_specs=hbm,
-        scratch_shapes=[pltpu.VMEM(shape, BF), pltpu.SemaphoreType.DMA((2 * parts,)), pltpu.SemaphoreType.DMA((parts,))],
+        out_shape=(jax.ShapeDtypeStruct(shape, BF),) * 2,
+        in_specs=[SMEM, hbm, hbm],
+        out_specs=(hbm, hbm),
+        scratch_shapes=[pltpu.VMEM((2, *shape), BF), pltpu.SemaphoreType.DMA((4,)), pltpu.SemaphoreType.DMA((2,))],
         cost_estimate=cost(10**6, 1 << 20),
-    )(left, right)
+    )(core, left, right)
+
+
+def of_owner(owners, block, core, mine, other):
+    def kernel(owners_ref, block_ref, core_ref, mine_ref, other_ref, out_ref):
+        here = lax.rem(owners_ref[block_ref[0]], C) == core_ref[0]
+
+        @pl.when(here)
+        def _():
+            out_ref[...] = mine_ref[...]
+
+        @pl.when(jnp.logical_not(here))
+        def _():
+            out_ref[...] = other_ref[...]
+
+    return pl.pallas_call(
+        kernel,
+        out_shape=jax.ShapeDtypeStruct(mine.shape, BF),
+        in_specs=[SMEM] * 3 + [VMEM] * 2,
+        out_specs=VMEM,
+        cost_estimate=cost(10**6, 1 << 20),
+    )(owners, block, core, in_vmem(mine), in_vmem(other))
+
+
+def first_sum(own, came):
+    def kernel(own_ref, came_ref, out_ref):
+        for i in range(own_ref.shape[0]):
+            out_ref[i] = own_ref[i] + came_ref[i].astype(F32)
+
+    return pl.pallas_call(
+        kernel,
+        out_shape=jax.ShapeDtypeStruct(own.shape, F32),
+        in_specs=[VMEM] * 2,
+        out_specs=VMEM,
+        cost_estimate=cost(10**11, 2 << 20),
+    )(in_vmem(own), in_vmem(came))
 
 
 def after_gather(me, whole, right_inverse, left_rows, exact, left_factor, right_factor):
@@ -114,15 +148,22 @@
 
     mine = gradients.reshape(Z, X, rows, width)
 
-    def column(step):
-        return pick(mine, lax.rem(x + step, X), 1)
+    def column(step, source=mine):
+        return pick(source, lax.rem(x + step, X), 1)
 
+    with jax.named_scope("owner_roots"):
+        core, block = lax.axis_index("c")[None], z * X + x
+        pair = [root.reshape(Y, C, rows, width) for root in (left_root, right_root)]
+        keep, give = rows_by_core(core, *pair)
+        given = lax.ppermute(give, "c", [(0, 1), (1, 0)])
+        given, after_swap, owners_too = lax.optimization_barrier((given, mine, owners))
+        slots = of_owner(owners, block[None], core, keep, given)
+        spread = lax.all_to_all(slots, "y", 0, 0, tiled=True)
     with jax.named_scope("sum_over_x"):
-        came = [along_x(column(step).astype(BF), step) for step in (2, 1, 3)]
-        over_x = sum((v.astype(F32) for v in came), lax.optimization_barrier(column(0)))
-    with jax.named_scope("owner_roots"):
-        slots = stacked(left_root.reshape(Y * C, rows, width), right_root.reshape(Y * C, rows, width))
-        roots = pick(lax.all_to_all(slots, ROWS, 0, 0, tiled=True), owners[z * X + x], 0)
+        across = along_x(column(2).astype(BF), 2)
+        beside = [along_x(column(step, after_swap).astype(BF), step) for step in (1, 3)]
+        over_x = first_sum(column(0, after_swap), across) + beside[0].astype(F32) + beside[1].astype(F32)
+        roots = pick(spread, lax.div(owners_too[block], C), 0)
         over_x, roots = lax.optimization_barrier((over_x.astype(BF), roots))
         right_inverse = lax.all_gather(roots[rows:], ROWS, axis=0, tiled=True)
     with jax.named_scope("sum_over_z"):

time: 94.9 us -> 95.4 us (level)
  waiting for transfers between devices: 11.2 us -> 4.25 us
  starting transfers between devices: 31.9 us -> 35 us
  Pallas kernels: 3.48 us -> 5.98 us
  local copies, waits for them, and re-layouts: 4.43 us -> 5.55 us
    ppermute x0 -> x1, starting transfers between devices: none -> 12.4 us  [on_device(): given = lax.ppermute(give, 'c', [(0, 1), (1, 0)])]
    all_to_all x1, starting transfers between devices: 14 us -> 3.49 us  [on_device(): spread = lax.all_to_all(slots, 'y', 0, 0, tiled=True)]
    ppermute x3, waiting for transfers between devices: 10.8 us -> 4.24 us  [along_x(): return lax.ppermute(value, 'x', [(i, (i + step) % X) for i in range(X)])]
    pallas_call x1 -> x3, Pallas kernels: 2.05 us -> 4.56 us  [the longest x1 2.06 us: rows_by_core(): pl.pallas_call(kernel, out_shape=(jax.ShapeDtypeStruct(shape, BF),) * 2,...]
    all_gather x1, blocking collectives: 18.9 us -> 20.2 us  [on_device(): right_inverse = lax.all_gather(roots[rows:], ROWS, axis=0, tiled=True)]
    all_gather x1, blocking collectives: 19.7 us -> 18.5 us  [on_device(): whole = lax.all_gather(my_rows, ROWS, axis=0, tiled=True)]
    all_to_all x1, starting transfers between devices: 9.49 us -> 10.7 us  [on_device(): exact = added(lax.all_to_all(over_x, 'z', 0, 0, tiled=True))]
    unnamed x6 -> x8, local copies, waits for them, and re-layouts: 0.02 us -> 1.05 us
  transfers between devices with their start and end apart: 5 -> 6, of which waited for: 3 -> 2; matrix products, arithmetic and copies ran while one was open for 7% -> 7% of each run, Pallas kernels for 0% -> 3%
where the time goes in v9:
time: 95.4 us; the launch traced here: 94.5 us
  blocking collectives  38.7 us (41%)
  starting transfers between devices  35 us (37%)
  Pallas kernels  5.98 us (6%)
  local copies, waits for them, and re-layouts  5.55 us (6%)
  waiting for transfers between devices  4.25 us (4%)
  between operations  2.77 us (3%)
  other arithmetic  2.22 us (2%)
    all_gather x1, blocking collectives, on_device(): right_inverse = lax.all_gather(roots[rows:], ROWS, axis=0, tiled=True)  20.2 us
    all_gather x1, blocking collectives, on_device(): whole = lax.all_gather(my_rows, ROWS, axis=0, tiled=True)  18.5 us
    ppermute x1, starting transfers between devices, on_device(): given = lax.ppermute(give, 'c', [(0, 1), (1, 0)])  12.4 us
    all_to_all x1, starting transfers between devices, on_device(): exact = added(lax.all_to_all(over_x, 'z', 0, 0, tiled=True))  10.7 us
    ppermute x3, starting transfers between devices, along_x(): return lax.ppermute(value, 'x', [(i, (i + step) % X) for i in range(X)])  8.41 us
    ppermute x3, waiting for transfers between devices, along_x(): return lax.ppermute(value, 'x', [(i, (i + step) % X) for i in range(X)])  4.24 us
    all_to_all x1, starting transfers between devices, on_device(): spread = lax.all_to_all(slots, 'y', 0, 0, tiled=True)  3.49 us
    convert_element_type x1, other arithmetic, on_device(): over_x, roots = lax.optimization_barrier((over_x.astype(BF), roots))  2.16 us
  transfers between devices with their start and end apart: 6, of which 2 were waited for; matrix products, arithmetic and copies ran while one was open for 7% of the time, Pallas kernels for 3%

profile of v9, /device:TPU:1, one launch (start us, length us, event | category | flops | bytes accessed | tf_op | source)
XLA Modules:
  0.0 94.5 jit_solution(267953052013826858)
XLA Ops:
  0.6 2.1 %owner_roots.2 = (bf16[8,64,512]{2,1,0:T(8,128)(2,1)}, bf16[8,64,512]{2,1,0:T(8,128)(2,1)}) custom-call(s32[1]{0:T(128)} %bitcast.1.core_ref, bf16[8,2,32,512]{3,2,1,0:T(8,128)(2,1)} %bitcast.27, bf16[8,2,32,512]{3,2,1,0:T(8,128)(2,1)} %bitcast.28), custom_call_target="tpu_custom_call" | custom-call | flops 1000000 | bytes 1048576 | tf_op jit(solution)/shard_map/owner_roots/pallas_call | solution.py:66
  2.7 12.4 %collective-permute-start = (bf16[8,64,512]{2,1,0:T(8,128)(2,1)}, bf16[8,64,512]{2,1,0:T(8,128)(2,1)S(1)}, u32[]{:S(2)}, u32[]{:S(2)}) collective-permute-start(bf16[8,64,512]{2,1,0:T(8,128)(2,1)} %get-tuple-element.12), channel_id=1, source_target_pairs={{0,48},{48,0},{1,49},{49,1},{2,50},{50,2},{3,51},{51,3},{4,52},{52... | collective-permute-start | bytes 1572872 | tf_op jit(solution)/shard_map/owner_roots/ppermute | solution.py:158
  15.1 1.2 %fusion.2 = bf16[12,32,512]{2,1,0:T(8,128)(2,1)S(1)} fusion(f32[12,4,32,512]{3,2,1,0:T(8,128)} %bitcast.24, s32[]{:T(128)S(6)} %select_n.21), kind=kLoop, calls=%fused_computation.7 | loop fusion | bytes 786436 | tf_op jit(solution)/shard_map/sum_over_x/convert_element_type | solution.py:163
  16.3 1.9 %collective-permute-start.1 = (bf16[12,32,512]{2,1,0:T(8,128)(2,1)S(1)}, bf16[12,32,512]{2,1,0:T(8,128)(2,1)S(1)}, u32[]{:S(2)}, u32[]{:S(2)}) collective-permute-start(bf16[12,32,512]{2,1,0:T(8,128)(2,1)S(1)} %fusion.2), channel_id=1, source_target_pairs={{0,2},{1,3},{2,0},{3,1},{4,6},{5,7},{6,4},{7,5},{8,10},{9,11},{10,... | collective-permute-start | bytes 1179656 | tf_op jit(solution)/shard_map/sum_over_x/ppermute | solution.py:15
  18.3 0.0 collective-permute-done.other_ref
  18.3 1.0 %copy-done = bf16[8,64,512]{2,1,0:T(8,128)(2,1)S(1)} copy-done((bf16[8,64,512]{2,1,0:T(8,128)(2,1)S(1)}, bf16[8,64,512]{2,1,0:T(8,128)(2,1)}, u32[]{:S(2)}) %copy-start) | copy-done | bytes 524312
  19.4 1.5 %owner_roots.3 = bf16[8,64,512]{2,1,0:T(8,128)(2,1)} custom-call(s32[48]{0:T(128)} %owners_ref.1, s32[1]{0:T(128)} %bitcast.9.block_ref, s32[1]{0:T(128)} %bitcast.1.core_ref, bf16[8,64,512]{2,1,0:T(8,128)(2,1)S(1)} %copy-done, bf16[8,64,512]{2,1,0:T(8,128)(2,1)S(1)} %collective-permute-done.other_ref), custom_call_target="tpu_custom_call" | custom-call | flops 1000000 | bytes 1048576 | tf_op jit(solution)/shard_map/owner_roots/pallas_call | solution.py:88
  20.9 3.5 %all-to-all-start = ((bf16[8,64,512]{2,1,0:T(8,128)(2,1)}), bf16[8,64,512]{2,1,0:T(8,128)(2,1)S(1)}, u32[]{:S(2)}, u32[]{:S(2)}) async-start(bf16[8,64,512]{2,1,0:T(8,128)(2,1)} %owner_roots.3), calls=%async_computation | async-start | bytes 1048576 | tf_op jit(solution)/shard_map/owner_roots/all_to_all | solution.py:161
  24.4 1.5 %fusion = (bf16[12,32,512]{2,1,0:T(8,128)(2,1)S(1)}, bf16[12,32,512]{2,1,0:T(8,128)(2,1)S(1)}) fusion(s32[]{:T(128)S(6)} %select_n.22, s32[]{:T(128)S(6)} %select_n.23, f32[12,4,32,512]{3,2,1,0:T(8,128)} %bitcast.25), kind=kLoop, calls=%fused_computation.5 | loop fusion | bytes 1572872 | tf_op jit(solution)/shard_map/sum_over_x/convert_element_type | solution.py:164
  25.9 1.9 %collective-permute-start.2 = (bf16[12,32,512]{2,1,0:T(8,128)(2,1)S(1)}, bf16[12,32,512]{2,1,0:T(8,128)(2,1)S(1)}, u32[]{:S(2)}, u32[]{:S(2)}) collective-permute-start(bf16[12,32,512]{2,1,0:T(8,128)(2,1)S(1)} %get-tuple-element.23), channel_id=1, source_target_pairs={{0,1},{1,2},{2,3},{3,0},{4,5},{5,6},{6,7},{7,4},{8,9},{9,10},{10,1... | collective-permute-start | bytes 1179656 | tf_op jit(solution)/shard_map/sum_over_x/ppermute | solution.py:15
  27.8 4.6 %collective-permute-start.3 = (bf16[12,32,512]{2,1,0:T(8,128)(2,1)S(1)}, bf16[12,32,512]{2,1,0:T(8,128)(2,1)}, u32[]{:S(2)}, u32[]{:S(2)}) collective-permute-start(bf16[12,32,512]{2,1,0:T(8,128)(2,1)S(1)} %get-tuple-element.24), channel_id=1, source_target_pairs={{0,3},{1,0},{2,1},{3,2},{4,7},{5,4},{6,5},{7,6},{8,11},{9,8},{10,9... | collective-permute-start | bytes 1179656 | tf_op jit(solution)/shard_map/sum_over_x/ppermute | solution.py:15
  32.4 1.2 %dynamic-slice_bitcast_fusion.own_ref = f32[12,32,512]{2,1,0:T(8,128)S(1)} fusion(f32[12,4,32,512]{3,2,1,0:T(8,128)} %bitcast.26, s32[]{:T(128)S(6)} %select_n.20), kind=kLoop, calls=%fused_computation.4 | loop fusion | bytes 1572868 | tf_op jit(solution)/shard_map/sum_over_x/jit(dynamic_index_in_dim)/squeeze | solution.py:23
  33.6 0.0 copy-start.3
  33.7 1.0 %sum_over_x.1 = f32[12,32,512]{2,1,0:T(8,128)} custom-call(f32[12,32,512]{2,1,0:T(8,128)S(1)} %dynamic-slice_bitcast_fusion.own_ref, bf16[12,32,512]{2,1,0:T(8,128)(2,1)S(1)} %collective-permute-done.1.came_ref), custom_call_target="tpu_custom_call" | custom-call | flops 99999997952 | bytes 2097152 | tf_op jit(solution)/shard_map/sum_over_x/pallas_call | solution.py:102
  34.6 0.6 dynamic_slice.24
  37.2 2.6 %collective-permute-done.2 = bf16[12,32,512]{2,1,0:T(8,128)(2,1)S(1)} collective-permute-done((bf16[12,32,512]{2,1,0:T(8,128)(2,1)S(1)}, bf16[12,32,512]{2,1,0:T(8,128)(2,1)S(1)}, u32[]{:S(2)}, u32[]{:S(2)}) %collective-permute-start.2) | collective-permute-done | bytes 393248 | tf_op jit(solution)/shard_map/sum_over_x/ppermute | solution.py:15
  39.7 1.7 %collective-permute-done.3 = bf16[12,32,512]{2,1,0:T(8,128)(2,1)} collective-permute-done((bf16[12,32,512]{2,1,0:T(8,128)(2,1)S(1)}, bf16[12,32,512]{2,1,0:T(8,128)(2,1)}, u32[]{:S(2)}, u32[]{:S(2)}) %collective-permute-start.3) | collective-permute-done | bytes 393248 | tf_op jit(solution)/shard_map/sum_over_x/ppermute | solution.py:15
  41.4 2.2 %add_convert_fusion = bf16[12,32,512]{2,1,0:T(8,128)(2,1)} fusion(bf16[12,32,512]{2,1,0:T(8,128)(2,1)} %collective-permute-done.3, f32[12,32,512]{2,1,0:T(8,128)} %sum_over_x.1, bf16[12,32,512]{2,1,0:T(8,128)(2,1)S(1)} %collective-permute-done.2), kind=kLoop, calls=%fused_computation.1 | loop fusion | flops 983040 | bytes 1966080 | tf_op jit(solution)/shard_map/sum_over_x/convert_element_type | solution.py:167
  43.6 0.0 all-to-all-done
  43.6 10.7 %all-to-all-start.1 = ((bf16[12,32,512]{2,1,0:T(8,128)(2,1)}), bf16[12,32,512]{2,1,0:T(8,128)(2,1)S(1)}, u32[]{:S(2)}, u32[]{:S(2)}) async-start(bf16[12,32,512]{2,1,0:T(8,128)(2,1)} %add_convert_fusion), calls=%async_computation.1 | async-start | bytes 786432 | tf_op jit(solution)/shard_map/sum_over_z/all_to_all | solution.py:170
  54.3 20.2 %all_gather.6.right_ref = bf16[512,512]{1,0:T(8,128)(2,1)S(1)} all-gather(bf16[32,512]{1,0:T(8,128)(2,1)S(1)} %get-tuple-element.26), channel_id=1, replica_groups=mesh['y'=8,'c'=2,'z'=12,'x'=4] {'y','c'}, dimensions={0}, use_global_device_ids=true | all-gather | bytes 557056 | tf_op jit(solution)/shard_map/sum_over_x/all_gather | solution.py:168
  74.5 0.1 fusion.3
  74.5 18.5 %all_gather.7.whole_ref = bf16[512,512]{1,0:T(8,128)(2,1)S(1)} all-gather(bf16[32,512]{1,0:T(8,128)(2,1)S(1)} %get-tuple-element.19), channel_id=1, replica_groups=mesh['y'=8,'c'=2,'z'=12,'x'=4] {'y','c'}, dimensions={0}, use_global_device_ids=true | all-gather | bytes 557056 | tf_op jit(solution)/shard_map/whole_block/all_gather | solution.py:174
  93.0 1.4 %direction_and_statistics.1 = (f32[1,32,512]{2,1,0:T(8,128)}, f32[1,32,512]{2,1,0:T(8,128)}, bf16[1,32,512]{2,1,0:T(8,128)(2,1)}) custom-call(s32[1]{0:T(128)} %bitcast.me_ref, bf16[512,512]{1,0:T(8,128)(2,1)S(1)} %all_gather.7.whole_ref, bf16[512,512]{1,0:T(8,128)(2,1)S(1)} %all_gather.6.right_ref, bf16[32,512]{1,0:T(8,128)(2,1)S(1)} %get-tuple-element.25.lrows_ref, ...), custom_call_target="tpu_custom_call" | custom-call | flops 100000000 | bytes 2097152 | tf_op jit(solution)/shard_map/direction_and_statistics/pallas_call | solution.py:134
  (10 shorter events, 0.0 us)
Async XLA Ops:
  2.7 15.6 %collective-permute-start = (bf16[8,64,512]{2,1,0:T(8,128)(2,1)}, bf16[8,64,512]{2,1,0:T(8,128)(2,1)S(1)}, u32[]{:S(2)}, u32[]{:S(2)}) collective-permute-start(bf16[8,64,512]{2,1,0:T(8,128)(2,1)} %get-tuple-element.12), channel_id=1, source_target_pairs={{0,48},{48,0},{1,49},{49,1},{2,50},{50,2},{3,51},{51,3},{4,52},{52... | collective-permute-start | bytes 1572872 | tf_op jit(solution)/shard_map/owner_roots/ppermute | solution.py:158
  16.3 17.3 %collective-permute-start.1 = (bf16[12,32,512]{2,1,0:T(8,128)(2,1)S(1)}, bf16[12,32,512]{2,1,0:T(8,128)(2,1)S(1)}, u32[]{:S(2)}, u32[]{:S(2)}) collective-permute-start(bf16[12,32,512]{2,1,0:T(8,128)(2,1)S(1)} %fusion.2), channel_id=1, source_target_pairs={{0,2},{1,3},{2,0},{3,1},{4,6},{5,7},{6,4},{7,5},{8,10},{9,11},{10,... | collective-permute-start | bytes 1179656 | tf_op jit(solution)/shard_map/sum_over_x/ppermute | solution.py:15
  18.3 1.0 %copy-start = (bf16[8,64,512]{2,1,0:T(8,128)(2,1)S(1)}, bf16[8,64,512]{2,1,0:T(8,128)(2,1)}, u32[]{:S(2)}) copy-start(bf16[8,64,512]{2,1,0:T(8,128)(2,1)} %get-tuple-element.14.mine_ref) | copy-start | bytes 1572868
  20.9 22.7 %all-to-all-start = ((bf16[8,64,512]{2,1,0:T(8,128)(2,1)}), bf16[8,64,512]{2,1,0:T(8,128)(2,1)S(1)}, u32[]{:S(2)}, u32[]{:S(2)}) async-start(bf16[8,64,512]{2,1,0:T(8,128)(2,1)} %owner_roots.3), calls=%async_computation | async-start | bytes 1048576 | tf_op jit(solution)/shard_map/owner_roots/all_to_all | solution.py:161
  25.9 13.8 %collective-permute-start.2 = (bf16[12,32,512]{2,1,0:T(8,128)(2,1)S(1)}, bf16[12,32,512]{2,1,0:T(8,128)(2,1)S(1)}, u32[]{:S(2)}, u32[]{:S(2)}) collective-permute-start(bf16[12,32,512]{2,1,0:T(8,128)(2,1)S(1)} %get-tuple-element.23), channel_id=1, source_target_pairs={{0,1},{1,2},{2,3},{3,0},{4,5},{5,6},{6,7},{7,4},{8,9},{9,10},{10,1... | collective-permute-start | bytes 1179656 | tf_op jit(solution)/shard_map/sum_over_x/ppermute | solution.py:15
  27.8 13.6 %collective-permute-start.3 = (bf16[12,32,512]{2,1,0:T(8,128)(2,1)S(1)}, bf16[12,32,512]{2,1,0:T(8,128)(2,1)}, u32[]{:S(2)}, u32[]{:S(2)}) collective-permute-start(bf16[12,32,512]{2,1,0:T(8,128)(2,1)S(1)} %get-tuple-element.24), channel_id=1, source_target_pairs={{0,3},{1,0},{2,1},{3,2},{4,7},{5,4},{6,5},{7,6},{8,11},{9,8},{10,9... | collective-permute-start | bytes 1179656 | tf_op jit(solution)/shard_map/sum_over_x/ppermute | solution.py:15
  33.6 1.0 %copy-start.3 = (s32[48]{0:T(128)S(1)}, s32[48]{0:T(128)}, u32[]{:S(2)}) copy-start(s32[48]{0:T(128)} %owners_ref.1) | copy-start | bytes 580
  34.6 58.4 %copy-start.1 = (f32[1,32,512]{2,1,0:T(8,128)S(1)}, f32[1,32,512]{2,1,0:T(8,128)}, u32[]{:S(2)}) copy-start(f32[1,32,512]{2,1,0:T(8,128)} %lf_ref.1) | copy-start | bytes 196612
  34.6 58.4 %copy-start.2 = (f32[1,32,512]{2,1,0:T(8,128)S(1)}, f32[1,32,512]{2,1,0:T(8,128)}, u32[]{:S(2)}) copy-start(f32[1,32,512]{2,1,0:T(8,128)} %rf_ref.1) | copy-start | bytes 196612
  43.6 30.9 %all-to-all-start.1 = ((bf16[12,32,512]{2,1,0:T(8,128)(2,1)}), bf16[12,32,512]{2,1,0:T(8,128)(2,1)S(1)}, u32[]{:S(2)}, u32[]{:S(2)}) async-start(bf16[12,32,512]{2,1,0:T(8,128)(2,1)} %add_convert_fusion), calls=%async_computation.1 | async-start | bytes 786432 | tf_op jit(solution)/shard_map/sum_over_z/all_to_all | solution.py:170

commit v10 on v9

--- a/solution.py
+++ b/solution.py
@@ -74,38 +74,57 @@
 
 
 def of_owner(owners, block, core, mine, other):
-    def kernel(owners_ref, block_ref, core_ref, mine_ref, other_ref, out_ref):
+    parts = 2
+    step = mine.shape[0] // parts
+
+    def kernel(owners_ref, block_ref, core_ref, mine_ref, other_ref, out_ref, held, arrived, sent):
         here = lax.rem(owners_ref[block_ref[0]], C) == core_ref[0]
+        pieces = [pl.ds(i * step, step) for i in range(parts)]
 
         @pl.when(here)
         def _():
-            out_ref[...] = mine_ref[...]
+            coming = [pltpu.make_async_copy(mine_ref.at[p], held.at[p], arrived.at[i]) for i, p in enumerate(pieces)]
+            going = [pltpu.make_async_copy(held.at[p], out_ref.at[p], sent.at[i]) for i, p in enumerate(pieces)]
+            for copy in coming:
+                copy.start()
+            for i in range(parts):
+                coming[i].wait()
+                going[i].start()
+            for copy in going:
+                copy.wait()
 
         @pl.when(jnp.logical_not(here))
         def _():
-            out_ref[...] = other_ref[...]
-
+            copies = [pltpu.make_async_copy(other_ref.at[p], out_ref.at[p], sent.at[i]) for i, p in enumerate(pieces)]
+            for copy in copies:
+                copy.start()
+            for copy in copies:
+                copy.wait()
+
+    hbm = pl.BlockSpec(memory_space=pltpu.HBM)
     return pl.pallas_call(
         kernel,
         out_shape=jax.ShapeDtypeStruct(mine.shape, BF),
-        in_specs=[SMEM] * 3 + [VMEM] * 2,
+        in_specs=[SMEM] * 3 + [hbm, VMEM],
+        out_specs=hbm,
+        scratch_shapes=[pltpu.VMEM(mine.shape, BF), pltpu.SemaphoreType.DMA((parts,)), pltpu.SemaphoreType.DMA((parts,))],
+        cost_estimate=cost(10**6, 1 << 20),
+    )(owners, block, core, mine, in_vmem(other))
+
+
+def sum_of(kind, flops, *parts):
+    def kernel(*refs):
+        *given, out_ref = refs
+        for i in range(out_ref.shape[0]):
+            out_ref[i] = sum((ref[i].astype(F32) for ref in given[1:]), given[0][i].astype(F32)).astype(kind)
+
+    return pl.pallas_call(
+        kernel,
+        out_shape=jax.ShapeDtypeStruct(parts[0].shape, kind),
+        in_specs=[VMEM] * len(parts),
         out_specs=VMEM,
-        cost_estimate=cost(10**6, 1 << 20),
-    )(owners, block, core, in_vmem(mine), in_vmem(other))
-
-
-def first_sum(own, came):
-    def kernel(own_ref, came_ref, out_ref):
-        for i in range(own_ref.shape[0]):
-            out_ref[i] = own_ref[i] + came_ref[i].astype(F32)
-
-    return pl.pallas_call(
-        kernel,
-        out_shape=jax.ShapeDtypeStruct(own.shape, F32),
-        in_specs=[VMEM] * 2,
-        out_specs=VMEM,
-        cost_estimate=cost(10**11, 2 << 20),
-    )(in_vmem(own), in_vmem(came))
+        cost_estimate=cost(flops, 2 << 20),
+    )(parts[0], *(in_vmem(part) for part in parts[1:]))
 
 
 def after_gather(me, whole, right_inverse, left_rows, exact, left_factor, right_factor):
@@ -162,9 +181,10 @@
     with jax.named_scope("sum_over_x"):
         across = along_x(column(2).astype(BF), 2)
         beside = [along_x(column(step, after_swap).astype(BF), step) for step in (1, 3)]
-        over_x = first_sum(column(0, after_swap), across) + beside[0].astype(F32) + beside[1].astype(F32)
+        over_x = sum_of(F32, 10**11, column(0, after_swap), across)
+        over_x = sum_of(BF, 10**6, over_x, *beside)
         roots = pick(spread, lax.div(owners_too[block], C), 0)
-        over_x, roots = lax.optimization_barrier((over_x.astype(BF), roots))
+        over_x, roots = lax.optimization_barrier((over_x, roots))
         right_inverse = lax.all_gather(roots[rows:], ROWS, axis=0, tiled=True)
     with jax.named_scope("sum_over_z"):
         exact = added(lax.all_to_all(over_x, "z", 0, 0, tiled=True))

time: 95.4 us -> 95.4 us (level)
  Pallas kernels: 5.98 us -> 10.1 us
  other arithmetic: 2.22 us -> 0.06 us
  waiting for transfers between devices: 4.25 us -> 2.65 us
    pallas_call x1 -> x2, Pallas kernels: 0.97 us -> 4.12 us  [sum_of(): pl.pallas_call(kernel, out_shape=jax.ShapeDtypeStruct(parts[0].shape, kin...]
    convert_element_type x1 -> x0, other arithmetic: 2.16 us -> none  [on_device(): over_x, roots = lax.optimization_barrier((over_x.astype(BF), roots))]
    ppermute x3, waiting for transfers between devices: 4.24 us -> 2.64 us  [along_x(): return lax.ppermute(value, 'x', [(i, (i + step) % X) for i in range(X)])]
    unnamed x8 -> x6, local copies, waits for them, and re-layouts: 1.05 us -> 0.01 us
  transfers between devices with their start and end apart: 6 -> 6, of which waited for: 2 -> 2; matrix products, arithmetic and copies ran while one was open for 7% -> 6% of each run, Pallas kernels for 3% -> 7%
where the time goes in v10:
time: 95.4 us; the launch traced here: 94.7 us
  blocking collectives  38.9 us (41%)
  starting transfers between devices  34.9 us (37%)
  Pallas kernels  10.1 us (11%)
  local copies, waits for them, and re-layouts  5.42 us (6%)
  between operations  2.75 us (3%)
  waiting for transfers between devices  2.65 us (3%)
    all_gather x1, blocking collectives, on_device(): right_inverse = lax.all_gather(roots[rows:], ROWS, axis=0, tiled=True)  19.7 us
    all_gather x1, blocking collectives, on_device(): whole = lax.all_gather(my_rows, ROWS, axis=0, tiled=True)  19.2 us
    ppermute x1, starting transfers between devices, on_device(): given = lax.ppermute(give, 'c', [(0, 1), (1, 0)])  12.4 us
    all_to_all x1, starting transfers between devices, on_device(): exact = added(lax.all_to_all(over_x, 'z', 0, 0, tiled=True))  10.5 us
    ppermute x3, starting transfers between devices, along_x(): return lax.ppermute(value, 'x', [(i, (i + step) % X) for i in range(X)])  8.41 us
    pallas_call x2, Pallas kernels, sum_of(): pl.pallas_call(kernel, out_shape=jax.ShapeDtypeStruct(parts[0].shape, kin...  4.12 us
    all_to_all x1, starting transfers between devices, on_device(): spread = lax.all_to_all(slots, 'y', 0, 0, tiled=True)  3.5 us
    ppermute x3, waiting for transfers between devices, along_x(): return lax.ppermute(value, 'x', [(i, (i + step) % X) for i in range(X)])  2.64 us
  transfers between devices with their start and end apart: 6, of which 2 were waited for; matrix products, arithmetic and copies ran while one was open for 6% of the time, Pallas kernels for 7%

profile of v10, /device:TPU:1, one launch (start us, length us, event | category | flops | bytes accessed | tf_op | source)
XLA Modules:
  0.0 94.7 jit_solution(12772730933446842887)
XLA Ops:
  0.6 2.1 %owner_roots.2 = (bf16[8,64,512]{2,1,0:T(8,128)(2,1)}, bf16[8,64,512]{2,1,0:T(8,128)(2,1)}) custom-call(s32[1]{0:T(128)} %bitcast.1.core_ref, bf16[8,2,32,512]{3,2,1,0:T(8,128)(2,1)} %bitcast.27, bf16[8,2,32,512]{3,2,1,0:T(8,128)(2,1)} %bitcast.28), custom_call_target="tpu_custom_call" | custom-call | flops 1000000 | bytes 1048576 | tf_op jit(solution)/shard_map/owner_roots/pallas_call | solution.py:66
  2.7 12.4 %collective-permute-start = (bf16[8,64,512]{2,1,0:T(8,128)(2,1)}, bf16[8,64,512]{2,1,0:T(8,128)(2,1)S(1)}, u32[]{:S(2)}, u32[]{:S(2)}) collective-permute-start(bf16[8,64,512]{2,1,0:T(8,128)(2,1)} %get-tuple-element.12), channel_id=1, source_target_pairs={{0,48},{48,0},{1,49},{49,1},{2,50},{50,2},{3,51},{51,3},{4,52},{52... | collective-permute-start | bytes 1572872 | tf_op jit(solution)/shard_map/owner_roots/ppermute | solution.py:177
  15.1 1.2 %fusion.2 = bf16[12,32,512]{2,1,0:T(8,128)(2,1)S(1)} fusion(f32[12,4,32,512]{3,2,1,0:T(8,128)} %bitcast.24, s32[]{:T(128)S(6)} %select_n.21), kind=kLoop, calls=%fused_computation.6 | loop fusion | bytes 786436 | tf_op jit(solution)/shard_map/sum_over_x/convert_element_type | solution.py:182
  16.3 1.9 %collective-permute-start.1 = (bf16[12,32,512]{2,1,0:T(8,128)(2,1)S(1)}, bf16[12,32,512]{2,1,0:T(8,128)(2,1)S(1)}, u32[]{:S(2)}, u32[]{:S(2)}) collective-permute-start(bf16[12,32,512]{2,1,0:T(8,128)(2,1)S(1)} %fusion.2), channel_id=1, source_target_pairs={{0,2},{1,3},{2,0},{3,1},{4,6},{5,7},{6,4},{7,5},{8,10},{9,11},{10,... | collective-permute-start | bytes 1179656 | tf_op jit(solution)/shard_map/sum_over_x/ppermute | solution.py:15
  18.3 0.0 collective-permute-done.other_ref
  18.3 2.5 %owner_roots.3 = bf16[8,64,512]{2,1,0:T(8,128)(2,1)} custom-call(s32[48]{0:T(128)} %owners_ref.1, s32[1]{0:T(128)} %bitcast.9.block_ref, s32[1]{0:T(128)} %bitcast.1.core_ref, bf16[8,64,512]{2,1,0:T(8,128)(2,1)} %get-tuple-element.14.mine_ref, bf16[8,64,512]{2,1,0:T(8,128)(2,1)S(1)} %collective-permute-done.other_ref), custom_call_target="tpu_custom_call" | custom-call | flops 1000000 | bytes 1048576 | tf_op jit(solution)/shard_map/owner_roots/pallas_call | solution.py:105
  20.8 3.5 %all-to-all-start = ((bf16[8,64,512]{2,1,0:T(8,128)(2,1)}), bf16[8,64,512]{2,1,0:T(8,128)(2,1)S(1)}, u32[]{:S(2)}, u32[]{:S(2)}) async-start(bf16[8,64,512]{2,1,0:T(8,128)(2,1)} %owner_roots.3), calls=%async_computation | async-start | bytes 1048576 | tf_op jit(solution)/shard_map/owner_roots/all_to_all | solution.py:180
  24.3 1.5 %fusion.1 = (bf16[12,32,512]{2,1,0:T(8,128)(2,1)S(1)}, bf16[12,32,512]{2,1,0:T(8,128)(2,1)S(1)}) fusion(s32[]{:T(128)S(6)} %select_n.23, s32[]{:T(128)S(6)} %select_n.22, f32[12,4,32,512]{3,2,1,0:T(8,128)} %bitcast.25), kind=kLoop, calls=%fused_computation.5 | loop fusion | bytes 1572872 | tf_op jit(solution)/shard_map/sum_over_x/convert_element_type | solution.py:183
  25.8 1.9 %collective-permute-start.2 = (bf16[12,32,512]{2,1,0:T(8,128)(2,1)S(1)}, bf16[12,32,512]{2,1,0:T(8,128)(2,1)S(1)}, u32[]{:S(2)}, u32[]{:S(2)}) collective-permute-start(bf16[12,32,512]{2,1,0:T(8,128)(2,1)S(1)} %get-tuple-element.24), channel_id=1, source_target_pairs={{0,1},{1,2},{2,3},{3,0},{4,5},{5,6},{6,7},{7,4},{8,9},{9,10},{10,1... | collective-permute-start | bytes 1179656 | tf_op jit(solution)/shard_map/sum_over_x/ppermute | solution.py:15
  27.7 4.6 %collective-permute-start.3 = (bf16[12,32,512]{2,1,0:T(8,128)(2,1)S(1)}, bf16[12,32,512]{2,1,0:T(8,128)(2,1)S(1)}, u32[]{:S(2)}, u32[]{:S(2)}) collective-permute-start(bf16[12,32,512]{2,1,0:T(8,128)(2,1)S(1)} %get-tuple-element.23), channel_id=1, source_target_pairs={{0,3},{1,0},{2,1},{3,2},{4,7},{5,4},{6,5},{7,6},{8,11},{9,8},{10,9... | collective-permute-start | bytes 1179656 | tf_op jit(solution)/shard_map/sum_over_x/ppermute | solution.py:15
  32.3 2.1 %dynamic-slice_bitcast_fusion.refs_0_ = f32[12,32,512]{2,1,0:T(8,128)} fusion(f32[12,4,32,512]{3,2,1,0:T(8,128)} %bitcast.26, s32[]{:T(128)S(6)} %select_n.20), kind=kLoop, calls=%fused_computation.3 | loop fusion | bytes 1572868 | tf_op jit(solution)/shard_map/sum_over_x/jit(dynamic_index_in_dim)/squeeze | solution.py:23
  34.4 0.0 collective-permute-done.1.refs_1_
  34.4 2.1 %sum_over_x.2.refs_0_ = f32[12,32,512]{2,1,0:T(8,128)} custom-call(f32[12,32,512]{2,1,0:T(8,128)} %dynamic-slice_bitcast_fusion.refs_0_, bf16[12,32,512]{2,1,0:T(8,128)(2,1)S(1)} %collective-permute-done.1.refs_1_), custom_call_target="tpu_custom_call" | custom-call | flops 99999997952 | bytes 2097152 | tf_op jit(solution)/shard_map/sum_over_x/pallas_call | solution.py:121
  36.6 0.6 dynamic_slice.24
  39.1 0.5 collective-permute-done.2.refs_1_
  39.6 2.2 %collective-permute-done.3.refs_2_ = bf16[12,32,512]{2,1,0:T(8,128)(2,1)S(1)} collective-permute-done((bf16[12,32,512]{2,1,0:T(8,128)(2,1)S(1)}, bf16[12,32,512]{2,1,0:T(8,128)(2,1)S(1)}, u32[]{:S(2)}, u32[]{:S(2)}) %collective-permute-start.3) | collective-permute-done | bytes 393248 | tf_op jit(solution)/shard_map/sum_over_x/ppermute | solution.py:15
  41.7 2.0 %sum_over_x.3 = bf16[12,32,512]{2,1,0:T(8,128)(2,1)} custom-call(f32[12,32,512]{2,1,0:T(8,128)} %sum_over_x.2.refs_0_, bf16[12,32,512]{2,1,0:T(8,128)(2,1)S(1)} %collective-permute-done.2.refs_1_, bf16[12,32,512]{2,1,0:T(8,128)(2,1)S(1)} %collective-permute-done.3.refs_2_), custom_call_target="tpu_custom_call" | custom-call | flops 1000000 | bytes 2097152 | tf_op jit(solution)/shard_map/sum_over_x/pallas_call | solution.py:121
  43.7 0.0 all-to-all-done
  43.7 10.5 %all-to-all-start.1 = ((bf16[12,32,512]{2,1,0:T(8,128)(2,1)}), bf16[12,32,512]{2,1,0:T(8,128)(2,1)S(1)}, u32[]{:S(2)}, u32[]{:S(2)}) async-start(bf16[12,32,512]{2,1,0:T(8,128)(2,1)} %sum_over_x.3), calls=%async_computation.1 | async-start | bytes 786432 | tf_op jit(solution)/shard_map/sum_over_z/all_to_all | solution.py:190
  54.3 19.7 %all_gather.6.right_ref = bf16[512,512]{1,0:T(8,128)(2,1)S(1)} all-gather(bf16[32,512]{1,0:T(8,128)(2,1)S(1)} %get-tuple-element.26), channel_id=1, replica_groups=mesh['y'=8,'c'=2,'z'=12,'x'=4] {'y','c'}, dimensions={0}, use_global_device_ids=true | all-gather | bytes 557056 | tf_op jit(solution)/shard_map/sum_over_x/all_gather | solution.py:188
  74.0 0.0 all-to-all-done.1
  74.0 0.1 fusion.3
  74.1 19.2 %all_gather.7.whole_ref = bf16[512,512]{1,0:T(8,128)(2,1)S(1)} all-gather(bf16[32,512]{1,0:T(8,128)(2,1)S(1)} %get-tuple-element.19), channel_id=1, replica_groups=mesh['y'=8,'c'=2,'z'=12,'x'=4] {'y','c'}, dimensions={0}, use_global_device_ids=true | all-gather | bytes 557056 | tf_op jit(solution)/shard_map/whole_block/all_gather | solution.py:194
  93.3 1.4 %direction_and_statistics.1 = (f32[1,32,512]{2,1,0:T(8,128)}, f32[1,32,512]{2,1,0:T(8,128)}, bf16[1,32,512]{2,1,0:T(8,128)(2,1)}) custom-call(s32[1]{0:T(128)} %bitcast.me_ref, bf16[512,512]{1,0:T(8,128)(2,1)S(1)} %all_gather.7.whole_ref, bf16[512,512]{1,0:T(8,128)(2,1)S(1)} %all_gather.6.right_ref, bf16[32,512]{1,0:T(8,128)(2,1)S(1)} %get-tuple-element.25.lrows_ref, ...), custom_call_target="tpu_custom_call" | custom-call | flops 100000000 | bytes 2097152 | tf_op jit(solution)/shard_map/direction_and_statistics/pallas_call | solution.py:153
  (8 shorter events, 0.0 us)
Async XLA Ops:
  2.7 15.6 %collective-permute-start = (bf16[8,64,512]{2,1,0:T(8,128)(2,1)}, bf16[8,64,512]{2,1,0:T(8,128)(2,1)S(1)}, u32[]{:S(2)}, u32[]{:S(2)}) collective-permute-start(bf16[8,64,512]{2,1,0:T(8,128)(2,1)} %get-tuple-element.12), channel_id=1, source_target_pairs={{0,48},{48,0},{1,49},{49,1},{2,50},{50,2},{3,51},{51,3},{4,52},{52... | collective-permute-start | bytes 1572872 | tf_op jit(solution)/shard_map/owner_roots/ppermute | solution.py:177
  16.3 18.1 %collective-permute-start.1 = (bf16[12,32,512]{2,1,0:T(8,128)(2,1)S(1)}, bf16[12,32,512]{2,1,0:T(8,128)(2,1)S(1)}, u32[]{:S(2)}, u32[]{:S(2)}) collective-permute-start(bf16[12,32,512]{2,1,0:T(8,128)(2,1)S(1)} %fusion.2), channel_id=1, source_target_pairs={{0,2},{1,3},{2,0},{3,1},{4,6},{5,7},{6,4},{7,5},{8,10},{9,11},{10,... | collective-permute-start | bytes 1179656 | tf_op jit(solution)/shard_map/sum_over_x/ppermute | solution.py:15
  20.8 23.0 %all-to-all-start = ((bf16[8,64,512]{2,1,0:T(8,128)(2,1)}), bf16[8,64,512]{2,1,0:T(8,128)(2,1)S(1)}, u32[]{:S(2)}, u32[]{:S(2)}) async-start(bf16[8,64,512]{2,1,0:T(8,128)(2,1)} %owner_roots.3), calls=%async_computation | async-start | bytes 1048576 | tf_op jit(solution)/shard_map/owner_roots/all_to_all | solution.py:180
  25.8 13.8 %collective-permute-start.2 = (bf16[12,32,512]{2,1,0:T(8,128)(2,1)S(1)}, bf16[12,32,512]{2,1,0:T(8,128)(2,1)S(1)}, u32[]{:S(2)}, u32[]{:S(2)}) collective-permute-start(bf16[12,32,512]{2,1,0:T(8,128)(2,1)S(1)} %get-tuple-element.24), channel_id=1, source_target_pairs={{0,1},{1,2},{2,3},{3,0},{4,5},{5,6},{6,7},{7,4},{8,9},{9,10},{10,1... | collective-permute-start | bytes 1179656 | tf_op jit(solution)/shard_map/sum_over_x/ppermute | solution.py:15
  27.7 14.0 %collective-permute-start.3 = (bf16[12,32,512]{2,1,0:T(8,128)(2,1)S(1)}, bf16[12,32,512]{2,1,0:T(8,128)(2,1)S(1)}, u32[]{:S(2)}, u32[]{:S(2)}) collective-permute-start(bf16[12,32,512]{2,1,0:T(8,128)(2,1)S(1)} %get-tuple-element.23), channel_id=1, source_target_pairs={{0,3},{1,0},{2,1},{3,2},{4,7},{5,4},{6,5},{7,6},{8,11},{9,8},{10,9... | collective-permute-start | bytes 1179656 | tf_op jit(solution)/shard_map/sum_over_x/ppermute | solution.py:15
  34.4 2.1 %copy-start.2 = (s32[48]{0:T(128)S(1)}, s32[48]{0:T(128)}, u32[]{:S(2)}) copy-start(s32[48]{0:T(128)} %owners_ref.1) | copy-start | bytes 580
  36.6 56.7 %copy-start = (f32[1,32,512]{2,1,0:T(8,128)S(1)}, f32[1,32,512]{2,1,0:T(8,128)}, u32[]{:S(2)}) copy-start(f32[1,32,512]{2,1,0:T(8,128)} %lf_ref.1) | copy-start | bytes 196612
  36.6 56.7 %copy-start.1 = (f32[1,32,512]{2,1,0:T(8,128)S(1)}, f32[1,32,512]{2,1,0:T(8,128)}, u32[]{:S(2)}) copy-start(f32[1,32,512]{2,1,0:T(8,128)} %rf_ref.1) | copy-start | bytes 196612
  43.7 30.3 %all-to-all-start.1 = ((bf16[12,32,512]{2,1,0:T(8,128)(2,1)}), bf16[12,32,512]{2,1,0:T(8,128)(2,1)S(1)}, u32[]{:S(2)}, u32[]{:S(2)}) async-start(bf16[12,32,512]{2,1,0:T(8,128)(2,1)} %sum_over_x.3), calls=%async_computation.1 | async-start | bytes 786432 | tf_op jit(solution)/shard_map/sum_over_z/all_to_all | solution.py:190

commit v11 on v10

--- a/solution.py
+++ b/solution.py
@@ -180,7 +180,7 @@
         spread = lax.all_to_all(slots, "y", 0, 0, tiled=True)
     with jax.named_scope("sum_over_x"):
         across = along_x(column(2).astype(BF), 2)
-        beside = [along_x(column(step, after_swap).astype(BF), step) for step in (1, 3)]
+        beside = [along_x(column(3).astype(BF), 3), along_x(column(1, after_swap).astype(BF), 1)]
         over_x = sum_of(F32, 10**11, column(0, after_swap), across)
         over_x = sum_of(BF, 10**6, over_x, *beside)
         roots = pick(spread, lax.div(owners_too[block], C), 0)

time: 95.4 us -> 97.4 us (1.021)
  starting transfers between devices: 34.9 us -> 36.5 us
  waiting for transfers between devices: 2.65 us -> 4.09 us
  blocking collectives: 38.9 us -> 37.8 us
    all_to_all x1, starting transfers between devices: 10.5 us -> 13.4 us  [on_device(): exact = added(lax.all_to_all(over_x, 'z', 0, 0, tiled=True))]
    all_to_all x1, waiting for transfers between devices: 0.01 us -> 1.37 us  [on_device(): spread = lax.all_to_all(slots, 'y', 0, 0, tiled=True)]
    all_gather x1, blocking collectives: 19.7 us -> 18.4 us  [on_device(): right_inverse = lax.all_gather(roots[rows:], ROWS, axis=0, tiled=True)]
    ppermute x3, starting transfers between devices: 8.41 us -> 7.2 us  [along_x(): return lax.ppermute(value, 'x', [(i, (i + step) % X) for i in range(X)])]
where the time goes in v11:
time: 97.4 us; the launch traced here: 96.7 us
  blocking collectives  37.8 us (39%)
  starting transfers between devices  36.5 us (37%)
  Pallas kernels  10.1 us (10%)
  local copies, waits for them, and re-layouts  5.42 us (6%)
  waiting for transfers between devices  4.09 us (4%)
  between operations  2.75 us (3%)
    all_gather x1, blocking collectives, on_device(): whole = lax.all_gather(my_rows, ROWS, axis=0, tiled=True)  19.4 us
    all_gather x1, blocking collectives, on_device(): right_inverse = lax.all_gather(roots[rows:], ROWS, axis=0, tiled=True)  18.4 us
    all_to_all x1, starting transfers between devices, on_device(): exact = added(lax.all_to_all(over_x, 'z', 0, 0, tiled=True))  13.4 us
    ppermute x1, starting transfers between devices, on_device(): given = lax.ppermute(give, 'c', [(0, 1), (1, 0)])  12.4 us
    ppermute x3, starting transfers between devices, along_x(): return lax.ppermute(value, 'x', [(i, (i + step) % X) for i in range(X)])  7.2 us
    pallas_call x2, Pallas kernels, sum_of(): pl.pallas_call(kernel, out_shape=jax.ShapeDtypeStruct(parts[0].shape, kin...  4.12 us
    all_to_all x1, starting transfers between devices, on_device(): spread = lax.all_to_all(slots, 'y', 0, 0, tiled=True)  3.5 us
    ppermute x3, waiting for transfers between devices, along_x(): return lax.ppermute(value, 'x', [(i, (i + step) % X) for i in range(X)])  2.71 us
  transfers between devices with their start and end apart: 6, of which 2 were waited for; matrix products, arithmetic and copies ran while one was open for 6% of the time, Pallas kernels for 7%

profile of v11, /device:TPU:1, one launch (start us, length us, event | category | flops | bytes accessed | tf_op | source)
XLA Modules:
  0.0 96.7 jit_solution(4462766148460227484)
XLA Ops:
  0.6 2.1 %owner_roots.2 = (bf16[8,64,512]{2,1,0:T(8,128)(2,1)}, bf16[8,64,512]{2,1,0:T(8,128)(2,1)}) custom-call(s32[1]{0:T(128)} %bitcast.1.core_ref, bf16[8,2,32,512]{3,2,1,0:T(8,128)(2,1)} %bitcast.31, bf16[8,2,32,512]{3,2,1,0:T(8,128)(2,1)} %bitcast.32), custom_call_target="tpu_custom_call" | custom-call | flops 1000000 | bytes 1048576 | tf_op jit(solution)/shard_map/owner_roots/pallas_call | solution.py:66
  2.7 12.4 %collective-permute-start = (bf16[8,64,512]{2,1,0:T(8,128)(2,1)}, bf16[8,64,512]{2,1,0:T(8,128)(2,1)S(1)}, u32[]{:S(2)}, u32[]{:S(2)}) collective-permute-start(bf16[8,64,512]{2,1,0:T(8,128)(2,1)} %get-tuple-element.12), channel_id=1, source_target_pairs={{0,48},{48,0},{1,49},{49,1},{2,50},{50,2},{3,51},{51,3},{4,52},{52... | collective-permute-start | bytes 1572872 | tf_op jit(solution)/shard_map/owner_roots/ppermute | solution.py:177
  15.2 1.5 %fusion.2 = (bf16[12,32,512]{2,1,0:T(8,128)(2,1)S(1)}, bf16[12,32,512]{2,1,0:T(8,128)(2,1)S(1)}) fusion(f32[12,4,32,512]{3,2,1,0:T(8,128)} %bitcast.28, s32[]{:T(128)S(6)} %select_n.22, s32[]{:T(128)S(6)} %select_n.21), kind=kLoop, calls=%fused_computation.6 | loop fusion | bytes 1572872 | tf_op jit(solution)/shard_map/sum_over_x/convert_element_type | solution.py:183
  16.7 1.9 %collective-permute-start.1 = (bf16[12,32,512]{2,1,0:T(8,128)(2,1)S(1)}, bf16[12,32,512]{2,1,0:T(8,128)(2,1)S(1)}, u32[]{:S(2)}, u32[]{:S(2)}) collective-permute-start(bf16[12,32,512]{2,1,0:T(8,128)(2,1)S(1)} %get-tuple-element.24), channel_id=1, source_target_pairs={{0,2},{1,3},{2,0},{3,1},{4,6},{5,7},{6,4},{7,5},{8,10},{9,11},{10,... | collective-permute-start | bytes 1179656 | tf_op jit(solution)/shard_map/sum_over_x/ppermute | solution.py:15
  18.6 1.9 %collective-permute-start.2 = (bf16[12,32,512]{2,1,0:T(8,128)(2,1)S(1)}, bf16[12,32,512]{2,1,0:T(8,128)(2,1)S(1)}, u32[]{:S(2)}, u32[]{:S(2)}) collective-permute-start(bf16[12,32,512]{2,1,0:T(8,128)(2,1)S(1)} %get-tuple-element.23), channel_id=1, source_target_pairs={{0,3},{1,0},{2,1},{3,2},{4,7},{5,4},{6,5},{7,6},{8,11},{9,8},{10,9... | collective-permute-start | bytes 1179656 | tf_op jit(solution)/shard_map/sum_over_x/ppermute | solution.py:15
  20.5 0.0 collective-permute-done.other_ref
  20.6 2.5 %owner_roots.3 = bf16[8,64,512]{2,1,0:T(8,128)(2,1)} custom-call(s32[48]{0:T(128)} %owners_ref.1, s32[1]{0:T(128)} %bitcast.9.block_ref, s32[1]{0:T(128)} %bitcast.1.core_ref, bf16[8,64,512]{2,1,0:T(8,128)(2,1)} %get-tuple-element.14.mine_ref, bf16[8,64,512]{2,1,0:T(8,128)(2,1)S(1)} %collective-permute-done.other_ref), custom_call_target="tpu_custom_call" | custom-call | flops 1000000 | bytes 1048576 | tf_op jit(solution)/shard_map/owner_roots/pallas_call | solution.py:105
  23.0 3.5 %all-to-all-start = ((bf16[8,64,512]{2,1,0:T(8,128)(2,1)}), bf16[8,64,512]{2,1,0:T(8,128)(2,1)S(1)}, u32[]{:S(2)}, u32[]{:S(2)}) async-start(bf16[8,64,512]{2,1,0:T(8,128)(2,1)} %owner_roots.3), calls=%async_computation | async-start | bytes 1048576 | tf_op jit(solution)/shard_map/owner_roots/all_to_all | solution.py:180
  26.5 1.2 %fusion = bf16[12,32,512]{2,1,0:T(8,128)(2,1)S(1)} fusion(s32[]{:T(128)S(6)} %select_n.23, f32[12,4,32,512]{3,2,1,0:T(8,128)} %bitcast.29), kind=kLoop, calls=%fused_computation.4 | loop fusion | bytes 786436 | tf_op jit(solution)/shard_map/sum_over_x/convert_element_type | solution.py:183
  27.7 3.4 %collective-permute-start.3 = (bf16[12,32,512]{2,1,0:T(8,128)(2,1)S(1)}, bf16[12,32,512]{2,1,0:T(8,128)(2,1)S(1)}, u32[]{:S(2)}, u32[]{:S(2)}) collective-permute-start(bf16[12,32,512]{2,1,0:T(8,128)(2,1)S(1)} %fusion), channel_id=1, source_target_pairs={{0,1},{1,2},{2,3},{3,0},{4,5},{5,6},{6,7},{7,4},{8,9},{9,10},{10,1... | collective-permute-start | bytes 1179656 | tf_op jit(solution)/shard_map/sum_over_x/ppermute | solution.py:15
  31.1 2.1 %dynamic-slice_bitcast_fusion.refs_0_ = f32[12,32,512]{2,1,0:T(8,128)} fusion(f32[12,4,32,512]{3,2,1,0:T(8,128)} %bitcast.30, s32[]{:T(128)S(6)} %select_n.20), kind=kLoop, calls=%fused_computation.3 | loop fusion | bytes 1572868 | tf_op jit(solution)/shard_map/sum_over_x/jit(dynamic_index_in_dim)/squeeze | solution.py:23
  33.2 0.0 collective-permute-done.1.refs_1_
  33.2 2.1 %sum_over_x.2.refs_0_ = f32[12,32,512]{2,1,0:T(8,128)} custom-call(f32[12,32,512]{2,1,0:T(8,128)} %dynamic-slice_bitcast_fusion.refs_0_, bf16[12,32,512]{2,1,0:T(8,128)(2,1)S(1)} %collective-permute-done.1.refs_1_), custom_call_target="tpu_custom_call" | custom-call | flops 99999997952 | bytes 2097152 | tf_op jit(solution)/shard_map/sum_over_x/pallas_call | solution.py:121
  35.4 0.6 dynamic_slice.24
  37.9 0.0 collective-permute-done.2.refs_1_
  37.9 2.7 %collective-permute-done.3.refs_2_ = bf16[12,32,512]{2,1,0:T(8,128)(2,1)S(1)} collective-permute-done((bf16[12,32,512]{2,1,0:T(8,128)(2,1)S(1)}, bf16[12,32,512]{2,1,0:T(8,128)(2,1)S(1)}, u32[]{:S(2)}, u32[]{:S(2)}) %collective-permute-start.3) | collective-permute-done | bytes 393248 | tf_op jit(solution)/shard_map/sum_over_x/ppermute | solution.py:15
  40.6 2.0 %sum_over_x.3 = bf16[12,32,512]{2,1,0:T(8,128)(2,1)} custom-call(f32[12,32,512]{2,1,0:T(8,128)} %sum_over_x.2.refs_0_, bf16[12,32,512]{2,1,0:T(8,128)(2,1)S(1)} %collective-permute-done.2.refs_1_, bf16[12,32,512]{2,1,0:T(8,128)(2,1)S(1)} %collective-permute-done.3.refs_2_), custom_call_target="tpu_custom_call" | custom-call | flops 1000000 | bytes 2097152 | tf_op jit(solution)/shard_map/sum_over_x/pallas_call | solution.py:121
  42.6 1.4 %all-to-all-done = bf16[8,64,512]{2,1,0:T(8,128)(2,1)S(1)} async-done(((bf16[8,64,512]{2,1,0:T(8,128)(2,1)}), bf16[8,64,512]{2,1,0:T(8,128)(2,1)S(1)}, u32[]{:S(2)}, u32[]{:S(2)}) %all-to-all-start) | async-done | bytes 524320 | tf_op jit(solution)/shard_map/owner_roots/all_to_all | solution.py:180
  44.0 13.4 %all-to-all-start.1 = ((bf16[12,32,512]{2,1,0:T(8,128)(2,1)}), bf16[12,32,512]{2,1,0:T(8,128)(2,1)S(1)}, u32[]{:S(2)}, u32[]{:S(2)}) async-start(bf16[12,32,512]{2,1,0:T(8,128)(2,1)} %sum_over_x.3), calls=%async_computation.1 | async-start | bytes 786432 | tf_op jit(solution)/shard_map/sum_over_z/all_to_all | solution.py:190
  57.4 18.4 %all_gather.6.right_ref = bf16[512,512]{1,0:T(8,128)(2,1)S(1)} all-gather(bf16[32,512]{1,0:T(8,128)(2,1)S(1)} %get-tuple-element.26), channel_id=1, replica_groups=mesh['y'=8,'c'=2,'z'=12,'x'=4] {'y','c'}, dimensions={0}, use_global_device_ids=true | all-gather | bytes 557056 | tf_op jit(solution)/shard_map/sum_over_x/all_gather | solution.py:188
  75.8 0.0 all-to-all-done.1
  75.8 0.1 fusion.3
  75.9 19.4 %all_gather.7.whole_ref = bf16[512,512]{1,0:T(8,128)(2,1)S(1)} all-gather(bf16[32,512]{1,0:T(8,128)(2,1)S(1)} %get-tuple-element.19), channel_id=1, replica_groups=mesh['y'=8,'c'=2,'z'=12,'x'=4] {'y','c'}, dimensions={0}, use_global_device_ids=true | all-gather | bytes 557056 | tf_op jit(solution)/shard_map/whole_block/all_gather | solution.py:194
  95.3 1.4 %direction_and_statistics.1 = (f32[1,32,512]{2,1,0:T(8,128)}, f32[1,32,512]{2,1,0:T(8,128)}, bf16[1,32,512]{2,1,0:T(8,128)(2,1)}) custom-call(s32[1]{0:T(128)} %bitcast.me_ref, bf16[512,512]{1,0:T(8,128)(2,1)S(1)} %all_gather.7.whole_ref, bf16[512,512]{1,0:T(8,128)(2,1)S(1)} %all_gather.6.right_ref, bf16[32,512]{1,0:T(8,128)(2,1)S(1)} %get-tuple-element.25.lrows_ref, ...), custom_call_target="tpu_custom_call" | custom-call | flops 100000000 | bytes 2097152 | tf_op jit(solution)/shard_map/direction_and_statistics/pallas_call | solution.py:153
  (8 shorter events, 0.0 us)
Async XLA Ops:
  2.7 17.8 %collective-permute-start = (bf16[8,64,512]{2,1,0:T(8,128)(2,1)}, bf16[8,64,512]{2,1,0:T(8,128)(2,1)S(1)}, u32[]{:S(2)}, u32[]{:S(2)}) collective-permute-start(bf16[8,64,512]{2,1,0:T(8,128)(2,1)} %get-tuple-element.12), channel_id=1, source_target_pairs={{0,48},{48,0},{1,49},{49,1},{2,50},{50,2},{3,51},{51,3},{4,52},{52... | collective-permute-start | bytes 1572872 | tf_op jit(solution)/shard_map/owner_roots/ppermute | solution.py:177
  16.7 16.6 %collective-permute-start.1 = (bf16[12,32,512]{2,1,0:T(8,128)(2,1)S(1)}, bf16[12,32,512]{2,1,0:T(8,128)(2,1)S(1)}, u32[]{:S(2)}, u32[]{:S(2)}) collective-permute-start(bf16[12,32,512]{2,1,0:T(8,128)(2,1)S(1)} %get-tuple-element.24), channel_id=1, source_target_pairs={{0,2},{1,3},{2,0},{3,1},{4,6},{5,7},{6,4},{7,5},{8,10},{9,11},{10,... | collective-permute-start | bytes 1179656 | tf_op jit(solution)/shard_map/sum_over_x/ppermute | solution.py:15
  18.6 19.3 %collective-permute-start.2 = (bf16[12,32,512]{2,1,0:T(8,128)(2,1)S(1)}, bf16[12,32,512]{2,1,0:T(8,128)(2,1)S(1)}, u32[]{:S(2)}, u32[]{:S(2)}) collective-permute-start(bf16[12,32,512]{2,1,0:T(8,128)(2,1)S(1)} %get-tuple-element.23), channel_id=1, source_target_pairs={{0,3},{1,0},{2,1},{3,2},{4,7},{5,4},{6,5},{7,6},{8,11},{9,8},{10,9... | collective-permute-start | bytes 1179656 | tf_op jit(solution)/shard_map/sum_over_x/ppermute | solution.py:15
  23.0 21.0 %all-to-all-start = ((bf16[8,64,512]{2,1,0:T(8,128)(2,1)}), bf16[8,64,512]{2,1,0:T(8,128)(2,1)S(1)}, u32[]{:S(2)}, u32[]{:S(2)}) async-start(bf16[8,64,512]{2,1,0:T(8,128)(2,1)} %owner_roots.3), calls=%async_computation | async-start | bytes 1048576 | tf_op jit(solution)/shard_map/owner_roots/all_to_all | solution.py:180
  27.7 12.9 %collective-permute-start.3 = (bf16[12,32,512]{2,1,0:T(8,128)(2,1)S(1)}, bf16[12,32,512]{2,1,0:T(8,128)(2,1)S(1)}, u32[]{:S(2)}, u32[]{:S(2)}) collective-permute-start(bf16[12,32,512]{2,1,0:T(8,128)(2,1)S(1)} %fusion), channel_id=1, source_target_pairs={{0,1},{1,2},{2,3},{3,0},{4,5},{5,6},{6,7},{7,4},{8,9},{9,10},{10,1... | collective-permute-start | bytes 1179656 | tf_op jit(solution)/shard_map/sum_over_x/ppermute | solution.py:15
  33.2 2.1 %copy-start.2 = (s32[48]{0:T(128)S(1)}, s32[48]{0:T(128)}, u32[]{:S(2)}) copy-start(s32[48]{0:T(128)} %owners_ref.1) | copy-start | bytes 580
  35.4 59.9 %copy-start = (f32[1,32,512]{2,1,0:T(8,128)S(1)}, f32[1,32,512]{2,1,0:T(8,128)}, u32[]{:S(2)}) copy-start(f32[1,32,512]{2,1,0:T(8,128)} %lf_ref.1) | copy-start | bytes 196612
  35.4 59.9 %copy-start.1 = (f32[1,32,512]{2,1,0:T(8,128)S(1)}, f32[1,32,512]{2,1,0:T(8,128)}, u32[]{:S(2)}) copy-start(f32[1,32,512]{2,1,0:T(8,128)} %rf_ref.1) | copy-start | bytes 196612
  44.0 31.8 %all-to-all-start.1 = ((bf16[12,32,512]{2,1,0:T(8,128)(2,1)}), bf16[12,32,512]{2,1,0:T(8,128)(2,1)S(1)}, u32[]{:S(2)}, u32[]{:S(2)}) async-start(bf16[12,32,512]{2,1,0:T(8,128)(2,1)} %sum_over_x.3), calls=%async_computation.1 | async-start | bytes 786432 | tf_op jit(solution)/shard_map/sum_over_z/all_to_all | solution.py:190
